TPU v7x, 32 devices: a whole 2x2x4 slice. The times are simulated.
32 devices in a mesh: groups: 2 (over x), azim: 16 (over z, y, core).
Axes of the slice: x: 2, y: 2, z: 4, core: 2. Of those that a mesh axis runs over, the one named last changes fastest.
Arguments:
- v_init: float32 [16, 16384], P('groups', 'azim'), parts along dimension 0, may hold values from -4 to 4
- g_init: float32 [16, 16384], P('groups', 'azim'), parts along dimension 0, may hold values from 0 to 1.5
- spikes: int32 [4, 16, 16384], P(None, 'groups', 'azim'), parts along dimension 1, may hold values 0 or 1
- decay: float32 [2, 16384], P('groups', 'azim'), parts along dimension 0, may hold values from 0.5 to 0.95
- w_local: bfloat16 [18, 64, 16384], P('groups', None, 'azim'), parts along dimension 0, may hold values from -0.75 to 0.75
- w_long: bfloat16 [128, 16384], P('groups', 'azim'), parts along dimension 0, may hold values from -0.75 to 0.75
- lr_src_tile: int32 [256, 2], P('azim', 'groups'), parts along dimension 1, may hold values from 0 to 15; in each aligned block of 16 rows (0 to 15, 16 to 31, ...) at most 2 rows name the same one
- lr_src_block: int32 [256, 2], P('azim', 'groups'), parts along dimension 1, may hold values from 0 to 15
- lr_tgt_block: int32 [256, 2], P('azim', 'groups'), parts along dimension 1, may hold values from 0 to 15
- adj_v_end: float32 [16, 16384], P('groups', 'azim'), parts along dimension 0, may hold values from -6 to 6
- adj_g_end: float32 [16, 16384], P('groups', 'azim'), parts along dimension 0, may hold values from -6 to 6
Outputs:
- adj_v_init: float32 [16, 16384], P('groups', 'azim'), parts along dimension 0
- adj_g_init: float32 [16, 16384], P('groups', 'azim'), parts along dimension 0
- grad_local: bfloat16 [18, 64, 16384], P('groups', None, 'azim'), parts along dimension 0
- grad_long: bfloat16 [128, 16384], P('groups', 'azim'), parts along dimension 0
There are 2 independent parts, one for each index of `groups`. A program takes and returns all parts, laid end to end along the dimension named above; each array names one. Nothing has to cross between parts.
Inputs may be any that keep to these rules, and one draw needn't show every extreme that they name: `lr_src_tile`: among the 16 entries of one tile no source tile appears more than 2 times; in some tile's list one source tile appears exactly 2 times.
All inputs are finite; a program needn't handle non-finite values. No bound on the sum of `spikes` on one device may be relied on, other than what follows from the above.
Results may differ from a plain program's by a relative error of at most 0.0054.
Values may be sent and summed in bfloat16 or wider, within the bound.
No kernel may reach another device: no remote copies, remote signals or barrier semaphores. Data moves between devices by JAX's collectives and lax.ppermute only.
A program may use at most 128 MiB of HBM per device.

v0:
```python
import jax
import jax.numpy as jnp
from jax import lax
from jax.sharding import PartitionSpec as P

BLK = 64
CAP = 2
STEPS = 4


offset_table = ((-1, -1), (-1, 0), (-1, 1), (0, -1), (0, 0), (0, 1), (1, -1), (1, 0), (1, 1))


def padded_2(block, sides, width):
    for axis, dim in sides:
        count = lax.axis_size(axis)
        forward = [(i, i + 1) for i in range(count - 1)]
        backward = [(target, source) for source, target in forward]
        low = lax.ppermute(
            lax.slice_in_dim(block, block.shape[dim] - width, None, axis=dim), axis, forward
        )
        high = lax.ppermute(lax.slice_in_dim(block, 0, width, axis=dim), axis, backward)
        block = jnp.concatenate([low, block, high], axis=dim)
    return block


def shifted(array, axis, by):
    devices = lax.axis_size(axis)
    pairs = [(i, i + by) for i in range(devices) if 0 <= i + by < devices]
    return lax.ppermute(array, axis, pairs)


def surrogate(voltage):
    return jax.nn.sigmoid(2.0 * (voltage - 1.0))


def shift_rows(values, amount):
    row_count = values.shape[1]
    padded = jnp.pad(values, ((0, 0), (1, 1), (0, 0)))
    return padded[:, 1 + amount : 1 + amount + row_count, :]


def local(
    v_init,
    g_init,
    spikes,
    decay,
    w_local,
    w_long,
    lr_src_tile,
    lr_src_block,
    lr_tgt_block,
    adj_v_end,
    adj_g_end,
):
    stimuli, neurons = v_init.shape
    blocks = neurons // BLK
    tile_count = lax.axis_size("azim")
    slot_count = tile_count * CAP
    entries = lr_src_tile.shape[0]
    w_grid = w_local.reshape(9, BLK, blocks, BLK)
    w_entry = w_long.reshape(BLK, entries, BLK)
    tiles_in = lr_src_tile[:, 0]
    blocks_in = lr_src_block[:, 0]
    targets = lr_tgt_block[:, 0]
    position = jnp.arange(entries, dtype=jnp.int32)
    earlier = (tiles_in[:, None] == tiles_in[None, :]) & (position[None, :] < position[:, None])
    slot_index = tiles_in * CAP + jnp.sum(earlier.astype(jnp.int32), axis=1)
    slot_hit = slot_index[:, None] == jnp.arange(slot_count, dtype=jnp.int32)[None, :]
    request = jnp.sum(jnp.where(slot_hit, blocks_in[:, None], 0), axis=0)
    wanted = lax.all_to_all(
        request.reshape(tile_count, CAP), "azim", split_axis=0, concat_axis=0, tiled=True
    ).reshape(slot_count)
    block_ids = jnp.arange(blocks, dtype=jnp.int32)
    target_hit = (targets[:, None] == block_ids[None, :]).astype(jnp.float32)
    wanted_hit = (wanted[:, None] == block_ids[None, :]).astype(jnp.bfloat16)
    voltage = v_init
    conduct = g_init
    records = []
    for moment in range(STEPS):
        spiking = spikes[moment].astype(jnp.float32)
        activity = (spiking * surrogate(voltage)).astype(jnp.bfloat16)
        rim_act = padded_2(activity.reshape(1, stimuli, neurons), (("azim", 0),), 1).reshape(
            3, stimuli, blocks, BLK
        )
        drive = jnp.zeros((stimuli, blocks, BLK), jnp.float32)
        for number, (step_a, step_e) in enumerate(offset_table):
            source = shift_rows(rim_act[step_a + 1], step_e)
            drive = drive + jnp.einsum(
                "bes,set->bet", source, w_grid[number], preferred_element_type=jnp.float32
            )
        outgoing = jnp.take(rim_act[1], wanted, axis=1).reshape(stimuli, tile_count, CAP * BLK)
        arrived = lax.all_to_all(outgoing, "azim", split_axis=1, concat_axis=1, tiled=True).reshape(
            stimuli, slot_count, BLK
        )
        fetched = jnp.take(arrived, slot_index, axis=1)
        product = jnp.einsum("bls,slt->blt", fetched, w_entry, preferred_element_type=jnp.float32)
        drive = drive + jnp.einsum(
            "blt,le->bet", product, target_hit, precision=lax.Precision.HIGHEST
        )
        drive = drive.reshape(stimuli, neurons)
        cond_next = decay * conduct + jax.nn.softplus(drive)
        volt_next = voltage + 0.1 * (cond_next * (3.0 - voltage) - voltage) - spiking
        records.append((voltage, cond_next, drive, rim_act, fetched, spiking))
        voltage = volt_next
        conduct = cond_next
    adj_volt = adj_v_end
    adj_cond = adj_g_end
    grad_list = [jnp.zeros((BLK, blocks, BLK), jnp.float32) for number in range(9)]
    grad_entry = jnp.zeros((BLK, entries, BLK), jnp.float32)
    for moment in reversed(range(STEPS)):
        voltage, cond_next, drive, rim_act, fetched, spiking = records[moment]
        total_g = adj_cond + adj_volt * 0.1 * (3.0 - voltage)
        adj_drive = (total_g * jax.nn.sigmoid(drive)).astype(jnp.bfloat16)
        adj_cond = decay * total_g
        adj_grid = adj_drive.reshape(stimuli, blocks, BLK)
        for number, (step_a, step_e) in enumerate(offset_table):
            source = shift_rows(rim_act[step_a + 1], step_e)
            grad_list[number] = grad_list[number] + jnp.einsum(
                "bes,bet->set", source, adj_grid, preferred_element_type=jnp.float32
            )
        toward = [jnp.zeros((stimuli, blocks, BLK), jnp.float32) for number in range(3)]
        for number, (step_a, step_e) in enumerate(offset_table):
            partial_value = jnp.einsum(
                "bet,set->bes", adj_grid, w_grid[number], preferred_element_type=jnp.float32
            )
            toward[step_a + 1] = toward[step_a + 1] + shift_rows(partial_value, -step_e)
        from_left = shifted(
            toward[2].reshape(stimuli, neurons).astype(jnp.bfloat16), "azim", 1
        ).astype(jnp.float32)
        from_right = shifted(
            toward[0].reshape(stimuli, neurons).astype(jnp.bfloat16), "azim", -1
        ).astype(jnp.float32)
        adj_act = toward[1] + (from_left + from_right).reshape(stimuli, blocks, BLK)
        gathered = jnp.take(adj_grid, targets, axis=1)
        partial_value = jnp.einsum(
            "blt,slt->bls", gathered, w_entry, preferred_element_type=jnp.float32
        ).astype(jnp.bfloat16)
        placed = (
            jnp.zeros((stimuli, slot_count, BLK), jnp.bfloat16)
            .at[:, slot_index, :]
            .set(partial_value)
        )
        returned = lax.all_to_all(
            placed.reshape(stimuli, tile_count, CAP * BLK),
            "azim",
            split_axis=1,
            concat_axis=1,
            tiled=True,
        ).reshape(stimuli, slot_count, BLK)
        adj_act = adj_act + jnp.einsum(
            "bqs,qe->bes", returned, wanted_hit, preferred_element_type=jnp.float32
        )
        grad_entry = grad_entry + jnp.einsum(
            "bls,blt->slt", fetched, gathered, preferred_element_type=jnp.float32
        )
        slope = surrogate(voltage)
        slope = 2.0 * slope * (1.0 - slope)
        adj_volt = (
            adj_volt * (0.9 - 0.1 * cond_next) + adj_act.reshape(stimuli, neurons) * spiking * slope
        )
    grad_local = jnp.stack(grad_list).reshape(9, BLK, neurons).astype(jnp.bfloat16)
    grad_long = grad_entry.reshape(BLK, entries * BLK).astype(jnp.bfloat16)
    return (adj_volt, adj_cond, grad_local, grad_long)


def solution(mesh):
    return jax.shard_map(
        local,
        mesh=mesh,
        in_specs=(
            P("groups", "azim"),
            P("groups", "azim"),
            P(None, "groups", "azim"),
            P("groups", "azim"),
            P("groups", None, "azim"),
            P("groups", "azim"),
            P("azim", "groups"),
            P("azim", "groups"),
            P("azim", "groups"),
            P("groups", "azim"),
            P("groups", "azim"),
        ),
        out_specs=(
            P("groups", "azim"),
            P("groups", "azim"),
            P("groups", None, "azim"),
            P("groups", "azim"),
        ),
        check_vma=False,
    )
```

profile of v0, /device:TPU:0, one launch (start us, length us, event | category | flops | bytes accessed | tf_op | source)
XLA Modules:
  0.0 289.1 jit_solution(6760738926922545198)
XLA Ops:
  2.7 3.0 %collective-permute-start = (bf16[1,8,1024]{2,1,0:T(8,128)(2,1)S(1)}, bf16[1,8,1024]{2,1,0:T(8,128)(2,1)S(1)}, u32[]{:S(2)}, u32[]{:S(2)}) collective-permute-start(bf16[1,8,1024]{2,1,0:T(8,128)(2,1)S(1)} %bitcast.348), channel_id=1, source_target_pairs={{0,1},{1,2},{2,3},{3,4},{4,5},{5,6},{6,7},{7,8},{8,9},{9,10},{10,1... | collective-permute-start | bytes 49160 | tf_op jit(solution)/shard_map/ppermute | solution.py:19
  9.4 8.0 %all-to-all-start = ((s32[16,1,2]{2,1,0:T(1,128)}), s32[16,1,2]{2,1,0:T(1,128)S(1)}, u32[]{:S(2)}, u32[]{:S(2)}) async-start(s32[16,1,2]{2,1,0:T(1,128)} %bitcast.9), calls=%async_computation | async-start | bytes 16384 | tf_op jit(solution)/shard_map/all_to_all | solution.py:71
  20.5 1.4 fusion.422
  27.2 6.0 %all-to-all-start.1 = ((bf16[8,16,128]{2,0,1:T(8,128)(2,1)}), bf16[8,16,128]{2,0,1:T(8,128)(2,1)S(1)}, u32[]{:S(2)}, u32[]{:S(2)}) async-start(bf16[8,16,128]{2,0,1:T(8,128)(2,1)} %copy.798), calls=%async_computation.1 | async-start | bytes 65536 | tf_op jit(solution)/shard_map/all_to_all | solution.py:93
  36.1 3.8 %all-to-all-done.1 = bf16[8,16,128]{2,0,1:T(8,128)(2,1)S(1)} async-done(((bf16[8,16,128]{2,0,1:T(8,128)(2,1)}), bf16[8,16,128]{2,0,1:T(8,128)(2,1)S(1)}, u32[]{:S(2)}, u32[]{:S(2)}) %all-to-all-start.1) | async-done | bytes 32800 | tf_op jit(solution)/shard_map/all_to_all | solution.py:93
  42.9 3.0 %collective-permute-start.2 = (bf16[1,8,1024]{2,1,0:T(8,128)(2,1)S(1)}, bf16[1,8,1024]{2,1,0:T(8,128)(2,1)S(1)}, u32[]{:S(2)}, u32[]{:S(2)}) collective-permute-start(bf16[1,8,1024]{2,1,0:T(8,128)(2,1)S(1)} %bitcast.352), channel_id=1, source_target_pairs={{0,1},{1,2},{2,3},{3,4},{4,5},{5,6},{6,7},{7,8},{8,9},{9,10},{10,1... | collective-permute-start | bytes 49160 | tf_op jit(solution)/shard_map/ppermute | solution.py:19
  47.6 3.7 %all-to-all-start.2 = ((bf16[8,16,128]{2,0,1:T(8,128)(2,1)}), bf16[8,16,128]{2,0,1:T(8,128)(2,1)S(1)}, u32[]{:S(2)}, u32[]{:S(2)}) async-start(bf16[8,16,128]{2,0,1:T(8,128)(2,1)} %copy.822), calls=%async_computation.2 | async-start | bytes 65536 | tf_op jit(solution)/shard_map/all_to_all | solution.py:93
  54.0 3.8 %all-to-all-done.2 = bf16[8,16,128]{2,0,1:T(8,128)(2,1)S(1)} async-done(((bf16[8,16,128]{2,0,1:T(8,128)(2,1)}), bf16[8,16,128]{2,0,1:T(8,128)(2,1)S(1)}, u32[]{:S(2)}, u32[]{:S(2)}) %all-to-all-start.2) | async-done | bytes 32800 | tf_op jit(solution)/shard_map/all_to_all | solution.py:93
  60.9 3.0 %collective-permute-start.4 = (bf16[1,8,1024]{2,1,0:T(8,128)(2,1)S(1)}, bf16[1,8,1024]{2,1,0:T(8,128)(2,1)S(1)}, u32[]{:S(2)}, u32[]{:S(2)}) collective-permute-start(bf16[1,8,1024]{2,1,0:T(8,128)(2,1)S(1)} %bitcast.354), channel_id=1, source_target_pairs={{0,1},{1,2},{2,3},{3,4},{4,5},{5,6},{6,7},{7,8},{8,9},{9,10},{10,1... | collective-permute-start | bytes 49160 | tf_op jit(solution)/shard_map/ppermute | solution.py:19
  65.5 3.7 %all-to-all-start.3 = ((bf16[8,16,128]{2,0,1:T(8,128)(2,1)}), bf16[8,16,128]{2,0,1:T(8,128)(2,1)S(1)}, u32[]{:S(2)}, u32[]{:S(2)}) async-start(bf16[8,16,128]{2,0,1:T(8,128)(2,1)} %copy.846), calls=%async_computation.3 | async-start | bytes 65536 | tf_op jit(solution)/shard_map/all_to_all | solution.py:93
  72.0 3.8 %all-to-all-done.3 = bf16[8,16,128]{2,0,1:T(8,128)(2,1)S(1)} async-done(((bf16[8,16,128]{2,0,1:T(8,128)(2,1)}), bf16[8,16,128]{2,0,1:T(8,128)(2,1)S(1)}, u32[]{:S(2)}, u32[]{:S(2)}) %all-to-all-start.3) | async-done | bytes 32800 | tf_op jit(solution)/shard_map/all_to_all | solution.py:93
  79.4 3.0 %collective-permute-start.6 = (bf16[1,8,1024]{2,1,0:T(8,128)(2,1)S(1)}, bf16[1,8,1024]{2,1,0:T(8,128)(2,1)S(1)}, u32[]{:S(2)}, u32[]{:S(2)}) collective-permute-start(bf16[1,8,1024]{2,1,0:T(8,128)(2,1)S(1)} %bitcast.350), channel_id=1, source_target_pairs={{0,1},{1,2},{2,3},{3,4},{4,5},{5,6},{6,7},{7,8},{8,9},{9,10},{10,1... | collective-permute-start | bytes 49160 | tf_op jit(solution)/shard_map/ppermute | solution.py:19
  84.1 3.7 %all-to-all-start.4 = ((bf16[8,16,128]{2,0,1:T(8,128)(2,1)}), bf16[8,16,128]{2,0,1:T(8,128)(2,1)S(1)}, u32[]{:S(2)}, u32[]{:S(2)}) async-start(bf16[8,16,128]{2,0,1:T(8,128)(2,1)} %copy.870), calls=%async_computation.4 | async-start | bytes 65536 | tf_op jit(solution)/shard_map/all_to_all | solution.py:93
  92.1 2.3 all-to-all-done.4
  106.6 3.6 %collective-permute-start.8 = (bf16[8,1024]{1,0:T(8,128)(2,1)}, bf16[8,1024]{1,0:T(8,128)(2,1)}, u32[]{:S(2)}, u32[]{:S(2)}) collective-permute-start(bf16[8,1024]{1,0:T(8,128)(2,1)} %convert_element_type.284), channel_id=1, source_target_pairs={{0,1},{1,2},{2,3},{3,4},{4,5},{5,6},{6,7},{7,8},{8,9},{9,10},{10,1... | collective-permute-start | bytes 49160 | tf_op jit(solution)/shard_map/ppermute | solution.py:30
  112.7 1.7 convolution_convert_fusion.3
  115.0 2.4 scatter_fusion
  117.4 1.5 copy.900
  118.8 1.6 reshape.268
  121.8 4.1 %all-to-all-start.5 = ((bf16[8,16,128]{2,0,1:T(8,128)(2,1)}), bf16[8,16,128]{2,0,1:T(8,128)(2,1)}, u32[]{:S(2)}, u32[]{:S(2)}) async-start(bf16[8,16,128]{2,0,1:T(8,128)(2,1)} %copy.901), calls=%async_computation.5 | async-start | bytes 65536 | tf_op jit(solution)/shard_map/all_to_all | solution.py:144
  127.3 1.5 reshape.267
  128.8 3.8 %all-to-all-done.5 = bf16[8,16,128]{2,0,1:T(8,128)(2,1)} async-done(((bf16[8,16,128]{2,0,1:T(8,128)(2,1)}), bf16[8,16,128]{2,0,1:T(8,128)(2,1)}, u32[]{:S(2)}, u32[]{:S(2)}) %all-to-all-start.5) | async-done | bytes 32800 | tf_op jit(solution)/shard_map/all_to_all | solution.py:144
  134.0 1.5 reshape.269
  138.2 1.5 reshape.270
  139.7 1.5 multiply_convert_fusion.2
  154.5 2.0 gather_fusion.9
  158.3 1.4 convert_element_type.296
  162.8 1.5 convert_element_type.293
  164.3 3.8 %collective-permute-start.10 = (bf16[8,1024]{1,0:T(8,128)(2,1)}, bf16[8,1024]{1,0:T(8,128)(2,1)}, u32[]{:S(2)}, u32[]{:S(2)}) collective-permute-start(bf16[8,1024]{1,0:T(8,128)(2,1)} %convert_element_type.293), channel_id=1, source_target_pairs={{0,1},{1,2},{2,3},{3,4},{4,5},{5,6},{6,7},{7,8},{8,9},{9,10},{10,1... | collective-permute-start | bytes 49160 | tf_op jit(solution)/shard_map/ppermute | solution.py:30
  168.0 2.1 convolution_add_fusion.25
  170.1 1.9 convolution_add_fusion.21
  181.1 3.5 %all-to-all-start.6 = ((bf16[8,16,128]{2,0,1:T(8,128)(2,1)}), bf16[8,16,128]{2,0,1:T(8,128)(2,1)S(1)}, u32[]{:S(2)}, u32[]{:S(2)}) async-start(bf16[8,16,128]{2,0,1:T(8,128)(2,1)} %copy.929), calls=%async_computation.6 | async-start | bytes 65536 | tf_op jit(solution)/shard_map/all_to_all | solution.py:144
  185.4 5.8 %all-to-all-done.6 = bf16[8,16,128]{2,0,1:T(8,128)(2,1)S(1)} async-done(((bf16[8,16,128]{2,0,1:T(8,128)(2,1)}), bf16[8,16,128]{2,0,1:T(8,128)(2,1)S(1)}, u32[]{:S(2)}, u32[]{:S(2)}) %all-to-all-start.6) | async-done | bytes 32800 | tf_op jit(solution)/shard_map/all_to_all | solution.py:144
  200.6 2.1 gather_fusion.10
  204.5 1.4 convert_element_type.305
  209.0 1.5 convert_element_type.302
  210.4 3.7 %collective-permute-start.12 = (bf16[8,1024]{1,0:T(8,128)(2,1)}, bf16[8,1024]{1,0:T(8,128)(2,1)}, u32[]{:S(2)}, u32[]{:S(2)}) collective-permute-start(bf16[8,1024]{1,0:T(8,128)(2,1)} %convert_element_type.302), channel_id=1, source_target_pairs={{0,1},{1,2},{2,3},{3,4},{4,5},{5,6},{6,7},{7,8},{8,9},{9,10},{10,1... | collective-permute-start | bytes 49160 | tf_op jit(solution)/shard_map/ppermute | solution.py:30
  214.2 2.1 convolution_add_fusion.24
  224.2 1.7 scatter_fusion.2
  226.5 1.6 reshape.278
  229.5 4.1 %all-to-all-start.7 = ((bf16[8,16,128]{2,0,1:T(8,128)(2,1)}), bf16[8,16,128]{2,0,1:T(8,128)(2,1)}, u32[]{:S(2)}, u32[]{:S(2)}) async-start(bf16[8,16,128]{2,0,1:T(8,128)(2,1)} %copy.957), calls=%async_computation.7 | async-start | bytes 65536 | tf_op jit(solution)/shard_map/all_to_all | solution.py:144
  235.0 1.4 reshape.277
  236.4 3.8 %all-to-all-done.7 = bf16[8,16,128]{2,0,1:T(8,128)(2,1)} async-done(((bf16[8,16,128]{2,0,1:T(8,128)(2,1)}), bf16[8,16,128]{2,0,1:T(8,128)(2,1)}, u32[]{:S(2)}, u32[]{:S(2)}) %all-to-all-start.7) | async-done | bytes 32800 | tf_op jit(solution)/shard_map/all_to_all | solution.py:144
  241.6 1.5 reshape.279
  246.8 1.4 broadcast_multiply_fusion
  257.6 4.1 %all-to-all-start.8 = ((bf16[8,16,128]{2,0,1:T(8,128)(2,1)}), bf16[8,16,128]{2,0,1:T(8,128)(2,1)}, u32[]{:S(2)}, u32[]{:S(2)}) async-start(bf16[8,16,128]{2,0,1:T(8,128)(2,1)} %copy.985), calls=%async_computation.8 | async-start | bytes 65536 | tf_op jit(solution)/shard_map/all_to_all | solution.py:144
  265.0 3.6 %collective-permute-start.14 = (bf16[8,1024]{1,0:T(8,128)(2,1)}, bf16[8,1024]{1,0:T(8,128)(2,1)}, u32[]{:S(2)}, u32[]{:S(2)}) collective-permute-start(bf16[8,1024]{1,0:T(8,128)(2,1)} %convert_element_type.311), channel_id=1, source_target_pairs={{0,1},{1,2},{2,3},{3,4},{4,5},{5,6},{6,7},{7,8},{8,9},{9,10},{10,1... | collective-permute-start | bytes 49160 | tf_op jit(solution)/shard_map/ppermute | solution.py:30
  269.7 1.4 fusion.5
  (526 shorter events, 152.3 us)
Async XLA Ops:
  1.4 32.3 %collective-permute-start.1 = (bf16[1,8,1024]{2,1,0:T(8,128)(2,1)S(1)}, bf16[1,8,1024]{2,1,0:T(8,128)(2,1)S(1)}, u32[]{:S(2)}, u32[]{:S(2)}) collective-permute-start(bf16[1,8,1024]{2,1,0:T(8,128)(2,1)S(1)} %bitcast.347), channel_id=1, source_target_pairs={{1,0},{2,1},{3,2},{4,3},{5,4},{6,5},{7,6},{8,7},{9,8},{10,9},{11,1... | collective-permute-start | bytes 49160 | tf_op jit(solution)/shard_map/ppermute | solution.py:22
  2.7 30.5 %collective-permute-start = (bf16[1,8,1024]{2,1,0:T(8,128)(2,1)S(1)}, bf16[1,8,1024]{2,1,0:T(8,128)(2,1)S(1)}, u32[]{:S(2)}, u32[]{:S(2)}) collective-permute-start(bf16[1,8,1024]{2,1,0:T(8,128)(2,1)S(1)} %bitcast.348), channel_id=1, source_target_pairs={{0,1},{1,2},{2,3},{3,4},{4,5},{5,6},{6,7},{7,8},{8,9},{9,10},{10,1... | collective-permute-start | bytes 49160 | tf_op jit(solution)/shard_map/ppermute | solution.py:19
  9.4 15.1 %all-to-all-start = ((s32[16,1,2]{2,1,0:T(1,128)}), s32[16,1,2]{2,1,0:T(1,128)S(1)}, u32[]{:S(2)}, u32[]{:S(2)}) async-start(s32[16,1,2]{2,1,0:T(1,128)} %bitcast.9), calls=%async_computation | async-start | bytes 16384 | tf_op jit(solution)/shard_map/all_to_all | solution.py:71
  17.4 17.0 %copy-start.50 = (bf16[8,16,64]{2,1,0:T(8,128)(2,1)}, bf16[8,16,64]{2,1,0:T(8,128)(2,1)S(1)}, u32[]{:S(2)}) copy-start(bf16[8,16,64]{2,1,0:T(8,128)(2,1)S(1)} %squeeze.46) | copy-start | bytes 49156
  24.1 51.9 %copy-start.99 = (s32[1024]{0:T(1024)}, s32[1024]{0:T(1024)S(1)}, u32[]{:S(2)}) copy-start(s32[1024]{0:T(1024)S(1)} %get-tuple-element.58) | copy-start | bytes 12292
  27.2 12.7 %all-to-all-start.1 = ((bf16[8,16,128]{2,0,1:T(8,128)(2,1)}), bf16[8,16,128]{2,0,1:T(8,128)(2,1)S(1)}, u32[]{:S(2)}, u32[]{:S(2)}) async-start(bf16[8,16,128]{2,0,1:T(8,128)(2,1)} %copy.798), calls=%async_computation.1 | async-start | bytes 65536 | tf_op jit(solution)/shard_map/all_to_all | solution.py:93
  41.4 17.9 %copy-start.35 = (f32[8,1024]{1,0:T(8,128)}, f32[8,1024]{1,0:T(8,128)S(1)}, u32[]{:S(2)}) copy-start(f32[8,1024]{1,0:T(8,128)S(1)} %get-tuple-element.42) | copy-start | bytes 98308
  41.5 17.9 %copy-start.69 = (f32[8,1024]{1,0:T(8,128)}, f32[8,1024]{1,0:T(8,128)S(1)}, u32[]{:S(2)}) copy-start(f32[8,1024]{1,0:T(8,128)S(1)} %get-tuple-element.43) | copy-start | bytes 98308
  41.6 10.2 %collective-permute-start.3 = (bf16[1,8,1024]{2,1,0:T(8,128)(2,1)S(1)}, bf16[1,8,1024]{2,1,0:T(8,128)(2,1)S(1)}, u32[]{:S(2)}, u32[]{:S(2)}) collective-permute-start(bf16[1,8,1024]{2,1,0:T(8,128)(2,1)S(1)} %bitcast.351), channel_id=1, source_target_pairs={{1,0},{2,1},{3,2},{4,3},{5,4},{6,5},{7,6},{8,7},{9,8},{10,9},{11,1... | collective-permute-start | bytes 49160 | tf_op jit(solution)/shard_map/ppermute | solution.py:22
  42.9 8.4 %collective-permute-start.2 = (bf16[1,8,1024]{2,1,0:T(8,128)(2,1)S(1)}, bf16[1,8,1024]{2,1,0:T(8,128)(2,1)S(1)}, u32[]{:S(2)}, u32[]{:S(2)}) collective-permute-start(bf16[1,8,1024]{2,1,0:T(8,128)(2,1)S(1)} %bitcast.352), channel_id=1, source_target_pairs={{0,1},{1,2},{2,3},{3,4},{4,5},{5,6},{6,7},{7,8},{8,9},{9,10},{10,1... | collective-permute-start | bytes 49160 | tf_op jit(solution)/shard_map/ppermute | solution.py:19
  47.6 10.3 %all-to-all-start.2 = ((bf16[8,16,128]{2,0,1:T(8,128)(2,1)}), bf16[8,16,128]{2,0,1:T(8,128)(2,1)S(1)}, u32[]{:S(2)}, u32[]{:S(2)}) async-start(bf16[8,16,128]{2,0,1:T(8,128)(2,1)} %copy.822), calls=%async_computation.2 | async-start | bytes 65536 | tf_op jit(solution)/shard_map/all_to_all | solution.py:93
  59.4 17.9 %copy-start.73 = (f32[8,1024]{1,0:T(8,128)}, f32[8,1024]{1,0:T(8,128)S(1)}, u32[]{:S(2)}) copy-start(f32[8,1024]{1,0:T(8,128)S(1)} %get-tuple-element.40) | copy-start | bytes 98308
  59.4 80.3 %copy-start.28 = (f32[8,1024]{1,0:T(8,128)}, f32[8,1024]{1,0:T(8,128)S(1)}, u32[]{:S(2)}) copy-start(f32[8,1024]{1,0:T(8,128)S(1)} %get-tuple-element.39) | copy-start | bytes 98308
  59.6 10.2 %collective-permute-start.5 = (bf16[1,8,1024]{2,1,0:T(8,128)(2,1)S(1)}, bf16[1,8,1024]{2,1,0:T(8,128)(2,1)S(1)}, u32[]{:S(2)}, u32[]{:S(2)}) collective-permute-start(bf16[1,8,1024]{2,1,0:T(8,128)(2,1)S(1)} %bitcast.353), channel_id=1, source_target_pairs={{1,0},{2,1},{3,2},{4,3},{5,4},{6,5},{7,6},{8,7},{9,8},{10,9},{11,1... | collective-permute-start | bytes 49160 | tf_op jit(solution)/shard_map/ppermute | solution.py:22
  60.9 8.4 %collective-permute-start.4 = (bf16[1,8,1024]{2,1,0:T(8,128)(2,1)S(1)}, bf16[1,8,1024]{2,1,0:T(8,128)(2,1)S(1)}, u32[]{:S(2)}, u32[]{:S(2)}) collective-permute-start(bf16[1,8,1024]{2,1,0:T(8,128)(2,1)S(1)} %bitcast.354), channel_id=1, source_target_pairs={{0,1},{1,2},{2,3},{3,4},{4,5},{5,6},{6,7},{7,8},{8,9},{9,10},{10,1... | collective-permute-start | bytes 49160 | tf_op jit(solution)/shard_map/ppermute | solution.py:19
  65.5 10.3 %all-to-all-start.3 = ((bf16[8,16,128]{2,0,1:T(8,128)(2,1)}), bf16[8,16,128]{2,0,1:T(8,128)(2,1)S(1)}, u32[]{:S(2)}, u32[]{:S(2)}) async-start(bf16[8,16,128]{2,0,1:T(8,128)(2,1)} %copy.846), calls=%async_computation.3 | async-start | bytes 65536 | tf_op jit(solution)/shard_map/all_to_all | solution.py:93
  78.0 18.6 %copy-start.71 = (f32[8,1024]{1,0:T(8,128)}, f32[8,1024]{1,0:T(8,128)S(1)}, u32[]{:S(2)}) copy-start(f32[8,1024]{1,0:T(8,128)S(1)} %get-tuple-element.36) | copy-start | bytes 98308
  78.1 10.8 %collective-permute-start.7 = (bf16[1,8,1024]{2,1,0:T(8,128)(2,1)S(1)}, bf16[1,8,1024]{2,1,0:T(8,128)(2,1)S(1)}, u32[]{:S(2)}, u32[]{:S(2)}) collective-permute-start(bf16[1,8,1024]{2,1,0:T(8,128)(2,1)S(1)} %bitcast.349), channel_id=1, source_target_pairs={{1,0},{2,1},{3,2},{4,3},{5,4},{6,5},{7,6},{8,7},{9,8},{10,9},{11,1... | collective-permute-start | bytes 49160 | tf_op jit(solution)/shard_map/ppermute | solution.py:22
  79.4 8.4 %collective-permute-start.6 = (bf16[1,8,1024]{2,1,0:T(8,128)(2,1)S(1)}, bf16[1,8,1024]{2,1,0:T(8,128)(2,1)S(1)}, u32[]{:S(2)}, u32[]{:S(2)}) collective-permute-start(bf16[1,8,1024]{2,1,0:T(8,128)(2,1)S(1)} %bitcast.350), channel_id=1, source_target_pairs={{0,1},{1,2},{2,3},{3,4},{4,5},{5,6},{6,7},{7,8},{8,9},{9,10},{10,1... | collective-permute-start | bytes 49160 | tf_op jit(solution)/shard_map/ppermute | solution.py:19
  84.1 10.3 %all-to-all-start.4 = ((bf16[8,16,128]{2,0,1:T(8,128)(2,1)}), bf16[8,16,128]{2,0,1:T(8,128)(2,1)S(1)}, u32[]{:S(2)}, u32[]{:S(2)}) async-start(bf16[8,16,128]{2,0,1:T(8,128)(2,1)} %copy.870), calls=%async_computation.4 | async-start | bytes 65536 | tf_op jit(solution)/shard_map/all_to_all | solution.py:93
  104.4 21.6 %collective-permute-start.9 = (bf16[8,1024]{1,0:T(8,128)(2,1)}, bf16[8,1024]{1,0:T(8,128)(2,1)}, u32[]{:S(2)}, u32[]{:S(2)}) collective-permute-start(bf16[8,1024]{1,0:T(8,128)(2,1)} %convert_element_type.287), channel_id=1, source_target_pairs={{1,0},{2,1},{3,2},{4,3},{5,4},{6,5},{7,6},{8,7},{9,8},{10,9},{11,1... | collective-permute-start | bytes 49160 | tf_op jit(solution)/shard_map/ppermute | solution.py:30
  106.6 19.3 %collective-permute-start.8 = (bf16[8,1024]{1,0:T(8,128)(2,1)}, bf16[8,1024]{1,0:T(8,128)(2,1)}, u32[]{:S(2)}, u32[]{:S(2)}) collective-permute-start(bf16[8,1024]{1,0:T(8,128)(2,1)} %convert_element_type.284), channel_id=1, source_target_pairs={{0,1},{1,2},{2,3},{3,4},{4,5},{5,6},{6,7},{7,8},{8,9},{9,10},{10,1... | collective-permute-start | bytes 49160 | tf_op jit(solution)/shard_map/ppermute | solution.py:30
  121.8 10.8 %all-to-all-start.5 = ((bf16[8,16,128]{2,0,1:T(8,128)(2,1)}), bf16[8,16,128]{2,0,1:T(8,128)(2,1)}, u32[]{:S(2)}, u32[]{:S(2)}) async-start(bf16[8,16,128]{2,0,1:T(8,128)(2,1)} %copy.901), calls=%async_computation.5 | async-start | bytes 65536 | tf_op jit(solution)/shard_map/all_to_all | solution.py:144
  152.4 15.7 %copy-start.66 = (bf16[8,16,64]{2,0,1:T(8,128)(2,1)S(1)}, bf16[8,16,64]{2,0,1:T(8,128)(2,1)}, u32[]{:S(2)}) copy-start(bf16[8,16,64]{2,0,1:T(8,128)(2,1)} %copy.853) | copy-start | bytes 49156
  159.8 24.8 %collective-permute-start.11 = (bf16[8,1024]{1,0:T(8,128)(2,1)}, bf16[8,1024]{1,0:T(8,128)(2,1)}, u32[]{:S(2)}, u32[]{:S(2)}) collective-permute-start(bf16[8,1024]{1,0:T(8,128)(2,1)} %convert_element_type.296), channel_id=1, source_target_pairs={{1,0},{2,1},{3,2},{4,3},{5,4},{6,5},{7,6},{8,7},{9,8},{10,9},{11,1... | collective-permute-start | bytes 49160 | tf_op jit(solution)/shard_map/ppermute | solution.py:30
  164.3 20.3 %collective-permute-start.10 = (bf16[8,1024]{1,0:T(8,128)(2,1)}, bf16[8,1024]{1,0:T(8,128)(2,1)}, u32[]{:S(2)}, u32[]{:S(2)}) collective-permute-start(bf16[8,1024]{1,0:T(8,128)(2,1)} %convert_element_type.293), channel_id=1, source_target_pairs={{0,1},{1,2},{2,3},{3,4},{4,5},{5,6},{6,7},{7,8},{8,9},{9,10},{10,1... | collective-permute-start | bytes 49160 | tf_op jit(solution)/shard_map/ppermute | solution.py:30
  178.8 12.6 %copy-start.90 = (f32[8,16,64]{2,0,1:T(8,128)S(1)}, f32[8,16,64]{2,0,1:T(8,128)}, u32[]{:S(2)}) copy-start(f32[8,16,64]{2,0,1:T(8,128)} %convolution_bitcast_fusion.26) | copy-start | bytes 98308
  178.8 13.0 %copy-start.29 = (f32[8,1024]{1,0:T(8,128)S(1)}, f32[8,1024]{1,0:T(8,128)}, u32[]{:S(2)}) copy-start(f32[8,1024]{1,0:T(8,128)} %copy-done.28) | copy-start | bytes 98308
  178.8 13.0 %copy-start.36 = (f32[8,1024]{1,0:T(8,128)S(1)}, f32[8,1024]{1,0:T(8,128)}, u32[]{:S(2)}) copy-start(f32[8,1024]{1,0:T(8,128)} %copy-done.35) | copy-start | bytes 98308
  178.8 13.0 %copy-start.55 = (f32[8,1024]{1,0:T(8,128)S(1)}, f32[8,1024]{1,0:T(8,128)}, u32[]{:S(2)}) copy-start(f32[8,1024]{1,0:T(8,128)} %copy-done.54) | copy-start | bytes 98308
  178.8 13.0 %copy-start.56 = (f32[8,1024]{1,0:T(8,128)S(1)}, f32[8,1024]{1,0:T(8,128)}, u32[]{:S(2)}) copy-start(f32[8,1024]{1,0:T(8,128)} %get-tuple-element.37) | copy-start | bytes 98308
  178.8 13.0 %copy-start.75 = (f32[8,1024]{1,0:T(8,128)S(1)}, f32[8,1024]{1,0:T(8,128)}, u32[]{:S(2)}) copy-start(f32[8,1024]{1,0:T(8,128)} %get-tuple-element.33) | copy-start | bytes 98308
  178.8 13.0 %copy-start.93 = (f32[8,1024]{1,0:T(8,128)S(1)}, f32[8,1024]{1,0:T(8,128)}, u32[]{:S(2)}) copy-start(f32[8,1024]{1,0:T(8,128)} %get-tuple-element.34) | copy-start | bytes 98308
  181.1 10.1 %all-to-all-start.6 = ((bf16[8,16,128]{2,0,1:T(8,128)(2,1)}), bf16[8,16,128]{2,0,1:T(8,128)(2,1)S(1)}, u32[]{:S(2)}, u32[]{:S(2)}) async-start(bf16[8,16,128]{2,0,1:T(8,128)(2,1)} %copy.929), calls=%async_computation.6 | async-start | bytes 65536 | tf_op jit(solution)/shard_map/all_to_all | solution.py:144
  199.5 14.6 %copy-start.61 = (bf16[8,16,64]{2,0,1:T(8,128)(2,1)S(1)}, bf16[8,16,64]{2,0,1:T(8,128)(2,1)}, u32[]{:S(2)}) copy-start(bf16[8,16,64]{2,0,1:T(8,128)(2,1)} %copy.805) | copy-start | bytes 49156
  200.6 15.7 %copy-start.11 = (f32[16,64,64]{2,1,0:T(8,128)S(1)}, f32[16,64,64]{2,1,0:T(8,128)}, u32[]{:S(2)}) copy-start(f32[16,64,64]{2,1,0:T(8,128)} %convolution_add_fusion.21) | copy-start | bytes 786436
  200.6 15.7 %copy-start.62 = (bf16[8,16,64]{2,0,1:T(8,128)(2,1)S(1)}, bf16[8,16,64]{2,0,1:T(8,128)(2,1)}, u32[]{:S(2)}) copy-start(bf16[8,16,64]{2,0,1:T(8,128)(2,1)} %copy.805) | copy-start | bytes 49156
  205.9 27.7 %collective-permute-start.13 = (bf16[8,1024]{1,0:T(8,128)(2,1)}, bf16[8,1024]{1,0:T(8,128)(2,1)}, u32[]{:S(2)}, u32[]{:S(2)}) collective-permute-start(bf16[8,1024]{1,0:T(8,128)(2,1)} %convert_element_type.305), channel_id=1, source_target_pairs={{1,0},{2,1},{3,2},{4,3},{5,4},{6,5},{7,6},{8,7},{9,8},{10,9},{11,1... | collective-permute-start | bytes 49160 | tf_op jit(solution)/shard_map/ppermute | solution.py:30
  210.4 23.2 %collective-permute-start.12 = (bf16[8,1024]{1,0:T(8,128)(2,1)}, bf16[8,1024]{1,0:T(8,128)(2,1)}, u32[]{:S(2)}, u32[]{:S(2)}) collective-permute-start(bf16[8,1024]{1,0:T(8,128)(2,1)} %convert_element_type.302), channel_id=1, source_target_pairs={{0,1},{1,2},{2,3},{3,4},{4,5},{5,6},{6,7},{7,8},{8,9},{9,10},{10,1... | collective-permute-start | bytes 49160 | tf_op jit(solution)/shard_map/ppermute | solution.py:30
  223.3 23.5 %copy-start.48 = (f32[8,1024]{1,0:T(8,128)S(1)}, f32[8,1024]{1,0:T(8,128)}, u32[]{:S(2)}) copy-start(f32[8,1024]{1,0:T(8,128)} %param.17) | copy-start | bytes 98308
  226.5 20.3 %copy-start.74 = (f32[8,1024]{1,0:T(8,128)S(1)}, f32[8,1024]{1,0:T(8,128)}, u32[]{:S(2)}) copy-start(f32[8,1024]{1,0:T(8,128)} %copy-done.73) | copy-start | bytes 98308
  226.5 21.7 %copy-start.59 = (f32[8,1024]{1,0:T(8,128)S(1)}, f32[8,1024]{1,0:T(8,128)}, u32[]{:S(2)}) copy-start(f32[8,1024]{1,0:T(8,128)} %copy-done.58) | copy-start | bytes 98308
  229.5 10.8 %all-to-all-start.7 = ((bf16[8,16,128]{2,0,1:T(8,128)(2,1)}), bf16[8,16,128]{2,0,1:T(8,128)(2,1)}, u32[]{:S(2)}, u32[]{:S(2)}) async-start(bf16[8,16,128]{2,0,1:T(8,128)(2,1)} %copy.957), calls=%async_computation.7 | async-start | bytes 65536 | tf_op jit(solution)/shard_map/all_to_all | solution.py:144
  254.0 14.6 %copy-start.7 = (f32[16,64,64]{2,1,0:T(8,128)S(1)}, f32[16,64,64]{2,1,0:T(8,128)}, u32[]{:S(2)}) copy-start(f32[16,64,64]{2,1,0:T(8,128)} %convolution_add_fusion.24) | copy-start | bytes 786436
  254.0 14.6 %copy-start.86 = (bf16[8,16,64]{2,0,1:T(8,128)(2,1)S(1)}, bf16[8,16,64]{2,0,1:T(8,128)(2,1)}, u32[]{:S(2)}) copy-start(bf16[8,16,64]{2,0,1:T(8,128)(2,1)} %copy.780) | copy-start | bytes 49156
  257.6 29.5 %all-to-all-start.8 = ((bf16[8,16,128]{2,0,1:T(8,128)(2,1)}), bf16[8,16,128]{2,0,1:T(8,128)(2,1)}, u32[]{:S(2)}, u32[]{:S(2)}) async-start(bf16[8,16,128]{2,0,1:T(8,128)(2,1)} %copy.985), calls=%async_computation.8 | async-start | bytes 65536 | tf_op jit(solution)/shard_map/all_to_all | solution.py:144
  262.7 23.6 %collective-permute-start.15 = (bf16[8,1024]{1,0:T(8,128)(2,1)}, bf16[8,1024]{1,0:T(8,128)(2,1)}, u32[]{:S(2)}, u32[]{:S(2)}) collective-permute-start(bf16[8,1024]{1,0:T(8,128)(2,1)} %convert_element_type.314), channel_id=1, source_target_pairs={{1,0},{2,1},{3,2},{4,3},{5,4},{6,5},{7,6},{8,7},{9,8},{10,9},{11,1... | collective-permute-start | bytes 49160 | tf_op jit(solution)/shard_map/ppermute | solution.py:30
  265.0 21.3 %collective-permute-start.14 = (bf16[8,1024]{1,0:T(8,128)(2,1)}, bf16[8,1024]{1,0:T(8,128)(2,1)}, u32[]{:S(2)}, u32[]{:S(2)}) collective-permute-start(bf16[8,1024]{1,0:T(8,128)(2,1)} %convert_element_type.311), channel_id=1, source_target_pairs={{0,1},{1,2},{2,3},{3,4},{4,5},{5,6},{6,7},{7,8},{8,9},{9,10},{10,1... | collective-permute-start | bytes 49160 | tf_op jit(solution)/shard_map/ppermute | solution.py:30
  (78 other events, 322.6 us)
where the time goes:
time: 294 us; the launch traced here: 289 us
  local copies, waits for them, and re-layouts  83.5 us (28%)
  matrix products  81.5 us (28%)
  starting transfers between devices  78.1 us (27%)
  waiting for transfers between devices  27.2 us (9%)
  other arithmetic  16.7 us (6%)
    dot_general x36, matrix products, local(): jnp.einsum('bes,bet->set', source, adj_grid, preferred_element_type=jnp.f...  37.5 us
    dot_general x36, matrix products, local(): jnp.einsum('bet,set->bes', adj_grid, w_grid[number], preferred_element_ty...  25 us
    ppermute x8, starting transfers between devices, shifted(): return lax.ppermute(array, axis, pairs)  19.9 us
    all_to_all x4, starting transfers between devices, local(): lax.all_to_all(outgoing, 'azim', split_axis=1, concat_axis=1, tiled=True)  17.1 us
    all_to_all x4, starting transfers between devices, local(): lax.all_to_all(placed.reshape(stimuli, tile_count, CAP * BLK), 'azim', sp...  15.9 us
    all_to_all x4, waiting for transfers between devices, local(): lax.all_to_all(outgoing, 'azim', split_axis=1, concat_axis=1, tiled=True)  13.8 us
    all_to_all x4, waiting for transfers between devices, local(): lax.all_to_all(placed.reshape(stimuli, tile_count, CAP * BLK), 'azim', sp...  13.4 us
    ppermute x4, starting transfers between devices, padded_2(): lax.ppermute(lax.slice_in_dim(block, block.shape[dim] - width, None, axis...  12.1 us
  transfers between devices with their start and end apart: 25, of which 7 were waited for; matrix products, arithmetic and copies ran while one was open for 36% of the time, Pallas kernels for 0%

commit v1 on v0

v1 whole, which is shorter than its diff:
```python
import functools

import jax
import jax.numpy as jnp
from jax import lax
from jax.experimental import pallas as pl
from jax.experimental.pallas import tpu as pltpu
from jax.sharding import PartitionSpec as P

BLK = 64
CAP = 2
STEPS = 4
LANES = 128
GROUP = 4
WIDE = GROUP * BLK
SIDE = 3 * BLK

f32 = jnp.float32
bf16 = jnp.bfloat16


def surrogate(voltage):
    return jax.nn.sigmoid(2.0 * (voltage - 1.0))


def lane_half(rows):
    return lax.broadcasted_iota(jnp.int32, (rows, LANES), 1) // BLK


def half_only(piece, half, which):
    return jnp.where(half == which, piece, 0.0)


def half_pair(first, second, half):
    return jnp.where(half == 0, first, second)


def swapped(piece):
    return pltpu.roll(piece, BLK, 1)


def chunks_of(values):
    return [values[:, c * LANES : (c + 1) * LANES] for c in range(values.shape[1] // LANES)]


def odd_chunks(chunks, half):
    turned = [swapped(piece) for piece in chunks]
    zero = jnp.zeros_like(chunks[0])
    return [
        half_pair(left, right, half) for left, right in zip([zero] + turned, turned + [zero])
    ]


def product(left, right):
    return lax.dot_general(left, right, (((1,), (0,)), ((), ())), preferred_element_type=f32)


def product_back(left, right):
    return lax.dot_general(left, right, (((1,), (1,)), ((), ())), preferred_element_type=f32)


def product_over(left, right):
    return lax.dot_general(left, right, (((0,), (0,)), ((), ())), preferred_element_type=f32)


def stacked(pieces):
    return jnp.concatenate(pieces, axis=0)


def folded(acc_ref, half):
    totals = []
    for block in range(acc_ref.shape[0]):
        piece = acc_ref[block]
        totals.append(piece + swapped(piece))
    return [half_pair(totals[b], totals[b + 1], half) for b in range(0, len(totals), 2)]


def start_kernel(v_ref, spikes_ref, table_ref, tile_ref, out_ref, rank_ref, ask_ref):
    chips = out_ref.shape[0]
    rows, neurons = v_ref.shape
    entries = table_ref.shape[1]
    activity = (spikes_ref[0].astype(f32) * surrogate(v_ref[...])).astype(bf16)
    table = table_ref[...]
    same = tile_ref[...] == table[0:1, :]
    before = lax.broadcasted_iota(jnp.int32, (entries, entries), 1) < lax.broadcasted_iota(
        jnp.int32, (entries, entries), 0
    )
    rank = jnp.sum(jnp.where(same & before, 1.0, 0.0), axis=1, keepdims=True).astype(jnp.int32)
    rank_ref[...] = rank
    ask_ref[...] = jnp.zeros_like(ask_ref)
    lane = lax.broadcasted_iota(jnp.int32, (rows, LANES), 1)
    for entry in range(entries):
        tile = table[0, entry]
        chip = tile // 2
        place = CAP * (tile - 2 * chip) + rank[entry, 0]
        ask_ref[chip] = jnp.where(lane == place, table[1, entry].astype(f32), ask_ref[chip])
    for chip in range(chips):
        out_ref[chip, :, :neurons] = activity
        out_ref[chip, :, neurons:] = ask_ref[chip].astype(bf16)


def forward_part(
    first, near_ref, far_ref, table_ref, w_ref, w_long_ref, source_ref, fetched_ref, acc_ref
):
    rows = near_ref.shape[1]
    neurons = w_ref.shape[1]
    blocks = neurons // BLK
    chips = near_ref.shape[0]
    entries = table_ref.shape[1]
    half = lane_half(rows)
    table = table_ref[...]
    me = table[3, 0]
    chip = me // 2
    core = me - 2 * chip
    low = chip - 1 + core
    high = chip + core
    own = near_ref[chip, :, :neurons].astype(f32)
    left = far_ref[jnp.maximum(low, 0), :, :neurons].astype(f32)
    right = far_ref[jnp.minimum(high, chips - 1), :, :neurons].astype(f32)
    left = jnp.where(low >= 0, left, 0.0)
    right = jnp.where(high < chips, right, 0.0)
    zero = jnp.zeros((rows, LANES), f32)
    for side, values in enumerate((left, own, right)):
        even = chunks_of(values)
        odd = odd_chunks(even, half)
        even = even + [zero]
        for group in range(blocks // GROUP):
            pieces = []
            for block in range(GROUP * group, GROUP * (group + 1)):
                line = even if block % 2 else odd
                pieces.append((line[block // 2], line[block // 2 + 1]))
            source_ref[group, :, side * WIDE : side * WIDE + LANES] = stacked(
                [piece[0] for piece in pieces]
            ).astype(bf16)
            source_ref[group, :, side * WIDE + LANES : (side + 1) * WIDE] = stacked(
                [piece[1] for piece in pieces]
            ).astype(bf16)
    drive = []
    for group in range(blocks // GROUP):
        columns = slice(group * WIDE, (group + 1) * WIDE)
        total = jnp.zeros((GROUP * rows, WIDE), f32)
        for side in range(3):
            total = total + product(
                source_ref[group, :, side * WIDE : side * WIDE + SIDE],
                w_ref[side * SIDE : (side + 1) * SIDE, columns],
            )
        for pair in range(GROUP // 2):
            lanes = slice(pair * LANES, (pair + 1) * LANES)
            at = 2 * pair * rows
            drive.append(
                half_pair(
                    total[at : at + rows, lanes], total[at + rows : at + 2 * rows, lanes], half
                )
            )
    acc_ref[...] = jnp.zeros_like(acc_ref)
    for group in range(entries // GROUP):
        columns = slice(group * WIDE, (group + 1) * WIDE)
        pieces = []
        for entry in range(GROUP * group, GROUP * (group + 1)):
            tile = table[0, entry]
            block = table[1, entry]
            place = tile // 2
            lanes = pl.ds(pl.multiple_of(block // 2 * LANES, LANES), LANES)
            piece = jnp.where(
                tile - 2 * place == core, near_ref[place, :, lanes], far_ref[place, :, lanes]
            )
            pieces.append(half_only(piece.astype(f32), half, block % 2))
        fetched = stacked(pieces).astype(bf16)
        fetched_ref[group] = fetched
        weights = w_long_ref[:, columns]
        total = product(fetched, stacked([weights, weights]))
        for at in range(GROUP):
            lanes = slice(at // 2 * LANES, (at // 2 + 1) * LANES)
            target = table[2, GROUP * group + at]
            acc_ref[target] += half_only(total[at * rows : (at + 1) * rows, lanes], half, at % 2)
    extra = folded(acc_ref, half)
    return jnp.concatenate([a + b for a, b in zip(drive, extra)], axis=1)


def forward_kernel(moment, *refs):
    (
        near_ref, far_ref, table_ref, w_ref, w_long_ref, v_ref, g_ref, decay_ref, spikes_ref,
    ) = refs[:9]
    v_out, g_out, gate_out, source_ref, fetched_ref, act_ref = refs[9:15]
    acc_ref = refs[-1]
    neurons = w_ref.shape[1]
    drive = forward_part(
        moment == 0, near_ref, far_ref, table_ref, w_ref, w_long_ref, source_ref, fetched_ref,
        acc_ref,
    )
    voltage = v_ref[...]
    conduct = decay_ref[...] * g_ref[...] + jax.nn.softplus(drive)
    voltage = (
        voltage + 0.1 * (conduct * (3.0 - voltage) - voltage) - spikes_ref[moment].astype(f32)
    )
    v_out[...] = voltage
    g_out[...] = conduct
    gate_out[...] = jax.nn.sigmoid(drive)
    activity = (spikes_ref[moment + 1].astype(f32) * surrogate(voltage)).astype(bf16)
    for chip in range(act_ref.shape[0]):
        act_ref[chip] = activity
    if moment == 0:
        wanted_ref = refs[15]
        core = table_ref[3, 0] % 2
        for chip in range(near_ref.shape[0]):
            for ref, place in ((near_ref, 2 * chip + core), (far_ref, 2 * chip + 1 - core)):
                asked = ref[chip, :, neurons:].astype(f32)
                asked = jnp.where(core == 1, pltpu.roll(asked, LANES - CAP, 1), asked)
                wanted_ref[place] = asked.astype(jnp.int32)


def backward_part(
    adj_cond, adj_volt, voltage, gate, decay, table_ref, rank_ref, w_ref, w_long_ref,
    adj_ref, gathered_ref, cond_out, own_out, pair_out, cross_out, placed_out, acc_ref, slot_ref,
):
    rows, neurons = voltage.shape
    blocks = neurons // BLK
    entries = table_ref.shape[1]
    half = lane_half(rows)
    table = table_ref[...]
    rank = rank_ref[...]
    core = table[3, 0] % 2
    total_g = adj_cond + adj_volt * 0.1 * (3.0 - voltage)
    adj_drive = (total_g * gate).astype(bf16).astype(f32)
    cond_out[...] = decay * total_g
    chunks = chunks_of(adj_drive)
    zero = jnp.zeros((rows, LANES), f32)
    for number, piece in enumerate(chunks):
        turned = swapped(piece)
        acc_ref[2 * number] = half_pair(piece, turned, half)
        acc_ref[2 * number + 1] = half_pair(turned, piece, half)
    even = [[zero] * (blocks // 2 + 1) for side in range(3)]
    odd = [[zero] * (blocks // 2 + 1) for side in range(3)]
    for group in range(blocks // GROUP):
        columns = slice(group * WIDE, (group + 1) * WIDE)
        left = stacked([half_only(chunks[2 * group], half, k) for k in range(2)] + [zero, zero])
        right = stacked(
            [zero, zero] + [half_only(chunks[2 * group + 1], half, k) for k in range(2)]
        )
        adj = jnp.concatenate([left, right], axis=1).astype(bf16)
        adj_ref[group] = adj
        for side in range(3):
            back = product_back(adj, w_ref[side * SIDE : (side + 1) * SIDE, columns])
            for at in range(GROUP):
                block = GROUP * group + at
                line = even[side] if block % 2 else odd[side]
                lower = back[at * rows : (at + 1) * rows, :LANES]
                upper = back[at * rows : (at + 1) * rows, LANES:]
                upper = jnp.concatenate([upper, jnp.zeros_like(upper)], axis=1)
                line[block // 2] = line[block // 2] + lower
                line[block // 2 + 1] = line[block // 2 + 1] + upper
    toward = []
    for side in range(3):
        turned = [swapped(piece) for piece in odd[side]]
        toward.append(
            jnp.concatenate(
                [
                    even[side][c] + half_pair(turned[c], turned[c + 1], half)
                    for c in range(blocks // 2)
                ],
                axis=1,
            )
        )
    own_out[...] = toward[1]
    pair_out[...] = jnp.where(core == 0, toward[2], toward[0]).astype(bf16)
    cross_out[...] = jnp.where(core == 0, toward[0], toward[2]).astype(bf16)
    slot_ref[...] = jnp.zeros_like(slot_ref)
    for group in range(entries // GROUP):
        columns = slice(group * WIDE, (group + 1) * WIDE)
        left, right = [], []
        for at in range(GROUP):
            piece = half_only(acc_ref[table[2, GROUP * group + at]], half, at % 2)
            left.append(piece if at < 2 else zero)
            right.append(zero if at < 2 else piece)
        gathered = jnp.concatenate([stacked(left), stacked(right)], axis=1).astype(bf16)
        gathered_ref[group] = gathered
        weights = w_long_ref[:, columns]
        back = product_back(gathered, stacked([weights, weights]))
        for at in range(GROUP):
            entry = GROUP * group + at
            tile = table[0, entry]
            slot_ref[tile] += half_only(back[at * rows : (at + 1) * rows], half, rank[entry, 0])
    placed_out[...] = slot_ref[...].astype(bf16)


def turn_kernel(*refs):
    (
        near_ref, far_ref, table_ref, rank_ref, w_ref, w_long_ref, v_ref, g_ref, decay_ref,
        adj_v_ref, adj_g_ref,
    ) = refs[:11]
    g_out, source_ref, fetched_ref = refs[11:14]
    outs = refs[14:21]
    acc_ref, slot_ref = refs[21:]
    drive = forward_part(
        False, near_ref, far_ref, table_ref, w_ref, w_long_ref, source_ref, fetched_ref, acc_ref
    )
    decay = decay_ref[...]
    g_out[...] = decay * g_ref[...] + jax.nn.softplus(drive)
    backward_part(
        adj_g_ref[...], adj_v_ref[...], v_ref[...], jax.nn.sigmoid(drive), decay,
        table_ref, rank_ref, w_ref, w_long_ref, *outs, acc_ref, slot_ref,
    )


def receive_part(
    moment, placed_ref, pair_ref, cross_ref, own_ref, wanted_ref, adj_v_ref, v_ref, g_ref,
    spikes_ref, acc_ref,
):
    rows = v_ref.shape[0]
    half = lane_half(rows)
    acc_ref[...] = jnp.zeros_like(acc_ref)
    for tile in range(placed_ref.shape[0]):
        arrived = placed_ref[tile].astype(f32)
        asked = wanted_ref[tile, 0:1, :]
        for slot in range(CAP):
            acc_ref[asked[0, slot]] += half_only(arrived, half, slot)
    adj_act = own_ref[...] + (pair_ref[...].astype(f32) + cross_ref[...].astype(f32))
    adj_act = adj_act + jnp.concatenate(folded(acc_ref, half), axis=1)
    slope = surrogate(v_ref[...])
    slope = 2.0 * slope * (1.0 - slope)
    return (
        adj_v_ref[...] * (0.9 - 0.1 * g_ref[...])
        + adj_act * spikes_ref[moment].astype(f32) * slope
    )


def backward_kernel(moment, *refs):
    received = refs[:9]
    (
        adj_g_ref, v_ref, gate_ref, decay_ref, table_ref, rank_ref, w_ref, w_long_ref,
    ) = refs[9:17]
    adj_v_out = refs[17]
    outs = refs[18:25]
    acc_ref, slot_ref = refs[25:]
    adj_volt = receive_part(moment, *received, acc_ref)
    adj_v_out[...] = adj_volt
    backward_part(
        adj_g_ref[...], adj_volt, v_ref[...], gate_ref[...], decay_ref[...],
        table_ref, rank_ref, w_ref, w_long_ref, *outs, acc_ref, slot_ref,
    )


def last_kernel(*refs):
    refs[9][...] = receive_part(0, *refs[:9], refs[10])


def grad_kernel(*refs):
    sources, fetched, adjs, gathered = (refs[k * STEPS : (k + 1) * STEPS] for k in range(4))
    local_ref, long_ref = refs[4 * STEPS :]
    for group in range(adjs[0].shape[0]):
        columns = slice(group * WIDE, (group + 1) * WIDE)
        adj = stacked([ref[group] for ref in adjs])
        for side in range(3):
            source = stacked([ref[group, :, side * WIDE : side * WIDE + SIDE] for ref in sources])
            local_ref[side * SIDE : (side + 1) * SIDE, columns] = product_over(
                source, adj
            ).astype(bf16)
    for group in range(gathered[0].shape[0]):
        columns = slice(group * WIDE, (group + 1) * WIDE)
        total = product_over(
            stacked([ref[group] for ref in fetched]), stacked([ref[group] for ref in gathered])
        )
        long_ref[:, columns] = (total[:BLK] + total[BLK:]).astype(bf16)


def call(kernel, outs, args, scratch=()):
    vmem = pl.BlockSpec(memory_space=pltpu.VMEM)
    return pl.pallas_call(
        kernel,
        out_shape=[jax.ShapeDtypeStruct(shape, dtype) for shape, dtype in outs],
        in_specs=[vmem] * len(args),
        out_specs=[vmem] * len(outs),
        scratch_shapes=[pltpu.VMEM(shape, dtype) for shape, dtype in scratch],
        compiler_params=pltpu.CompilerParams(vmem_limit_bytes=24 * 2**20),
    )(*args)


def local(
    v_init, g_init, spikes, decay, w_local, w_long, lr_src_tile, lr_src_block, lr_tgt_block,
    adj_v_end, adj_g_end,
):
    rows, neurons = v_init.shape
    blocks = neurons // BLK
    tiles = lax.axis_size("azim")
    chips = tiles // 2
    entries = lr_src_tile.shape[0]
    me = lax.axis_index("azim")
    cores = [list(range(core, tiles, 2)) for core in range(2)]
    pair = [(i, i ^ 1) for i in range(tiles)]
    cross = [(i, i + 1) for i in range(1, tiles - 1, 2)]
    cross = cross + [(target, source) for source, target in cross]
    table = jnp.concatenate(
        [
            jnp.concatenate([lr_src_tile, lr_src_block, lr_tgt_block], axis=1).T,
            jnp.full((1, entries), me, jnp.int32),
        ]
    )
    w_all = w_local.reshape(9 * BLK, neurons)

    def spread(values):
        near = lax.all_to_all(
            values, "azim", split_axis=0, concat_axis=0, tiled=True, axis_index_groups=cores
        )
        return near, lax.ppermute(near, "azim", pair)

    state = ((rows, neurons), f32)
    block_sum = ((blocks, rows, LANES), f32)
    slots = ((tiles, rows, LANES), f32)
    source = ((blocks // GROUP, GROUP * rows, 3 * WIDE), bf16)
    fetched = ((entries // GROUP, GROUP * rows, LANES), bf16)
    back_outs = [
        ((blocks // GROUP, GROUP * rows, WIDE), bf16),
        ((entries // GROUP, GROUP * rows, WIDE), bf16),
        state,
        state,
        ((rows, neurons), bf16),
        ((rows, neurons), bf16),
        ((tiles, rows, LANES), bf16),
    ]
    out, rank = call(
        start_kernel,
        [((chips, rows, neurons + LANES), bf16), ((entries, 1), jnp.int32)],
        (v_init, spikes, table, lr_src_tile),
        [((chips, rows, LANES), f32)],
    )
    voltages, conducts, gates, sources, fetches = [v_init], [g_init], [], [], []
    for moment in range(STEPS - 1):
        near, far = spread(out)
        outs = [state, state, state, source, fetched, ((chips, rows, neurons), bf16)]
        if moment == 0:
            outs.append(((tiles, rows, LANES), jnp.int32))
        results = call(
            functools.partial(forward_kernel, moment),
            outs,
            (
                near, far, table, w_all, w_long, voltages[-1], conducts[-1], decay, spikes,
            ),
            [block_sum],
        )
        if moment == 0:
            wanted = results[6]
        voltage, conduct, gate, source_t, fetched_t, out = results[:6]
        voltages.append(voltage)
        conducts.append(conduct)
        gates.append(gate)
        sources.append(source_t)
        fetches.append(fetched_t)
    near, far = spread(out)
    conduct, source_t, fetched_t, *back = call(
        turn_kernel,
        [state, source, fetched] + back_outs,
        (
            near, far, table, rank, w_all, w_long, voltages[-1], conducts[-1], decay,
            adj_v_end, adj_g_end,
        ),
        [block_sum, slots],
    )
    conducts.append(conduct)
    sources.append(source_t)
    fetches.append(fetched_t)
    adj_volt = adj_v_end
    adjs, gathers = [], []
    for moment in reversed(range(STEPS)):
        adj_t, gathered_t, adj_cond, own, to_pair, to_cross, placed = back
        adjs.insert(0, adj_t)
        gathers.insert(0, gathered_t)
        arrived = lax.all_to_all(placed, "azim", split_axis=0, concat_axis=0, tiled=True)
        from_pair = lax.ppermute(to_pair, "azim", pair)
        from_cross = lax.ppermute(to_cross, "azim", cross)
        received = (
            arrived, from_pair, from_cross, own, wanted, adj_volt, voltages[moment],
            conducts[moment + 1], spikes,
        )
        if moment > 0:
            adj_volt, *back = call(
                functools.partial(backward_kernel, moment),
                [state] + back_outs,
                received
                + (
                    adj_cond, voltages[moment - 1], gates[moment - 1], decay, table, rank, w_all,
                    w_long,
                ),
                [block_sum, slots],
            )
    grad_local, grad_long = call(
        grad_kernel,
        [((9 * BLK, neurons), bf16), ((BLK, entries * BLK), bf16)],
        (*sources, *fetches, *adjs, *gathers),
    )
    (adj_volt,) = call(last_kernel, [state], received, [block_sum])
    return (adj_volt, adj_cond, grad_local.reshape(9, BLK, neurons), grad_long)


def solution(mesh):
    return jax.shard_map(
        local,
        mesh=mesh,
        in_specs=(
            P("groups", "azim"),
            P("groups", "azim"),
            P(None, "groups", "azim"),
            P("groups", "azim"),
            P("groups", None, "azim"),
            P("groups", "azim"),
            P("azim", "groups"),
            P("azim", "groups"),
            P("azim", "groups"),
            P("groups", "azim"),
            P("groups", "azim"),
        ),
        out_specs=(
            P("groups", "azim"),
            P("groups", "azim"),
            P("groups", None, "azim"),
            P("groups", "azim"),
        ),
        check_vma=False,
    )
```

time: 294 us -> 112 us (0.38); the launches traced: 289 us -> 111 us
  matrix products: 81.5 us -> 0 us
  local copies, waits for them, and re-layouts: 83.5 us -> 6.05 us
  starting transfers between devices: 78.1 us -> 21.7 us
  blocking collectives: 0 us -> 44.6 us
  other arithmetic: 16.7 us -> 0.7 us
  Pallas kernels: 0 us -> 11.1 us
    dot_general x128 -> x0, matrix products: 81.5 us -> none  [the longest x36 37.5 us: local(): jnp.einsum('bes,bet->set', source, adj_grid, preferred_element_type=jnp.f...]
    all_to_all x0 -> x4, blocking collectives: none -> 44.6 us  [spread(): lax.all_to_all(values, 'azim', split_axis=0, concat_axis=0, tiled=True, a...]
    ppermute x16 -> x12, starting transfers between devices: 37.2 us -> 4.13 us  [the longest x4 2.6 us: local(): from_cross = lax.ppermute(to_cross, 'azim', cross)]
    reshape x50 -> x0, local copies, waits for them, and re-layouts: 23.4 us -> none  [the longest x8 7.32 us: local(): placed.reshape(stimuli, tile_count, CAP * BLK)]
    all_to_all x9 -> x4, starting transfers between devices: 40.9 us -> 17.6 us  [local(): lax.all_to_all(placed, 'azim', split_axis=0, concat_axis=0, tiled=True)]
    convert_element_type x16 -> x0, local copies, waits for them, and re-layouts: 11.2 us -> none  [the longest x8 5.61 us: local(): toward[2].reshape(stimuli, neurons).astype(jnp.bfloat16)]
    pallas_call x0 -> x10, Pallas kernels: none -> 11.1 us  [call(): pl.pallas_call(kernel, out_shape=[jax.ShapeDtypeStruct(shape, dtype) for...]
    gather x12 -> x0, local copies, waits for them, and re-layouts: 11.1 us -> none  [the longest x4 6.3 us: local(): gathered = jnp.take(adj_grid, targets, axis=1)]
  transfers between devices with their start and end apart: 25 -> 16, of which waited for: 7 -> 11; matrix products, arithmetic and copies ran while one was open for 36% -> 0% of each run, Pallas kernels for 0% -> 1%
where the time goes in v1:
time: 112 us; the launch traced here: 111 us
  blocking collectives  44.6 us (40%)
  waiting for transfers between devices  26.2 us (23%)
  starting transfers between devices  21.7 us (19%)
  Pallas kernels  11.1 us (10%)
  local copies, waits for them, and re-layouts  6.05 us (5%)
    all_to_all x4, blocking collectives, spread(): lax.all_to_all(values, 'azim', split_axis=0, concat_axis=0, tiled=True, a...  44.6 us
    all_to_all x4, waiting for transfers between devices, local(): lax.all_to_all(placed, 'azim', split_axis=0, concat_axis=0, tiled=True)  20.1 us
    all_to_all x4, starting transfers between devices, local(): lax.all_to_all(placed, 'azim', split_axis=0, concat_axis=0, tiled=True)  17.6 us
    pallas_call x10, Pallas kernels, call(): pl.pallas_call(kernel, out_shape=[jax.ShapeDtypeStruct(shape, dtype) for...  11.1 us
    unnamed x27, local copies, waits for them, and re-layouts  6.04 us
    ppermute x4, waiting for transfers between devices, spread(): return (near, lax.ppermute(near, 'azim', pair))  5.4 us
    ppermute x4, starting transfers between devices, local(): from_cross = lax.ppermute(to_cross, 'azim', cross)  2.6 us
  transfers between devices with their start and end apart: 16, of which 11 were waited for; matrix products, arithmetic and copies ran while one was open for 0% of the time, Pallas kernels for 1%

profile of v1, /device:TPU:0, one launch (start us, length us, event | category | flops | bytes accessed | tf_op | source)
XLA Modules:
  0.0 111.1 jit_solution(17914887762679767742)
XLA Ops:
  0.6 0.7 copy.15.tile_ref
  1.4 0.7 add_bitcast_fusion
  2.1 0.9 copy-done.2
  3.0 0.8 copy-done.6
  3.7 0.3 shard_map.138
  4.0 0.0 copy-start.3
  4.0 0.0 copy-start.5
  4.1 14.7 %all_to_all.40.refs_0_ = bf16[8,8,1152]{2,1,0:T(8,128)(2,1)S(1)} all-to-all(bf16[8,8,1152]{2,1,0:T(8,128)(2,1)S(1)} %get-tuple-element.61), channel_id=1, replica_groups={{0,2,4,6,8,10,12,14},{1,3,5,7,9,11,13,15},{16,18,20,22,24,26,28,30},{17..., dimensions={0} | all-to-all | bytes 294912 | tf_op jit(solution)/shard_map/all_to_all | solution.py:401
  18.7 1.4 %collective-permute-done.refs_1_ = bf16[8,8,1152]{2,1,0:T(8,128)(2,1)S(1)} collective-permute-done((bf16[8,8,1152]{2,1,0:T(8,128)(2,1)S(1)}, bf16[8,8,1152]{2,1,0:T(8,128)(2,1)S(1)}, u32[]{:S(2)}, u32[]{:S(2)}) %collective-permute-start) | collective-permute-done | bytes 147488 | tf_op jit(solution)/shard_map/ppermute | solution.py:404
  20.1 1.3 %copy-done = bf16[9,64,1024]{2,1,0:T(8,128)(2,1)S(1)} copy-done((bf16[9,64,1024]{2,1,0:T(8,128)(2,1)S(1)}, bf16[9,64,1024]{2,1,0:T(8,128)(2,1)}, u32[]{:S(2)}) %copy-start) | copy-done | bytes 1179672
  21.4 0.9 copy-done.4
  22.3 0.7 copy-done.8
  23.0 0.8 copy-done.11
  23.7 0.7 shard_map.139
  24.4 10.0 %all_to_all.41.refs_0_ = bf16[8,8,1024]{2,1,0:T(8,128)(2,1)S(1)} all-to-all(bf16[8,8,1024]{2,1,0:T(8,128)(2,1)S(1)} %get-tuple-element.62), channel_id=1, replica_groups={{0,2,4,6,8,10,12,14},{1,3,5,7,9,11,13,15},{16,18,20,22,24,26,28,30},{17..., dimensions={0} | all-to-all | bytes 262144 | tf_op jit(solution)/shard_map/all_to_all | solution.py:401
  34.4 1.3 %collective-permute-done.1.refs_1_ = bf16[8,8,1024]{2,1,0:T(8,128)(2,1)S(1)} collective-permute-done((bf16[8,8,1024]{2,1,0:T(8,128)(2,1)S(1)}, bf16[8,8,1024]{2,1,0:T(8,128)(2,1)S(1)}, u32[]{:S(2)}, u32[]{:S(2)}) %collective-permute-start.1) | collective-permute-done | bytes 131104 | tf_op jit(solution)/shard_map/ppermute | solution.py:404
  35.8 0.7 shard_map.140
  36.5 0.0 copy-start.10
  36.5 10.0 %all_to_all.42.refs_0_ = bf16[8,8,1024]{2,1,0:T(8,128)(2,1)S(1)} all-to-all(bf16[8,8,1024]{2,1,0:T(8,128)(2,1)S(1)} %get-tuple-element.65), channel_id=1, replica_groups={{0,2,4,6,8,10,12,14},{1,3,5,7,9,11,13,15},{16,18,20,22,24,26,28,30},{17..., dimensions={0} | all-to-all | bytes 262144 | tf_op jit(solution)/shard_map/all_to_all | solution.py:401
  46.4 1.3 %collective-permute-done.2.refs_1_ = bf16[8,8,1024]{2,1,0:T(8,128)(2,1)S(1)} collective-permute-done((bf16[8,8,1024]{2,1,0:T(8,128)(2,1)S(1)}, bf16[8,8,1024]{2,1,0:T(8,128)(2,1)S(1)}, u32[]{:S(2)}, u32[]{:S(2)}) %collective-permute-start.2) | collective-permute-done | bytes 131104 | tf_op jit(solution)/shard_map/ppermute | solution.py:404
  47.8 0.7 shard_map.141
  48.5 10.0 %all_to_all.43.refs_0_ = bf16[8,8,1024]{2,1,0:T(8,128)(2,1)S(1)} all-to-all(bf16[8,8,1024]{2,1,0:T(8,128)(2,1)S(1)} %get-tuple-element.68), channel_id=1, replica_groups={{0,2,4,6,8,10,12,14},{1,3,5,7,9,11,13,15},{16,18,20,22,24,26,28,30},{17..., dimensions={0} | all-to-all | bytes 262144 | tf_op jit(solution)/shard_map/all_to_all | solution.py:401
  58.5 1.3 %collective-permute-done.3.refs_1_ = bf16[8,8,1024]{2,1,0:T(8,128)(2,1)S(1)} collective-permute-done((bf16[8,8,1024]{2,1,0:T(8,128)(2,1)S(1)}, bf16[8,8,1024]{2,1,0:T(8,128)(2,1)S(1)}, u32[]{:S(2)}, u32[]{:S(2)}) %collective-permute-start.3) | collective-permute-done | bytes 131104 | tf_op jit(solution)/shard_map/ppermute | solution.py:404
  59.8 1.8 %shard_map.142 = (f32[8,1024]{1,0:T(8,128)S(1)}, bf16[4,32,768]{2,1,0:T(8,128)(2,1)S(1)}, bf16[4,32,128]{2,1,0:T(8,128)(2,1)S(1)}, bf16[4,32,256]{2,1,0:T(8,128)...) custom-call(bf16[8,8,1024]{2,1,0:T(8,128)(2,1)S(1)} %all_to_all.43.r, ...), custom_call_target="tpu_custom_call" | custom-call | tf_op jit(solution)/shard_map/pallas_call | solution.py:368
  61.6 3.6 %all-to-all-start.4 = ((bf16[16,8,128]{2,1,0:T(8,128)(2,1)}), bf16[16,8,128]{2,1,0:T(8,128)(2,1)S(1)}, u32[]{:S(2)}, u32[]{:S(2)}) async-start(bf16[16,8,128]{2,1,0:T(8,128)(2,1)} %get-tuple-element.72), calls=%async_computation.4 | async-start | bytes 65536 | tf_op jit(solution)/shard_map/all_to_all | solution.py:467
  65.3 0.3 collective-permute-start.4
  65.6 0.7 collective-permute-start.5
  66.2 0.3 collective-permute-done.4.refs_1_
  66.5 5.3 %all-to-all-done.4.refs_0_ = bf16[16,8,128]{2,1,0:T(8,128)(2,1)S(1)} async-done(((bf16[16,8,128]{2,1,0:T(8,128)(2,1)}), bf16[16,8,128]{2,1,0:T(8,128)(2,1)S(1)}, u32[]{:S(2)}, u32[]{:S(2)}) %all-to-all-start.4) | async-done | bytes 32800 | tf_op jit(solution)/shard_map/all_to_all | solution.py:467
  71.9 1.5 %shard_map.143 = (f32[8,1024]{1,0:T(8,128)S(1)}, bf16[4,32,256]{2,1,0:T(8,128)(2,1)S(1)}, bf16[4,32,256]{2,1,0:T(8,128)(2,1)S(1)}, f32[8,1024]{1,0:T(8,128)S(1)}...) custom-call(bf16[16,8,128]{2,1,0:T(8,128)(2,1)S(1)} %all-to-all-done, ...), custom_call_target="tpu_custom_call" | custom-call | tf_op jit(solution)/shard_map/pallas_call | solution.py:368
  73.4 4.7 %all-to-all-start.5 = ((bf16[16,8,128]{2,1,0:T(8,128)(2,1)}), bf16[16,8,128]{2,1,0:T(8,128)(2,1)S(1)}, u32[]{:S(2)}, u32[]{:S(2)}) async-start(bf16[16,8,128]{2,1,0:T(8,128)(2,1)} %get-tuple-element.80), calls=%async_computation.5 | async-start | bytes 65536 | tf_op jit(solution)/shard_map/all_to_all | solution.py:467
  78.1 0.4 collective-permute-start.6
  78.5 0.7 collective-permute-start.7
  79.2 0.2 collective-permute-done.6.refs_1_
  79.4 5.4 %all-to-all-done.5.refs_0_ = bf16[16,8,128]{2,1,0:T(8,128)(2,1)S(1)} async-done(((bf16[16,8,128]{2,1,0:T(8,128)(2,1)}), bf16[16,8,128]{2,1,0:T(8,128)(2,1)S(1)}, u32[]{:S(2)}, u32[]{:S(2)}) %all-to-all-start.5) | async-done | bytes 32800 | tf_op jit(solution)/shard_map/all_to_all | solution.py:467
  84.7 1.5 %shard_map.144 = (f32[8,1024]{1,0:T(8,128)S(1)}, bf16[4,32,256]{2,1,0:T(8,128)(2,1)S(1)}, bf16[4,32,256]{2,1,0:T(8,128)(2,1)S(1)}, f32[8,1024]{1,0:T(8,128)S(1)}...) custom-call(bf16[16,8,128]{2,1,0:T(8,128)(2,1)S(1)} %all-to-all-done, ...), custom_call_target="tpu_custom_call" | custom-call | tf_op jit(solution)/shard_map/pallas_call | solution.py:368
  86.2 4.6 %all-to-all-start.6 = ((bf16[16,8,128]{2,1,0:T(8,128)(2,1)}), bf16[16,8,128]{2,1,0:T(8,128)(2,1)S(1)}, u32[]{:S(2)}, u32[]{:S(2)}) async-start(bf16[16,8,128]{2,1,0:T(8,128)(2,1)} %get-tuple-element.87), calls=%async_computation.6 | async-start | bytes 65536 | tf_op jit(solution)/shard_map/all_to_all | solution.py:467
  90.8 0.4 collective-permute-start.8
  91.2 0.7 collective-permute-start.9
  91.9 0.2 collective-permute-done.8.refs_1_
  92.1 5.4 %all-to-all-done.6.refs_0_ = bf16[16,8,128]{2,1,0:T(8,128)(2,1)S(1)} async-done(((bf16[16,8,128]{2,1,0:T(8,128)(2,1)}), bf16[16,8,128]{2,1,0:T(8,128)(2,1)S(1)}, u32[]{:S(2)}, u32[]{:S(2)}) %all-to-all-start.6) | async-done | bytes 32800 | tf_op jit(solution)/shard_map/all_to_all | solution.py:467
  97.5 1.5 %shard_map.145 = (f32[8,1024]{1,0:T(8,128)S(1)}, bf16[4,32,256]{2,1,0:T(8,128)(2,1)S(1)}, bf16[4,32,256]{2,1,0:T(8,128)(2,1)S(1)}, f32[8,1024]{1,0:T(8,128)}, f3...) custom-call(bf16[16,8,128]{2,1,0:T(8,128)(2,1)S(1)} %all-to-all-done, ...), custom_call_target="tpu_custom_call" | custom-call | tf_op jit(solution)/shard_map/pallas_call | solution.py:368
  98.9 4.6 %all-to-all-start.7 = ((bf16[16,8,128]{2,1,0:T(8,128)(2,1)}), bf16[16,8,128]{2,1,0:T(8,128)(2,1)S(1)}, u32[]{:S(2)}, u32[]{:S(2)}) async-start(bf16[16,8,128]{2,1,0:T(8,128)(2,1)} %get-tuple-element.94), calls=%async_computation.7 | async-start | bytes 65536 | tf_op jit(solution)/shard_map/all_to_all | solution.py:467
  103.6 0.4 collective-permute-start.10
  104.0 0.7 collective-permute-start.11
  104.6 1.6 %shard_map.147 = (bf16[576,1024]{1,0:T(8,128)(2,1)}, bf16[64,1024]{1,0:T(8,128)(2,1)}) custom-call(bf16[4,32,768]{2,1,0:T(8,128)(2,1)S(1)} %get-tuple-element.100.refs_0_, bf16[4,32,768]{2,1,0:T(8,128)(2,1)S(1)} %get-tuple-element.101.refs_1_, bf16[4,32,768]{2,1,0:T(8,128)(2,1)S(1)} %get-tuple-element.102.refs_2_, ...), custom_call_target="tpu_custom_call" | custom-call | tf_op jit(solution)/shard_map/pallas_call | solution.py:368
  106.2 4.0 %all-to-all-done.7.refs_0_ = bf16[16,8,128]{2,1,0:T(8,128)(2,1)S(1)} async-done(((bf16[16,8,128]{2,1,0:T(8,128)(2,1)}), bf16[16,8,128]{2,1,0:T(8,128)(2,1)S(1)}, u32[]{:S(2)}, u32[]{:S(2)}) %all-to-all-start.7) | async-done | bytes 32800 | tf_op jit(solution)/shard_map/all_to_all | solution.py:467
  110.2 0.9 shard_map.146
  (27 shorter events, 0.1 us)
Async XLA Ops:
  2.1 0.9 copy-start.2
  3.0 0.8 copy-start.6
  4.0 31.7 %copy-start.3 = (s32[4,8,1024]{2,1,0:T(8,128)S(1)}, s32[4,8,1024]{2,1,0:T(8,128)}, u32[]{:S(2)}) copy-start(s32[4,8,1024]{2,1,0:T(8,128)} %refs_8_.15) | copy-start | bytes 393220
  4.0 31.7 %copy-start.5 = (bf16[64,1024]{1,0:T(8,128)(2,1)S(1)}, bf16[64,1024]{1,0:T(8,128)(2,1)}, u32[]{:S(2)}) copy-start(bf16[64,1024]{1,0:T(8,128)(2,1)} %refs_16_.5) | copy-start | bytes 393220
  18.7 1.4 %collective-permute-start = (bf16[8,8,1152]{2,1,0:T(8,128)(2,1)S(1)}, bf16[8,8,1152]{2,1,0:T(8,128)(2,1)S(1)}, u32[]{:S(2)}, u32[]{:S(2)}) collective-permute-start(bf16[8,8,1152]{2,1,0:T(8,128)(2,1)S(1)} %all_to_all.40.refs_0_), channel_id=1, source_target_pairs={{0,1},{1,0},{2,3},{3,2},{4,5},{5,4},{6,7},{7,6},{8,9},{9,8},{10,11... | collective-permute-start | bytes 442376 | tf_op jit(solution)/shard_map/ppermute | solution.py:404
  20.1 1.3 %copy-start = (bf16[9,64,1024]{2,1,0:T(8,128)(2,1)S(1)}, bf16[9,64,1024]{2,1,0:T(8,128)(2,1)}, u32[]{:S(2)}) copy-start(bf16[9,64,1024]{2,1,0:T(8,128)(2,1)} %param.15) | copy-start | bytes 3538948
  21.4 0.9 copy-start.4
  22.3 0.7 copy-start.8
  23.0 0.8 copy-start.11
  23.7 12.0 %copy-start.1 = (bf16[9,64,1024]{2,1,0:T(8,128)(2,1)S(1)}, bf16[9,64,1024]{2,1,0:T(8,128)(2,1)}, u32[]{:S(2)}) copy-start(bf16[9,64,1024]{2,1,0:T(8,128)(2,1)} %param.15) | copy-start | bytes 3538948
  34.4 1.3 %collective-permute-start.1 = (bf16[8,8,1024]{2,1,0:T(8,128)(2,1)S(1)}, bf16[8,8,1024]{2,1,0:T(8,128)(2,1)S(1)}, u32[]{:S(2)}, u32[]{:S(2)}) collective-permute-start(bf16[8,8,1024]{2,1,0:T(8,128)(2,1)S(1)} %all_to_all.41.refs_0_), channel_id=1, source_target_pairs={{0,1},{1,0},{2,3},{3,2},{4,5},{5,4},{6,7},{7,6},{8,9},{9,8},{10,11... | collective-permute-start | bytes 393224 | tf_op jit(solution)/shard_map/ppermute | solution.py:404
  36.5 23.4 %copy-start.10 = (f32[8,1024]{1,0:T(8,128)S(1)}, f32[8,1024]{1,0:T(8,128)}, u32[]{:S(2)}) copy-start(f32[8,1024]{1,0:T(8,128)} %refs_5_.5) | copy-start | bytes 98308
  36.5 23.3 %copy-start.12 = (f32[8,1024]{1,0:T(8,128)S(1)}, f32[8,1024]{1,0:T(8,128)}, u32[]{:S(2)}) copy-start(f32[8,1024]{1,0:T(8,128)} %refs_10_.2) | copy-start | bytes 98308
  46.4 1.3 %collective-permute-start.2 = (bf16[8,8,1024]{2,1,0:T(8,128)(2,1)S(1)}, bf16[8,8,1024]{2,1,0:T(8,128)(2,1)S(1)}, u32[]{:S(2)}, u32[]{:S(2)}) collective-permute-start(bf16[8,8,1024]{2,1,0:T(8,128)(2,1)S(1)} %all_to_all.42.refs_0_), channel_id=1, source_target_pairs={{0,1},{1,0},{2,3},{3,2},{4,5},{5,4},{6,7},{7,6},{8,9},{9,8},{10,11... | collective-permute-start | bytes 393224 | tf_op jit(solution)/shard_map/ppermute | solution.py:404
  58.5 1.3 %collective-permute-start.3 = (bf16[8,8,1024]{2,1,0:T(8,128)(2,1)S(1)}, bf16[8,8,1024]{2,1,0:T(8,128)(2,1)S(1)}, u32[]{:S(2)}, u32[]{:S(2)}) collective-permute-start(bf16[8,8,1024]{2,1,0:T(8,128)(2,1)S(1)} %all_to_all.43.refs_0_), channel_id=1, source_target_pairs={{0,1},{1,0},{2,3},{3,2},{4,5},{5,4},{6,7},{7,6},{8,9},{9,8},{10,11... | collective-permute-start | bytes 393224 | tf_op jit(solution)/shard_map/ppermute | solution.py:404
  61.6 23.1 %copy-start.9 = (f32[1,1024]{1,0:T(1,128)S(1)}, f32[1,1024]{1,0:T(1,128)}, u32[]{:S(2)}) copy-start(f32[1,1024]{1,0:T(1,128)} %refs_12_.5) | copy-start | bytes 12292
  61.6 10.2 %all-to-all-start.4 = ((bf16[16,8,128]{2,1,0:T(8,128)(2,1)}), bf16[16,8,128]{2,1,0:T(8,128)(2,1)S(1)}, u32[]{:S(2)}, u32[]{:S(2)}) async-start(bf16[16,8,128]{2,1,0:T(8,128)(2,1)} %get-tuple-element.72), calls=%async_computation.4 | async-start | bytes 65536 | tf_op jit(solution)/shard_map/all_to_all | solution.py:467
  65.3 1.2 %collective-permute-start.4 = (bf16[8,1024]{1,0:T(8,128)(2,1)S(1)}, bf16[8,1024]{1,0:T(8,128)(2,1)S(1)}, u32[]{:S(2)}, u32[]{:S(2)}) collective-permute-start(bf16[8,1024]{1,0:T(8,128)(2,1)S(1)} %get-tuple-element.73), channel_id=1, source_target_pairs={{0,1},{1,0},{2,3},{3,2},{4,5},{5,4},{6,7},{7,6},{8,9},{9,8},{10,11... | collective-permute-start | bytes 49160 | tf_op jit(solution)/shard_map/ppermute | solution.py:468
  65.6 1.0 collective-permute-start.5
  73.3 24.1 %copy-start.7 = (f32[8,1024]{1,0:T(8,128)S(1)}, f32[8,1024]{1,0:T(8,128)}, u32[]{:S(2)}) copy-start(f32[8,1024]{1,0:T(8,128)} %refs_6_.3) | copy-start | bytes 98308
  73.4 11.4 %all-to-all-start.5 = ((bf16[16,8,128]{2,1,0:T(8,128)(2,1)}), bf16[16,8,128]{2,1,0:T(8,128)(2,1)S(1)}, u32[]{:S(2)}, u32[]{:S(2)}) async-start(bf16[16,8,128]{2,1,0:T(8,128)(2,1)} %get-tuple-element.80), calls=%async_computation.5 | async-start | bytes 65536 | tf_op jit(solution)/shard_map/all_to_all | solution.py:467
  78.1 1.2 %collective-permute-start.6 = (bf16[8,1024]{1,0:T(8,128)(2,1)S(1)}, bf16[8,1024]{1,0:T(8,128)(2,1)S(1)}, u32[]{:S(2)}, u32[]{:S(2)}) collective-permute-start(bf16[8,1024]{1,0:T(8,128)(2,1)S(1)} %get-tuple-element.81), channel_id=1, source_target_pairs={{0,1},{1,0},{2,3},{3,2},{4,5},{5,4},{6,7},{7,6},{8,9},{9,8},{10,11... | collective-permute-start | bytes 49160 | tf_op jit(solution)/shard_map/ppermute | solution.py:468
  78.5 0.8 collective-permute-start.7
  86.2 11.3 %all-to-all-start.6 = ((bf16[16,8,128]{2,1,0:T(8,128)(2,1)}), bf16[16,8,128]{2,1,0:T(8,128)(2,1)S(1)}, u32[]{:S(2)}, u32[]{:S(2)}) async-start(bf16[16,8,128]{2,1,0:T(8,128)(2,1)} %get-tuple-element.87), calls=%async_computation.6 | async-start | bytes 65536 | tf_op jit(solution)/shard_map/all_to_all | solution.py:467
  90.8 1.2 %collective-permute-start.8 = (bf16[8,1024]{1,0:T(8,128)(2,1)S(1)}, bf16[8,1024]{1,0:T(8,128)(2,1)S(1)}, u32[]{:S(2)}, u32[]{:S(2)}) collective-permute-start(bf16[8,1024]{1,0:T(8,128)(2,1)S(1)} %get-tuple-element.88), channel_id=1, source_target_pairs={{0,1},{1,0},{2,3},{3,2},{4,5},{5,4},{6,7},{7,6},{8,9},{9,8},{10,11... | collective-permute-start | bytes 49160 | tf_op jit(solution)/shard_map/ppermute | solution.py:468
  91.2 0.8 collective-permute-start.9
  98.9 11.3 %all-to-all-start.7 = ((bf16[16,8,128]{2,1,0:T(8,128)(2,1)}), bf16[16,8,128]{2,1,0:T(8,128)(2,1)S(1)}, u32[]{:S(2)}, u32[]{:S(2)}) async-start(bf16[16,8,128]{2,1,0:T(8,128)(2,1)} %get-tuple-element.94), calls=%async_computation.7 | async-start | bytes 65536 | tf_op jit(solution)/shard_map/all_to_all | solution.py:467
  103.6 2.6 %collective-permute-start.10 = (bf16[8,1024]{1,0:T(8,128)(2,1)S(1)}, bf16[8,1024]{1,0:T(8,128)(2,1)S(1)}, u32[]{:S(2)}, u32[]{:S(2)}) collective-permute-start(bf16[8,1024]{1,0:T(8,128)(2,1)S(1)} %get-tuple-element.95), channel_id=1, source_target_pairs={{0,1},{1,0},{2,3},{3,2},{4,5},{5,4},{6,7},{7,6},{8,9},{9,8},{10,11... | collective-permute-start | bytes 49160 | tf_op jit(solution)/shard_map/ppermute | solution.py:468
  104.0 2.2 %collective-permute-start.11 = (bf16[8,1024]{1,0:T(8,128)(2,1)S(1)}, bf16[8,1024]{1,0:T(8,128)(2,1)S(1)}, u32[]{:S(2)}, u32[]{:S(2)}) collective-permute-start(bf16[8,1024]{1,0:T(8,128)(2,1)S(1)} %get-tuple-element.96), channel_id=1, source_target_pairs={{1,2},{3,4},{5,6},{7,8},{9,10},{11,12},{13,14},{2,1},{4,3},{6,5},{... | collective-permute-start | bytes 49160 | tf_op jit(solution)/shard_map/ppermute | solution.py:469

commit v2 on v1

v2 whole, which is shorter than its diff:
```python
import functools

import jax
import jax.numpy as jnp
from jax import lax
from jax.experimental import pallas as pl
from jax.experimental.pallas import tpu as pltpu
from jax.sharding import PartitionSpec as P

BLK = 64
CAP = 2
STEPS = 4
LANES = 128
GROUP = 4
WIDE = GROUP * BLK
SIDE = 3 * BLK

f32 = jnp.float32
bf16 = jnp.bfloat16


def surrogate(voltage):
    return jax.nn.sigmoid(2.0 * (voltage - 1.0))


def lane_half(rows):
    return lax.broadcasted_iota(jnp.int32, (rows, LANES), 1) // BLK


def half_only(piece, half, which):
    return jnp.where(half == which, piece, 0.0)


def half_pair(first, second, half):
    return jnp.where(half == 0, first, second)


def swapped(piece):
    return pltpu.roll(piece, BLK, 1)


def chunks_of(values):
    return [values[:, c * LANES : (c + 1) * LANES] for c in range(values.shape[1] // LANES)]


def odd_chunks(chunks, half):
    turned = [swapped(piece) for piece in chunks]
    zero = jnp.zeros_like(chunks[0])
    return [
        half_pair(left, right, half) for left, right in zip([zero] + turned, turned + [zero])
    ]


def product(left, right):
    return lax.dot_general(left, right, (((1,), (0,)), ((), ())), preferred_element_type=f32)


def product_back(left, right):
    return lax.dot_general(left, right, (((1,), (1,)), ((), ())), preferred_element_type=f32)


def product_over(left, right):
    return lax.dot_general(left, right, (((0,), (0,)), ((), ())), preferred_element_type=f32)


def stacked(pieces):
    return jnp.concatenate(pieces, axis=0)


def folded(acc_ref, half):
    totals = []
    for block in range(acc_ref.shape[1]):
        piece = half_pair(acc_ref[0, block], acc_ref[1, block], half)
        totals.append(piece + swapped(piece))
    return [half_pair(totals[b], totals[b + 1], half) for b in range(0, len(totals), 2)]


def entry_code(tile, block, target, rank):
    return ((tile * 256 + rank) * 16 + target) * 16 + block


def decoded(code):
    return code >> 16, (code >> 8) & 1, (code >> 4) & 15, code & 15


def hold_kernel(
    entry_ref, pack_ref, w_ref, w_long_ref,
    me_out, table_out, v_out, g_out, decay_out, spikes_out, w_out, w_long_out,
):
    rows = v_out.shape[0]
    v_out[...] = pack_ref[:rows]
    g_out[...] = pack_ref[rows : 2 * rows]
    for moment in range(STEPS):
        spikes_out[moment] = pack_ref[(2 + moment) * rows : (3 + moment) * rows]
    decay_out[...] = pack_ref[(2 + STEPS) * rows :]
    w_out[...] = w_ref[...]
    w_long_out[...] = w_long_ref[...]
    entries = entry_ref.shape[1]
    across = lax.broadcasted_iota(jnp.int32, (entries, entries), 1)
    down = lax.broadcasted_iota(jnp.int32, (entries, entries), 0)
    tiles = entry_ref[0:1, :]
    tiles_down = jnp.sum(
        jnp.where(across == down, tiles.astype(f32), 0.0), axis=1, keepdims=True
    ).astype(jnp.int32)
    earlier = (tiles_down == tiles) & (down < across)
    rank = jnp.sum(jnp.where(earlier, 1.0, 0.0), axis=0, keepdims=True).astype(jnp.int32)
    me_out[...] = jnp.full(me_out.shape, lax.axis_index("azim"), jnp.int32)
    table_out[...] = entry_code(tiles, entry_ref[1:2, :], entry_ref[2:3, :], rank)


def forward_part(
    near_ref, far_ref, me_ref, table_ref, w_ref, w_long_ref, source_ref, fetched_ref, acc_ref
):
    rows = near_ref.shape[1]
    neurons = w_ref.shape[1]
    blocks = neurons // BLK
    chips = near_ref.shape[0]
    entries = table_ref.shape[1]
    half = lane_half(rows)
    table = table_ref[...]
    me = me_ref[...][0, 0]
    chip = me >> 1
    core = me & 1
    acc_ref[...] = jnp.zeros_like(acc_ref)
    for group in range(entries // GROUP):
        columns = slice(group * WIDE, (group + 1) * WIDE)
        pieces, targets = [], []
        for entry in range(GROUP * group, GROUP * (group + 1)):
            tile, _, target, block = decoded(table[0, entry])
            targets.append(target)
            place = tile >> 1
            lanes = pl.ds(pl.multiple_of((block >> 1) * LANES, LANES), LANES)
            piece = jnp.where(
                (tile & 1) == core, near_ref[place, :, lanes], far_ref[place, :, lanes]
            )
            pieces.append(half_only(piece.astype(f32), half, block & 1))
        fetched = stacked(pieces).astype(bf16)
        fetched_ref[group] = fetched
        weights = w_long_ref[:, columns]
        total = product(fetched, stacked([weights, weights]))
        for at, target in enumerate(targets):
            lanes = slice(at // 2 * LANES, (at // 2 + 1) * LANES)
            acc_ref[at % 2, target] += total[at * rows : (at + 1) * rows, lanes]
    low = chip - 1 + core
    high = chip + core
    own = near_ref[chip, :, :neurons].astype(f32)
    left = far_ref[jnp.maximum(low, 0), :, :neurons].astype(f32)
    right = far_ref[jnp.minimum(high, chips - 1), :, :neurons].astype(f32)
    left = jnp.where(low >= 0, left, 0.0)
    right = jnp.where(high < chips, right, 0.0)
    zero = jnp.zeros((rows, LANES), f32)
    for side, values in enumerate((left, own, right)):
        even = chunks_of(values)
        odd = odd_chunks(even, half)
        even = even + [zero]
        for group in range(blocks // GROUP):
            pieces = []
            for block in range(GROUP * group, GROUP * (group + 1)):
                line = even if block % 2 else odd
                pieces.append((line[block // 2], line[block // 2 + 1]))
            source_ref[group, :, side * WIDE : side * WIDE + LANES] = stacked(
                [piece[0] for piece in pieces]
            ).astype(bf16)
            source_ref[group, :, side * WIDE + LANES : (side + 1) * WIDE] = stacked(
                [piece[1] for piece in pieces]
            ).astype(bf16)
    drive = []
    for group in range(blocks // GROUP):
        columns = slice(group * WIDE, (group + 1) * WIDE)
        total = jnp.zeros((GROUP * rows, WIDE), f32)
        for side in range(3):
            total = total + product(
                source_ref[group, :, side * WIDE : side * WIDE + SIDE],
                w_ref[side * SIDE : (side + 1) * SIDE, columns],
            )
        for pair in range(GROUP // 2):
            lanes = slice(pair * LANES, (pair + 1) * LANES)
            at = 2 * pair * rows
            drive.append(
                half_pair(
                    total[at : at + rows, lanes], total[at + rows : at + 2 * rows, lanes], half
                )
            )
    extra = folded(acc_ref, half)
    return jnp.concatenate([a + b for a, b in zip(drive, extra)], axis=1)


def forward_kernel(moment, *refs):
    (
        near_ref, far_ref, me_ref, table_ref, w_ref, w_long_ref, v_ref, g_ref, decay_ref,
        spikes_ref,
    ) = refs[:10]
    v_out, g_out, gate_out, source_ref, fetched_ref, act_ref = refs[10:16]
    acc_ref = refs[-1]
    rows, neurons = v_ref.shape
    chips = act_ref.shape[0]
    drive = forward_part(
        near_ref, far_ref, me_ref, table_ref, w_ref, w_long_ref, source_ref, fetched_ref, acc_ref
    )
    voltage = v_ref[...]
    conduct = decay_ref[...] * g_ref[...] + jax.nn.softplus(drive)
    voltage = (
        voltage + 0.1 * (conduct * (3.0 - voltage) - voltage) - spikes_ref[moment]
    )
    v_out[...] = voltage
    g_out[...] = conduct
    gate_out[...] = jax.nn.sigmoid(drive)
    activity = (spikes_ref[moment + 1] * surrogate(voltage)).astype(bf16)
    for chip in range(chips):
        act_ref[chip, :, :neurons] = activity
    if moment == 0:
        ask_ref = refs[-2]
        table = table_ref[...]
        lane = lax.broadcasted_iota(jnp.int32, (rows, LANES), 1)
        ask_ref[...] = jnp.zeros_like(ask_ref)
        for entry in range(table_ref.shape[1]):
            tile, rank, _, block = decoded(table[0, entry])
            place = CAP * (tile & 1) + rank
            ask_ref[tile >> 1] = jnp.where(lane == place, block.astype(f32), ask_ref[tile >> 1])
        for chip in range(chips):
            act_ref[chip, :, neurons:] = ask_ref[chip].astype(bf16)
    if moment == 1:
        wanted_ref = refs[16]
        core = me_ref[...][0, 0] & 1
        for chip in range(chips):
            for ref, place in ((near_ref, 2 * chip + core), (far_ref, 2 * chip + 1 - core)):
                asked = ref[chip, :, neurons:].astype(f32)
                asked = jnp.where(core == 1, pltpu.roll(asked, LANES - CAP, 1), asked)
                asked = asked + 16.0 * pltpu.roll(asked, LANES - 1, 1)
                wanted_ref[place] = asked.astype(jnp.int32)


def toward_tile(side, adj_ref, w_ref):
    groups, rows, _ = adj_ref.shape
    rows = rows // GROUP
    blocks = groups * GROUP
    half = lane_half(rows)
    zero = jnp.zeros((rows, LANES), f32)
    even = [zero] * (blocks // 2 + 1)
    odd = [zero] * (blocks // 2 + 1)
    for group in range(groups):
        columns = slice(group * WIDE, (group + 1) * WIDE)
        back = product_back(adj_ref[group], w_ref[side * SIDE : (side + 1) * SIDE, columns])
        for at in range(GROUP):
            block = GROUP * group + at
            line = even if block % 2 else odd
            lower = back[at * rows : (at + 1) * rows, :LANES]
            upper = back[at * rows : (at + 1) * rows, LANES:]
            upper = jnp.concatenate([upper, jnp.zeros_like(upper)], axis=1)
            line[block // 2] = line[block // 2] + lower
            line[block // 2 + 1] = line[block // 2 + 1] + upper
    turned = [swapped(piece) for piece in odd]
    return jnp.concatenate(
        [even[c] + half_pair(turned[c], turned[c + 1], half) for c in range(blocks // 2)], axis=1
    )


def backward_part(
    adj_cond, adj_volt, voltage, gate, decay, me_ref, table_ref, w_ref, w_long_ref,
    adj_ref, gathered_ref, cond_out, pair_out, cross_out, placed_out, acc_ref, slot_ref,
    stage_ref, sem,
):
    rows, neurons = voltage.shape
    blocks = neurons // BLK
    entries = table_ref.shape[1]
    half = lane_half(rows)
    table = table_ref[...]
    core = me_ref[...][0, 0] & 1
    total_g = adj_cond + adj_volt * 0.1 * (3.0 - voltage)
    adj_drive = (total_g * gate).astype(bf16).astype(f32)
    cond_out[...] = decay * total_g
    chunks = chunks_of(adj_drive)
    zero = jnp.zeros((rows, LANES), f32)
    for number, piece in enumerate(chunks):
        turned = swapped(piece)
        acc_ref[0, 2 * number] = half_pair(piece, turned, half)
        acc_ref[0, 2 * number + 1] = half_pair(turned, piece, half)
    slot_ref[...] = jnp.zeros_like(slot_ref)
    for group in range(entries // GROUP):
        columns = slice(group * WIDE, (group + 1) * WIDE)
        left, right, slots = [], [], []
        for at in range(GROUP):
            tile, rank, target, _ = decoded(table[0, GROUP * group + at])
            slots.append((rank, tile))
            piece = half_only(acc_ref[0, target], half, at % 2)
            left.append(piece if at < 2 else zero)
            right.append(zero if at < 2 else piece)
        gathered = jnp.concatenate([stacked(left), stacked(right)], axis=1).astype(bf16)
        gathered_ref[group] = gathered
        weights = w_long_ref[:, columns]
        back = product_back(gathered, stacked([weights, weights]))
        for at, slot in enumerate(slots):
            slot_ref[slot] = back[at * rows : (at + 1) * rows]
    for tile in range(stage_ref.shape[0]):
        stage_ref[tile] = half_pair(slot_ref[0, tile], slot_ref[1, tile], half).astype(bf16)
    copy = pltpu.make_async_copy(stage_ref, placed_out, sem)
    copy.start()
    for group in range(blocks // GROUP):
        left = stacked([half_only(chunks[2 * group], half, k) for k in range(2)] + [zero, zero])
        right = stacked(
            [zero, zero] + [half_only(chunks[2 * group + 1], half, k) for k in range(2)]
        )
        adj_ref[group] = jnp.concatenate([left, right], axis=1).astype(bf16)
    before = toward_tile(0, adj_ref, w_ref)
    after = toward_tile(2, adj_ref, w_ref)
    pair_out[...] = jnp.where(core == 0, after, before).astype(bf16)
    cross_out[...] = jnp.where(core == 0, before, after).astype(bf16)
    copy.wait()


def own_kernel(adj_ref, w_ref, own_out):
    own_out[...] = toward_tile(1, adj_ref, w_ref)


def turn_kernel(*refs):
    (
        near_ref, far_ref, me_ref, table_ref, w_ref, w_long_ref, v_ref, g_ref, decay_ref,
        adj_v_ref, adj_g_ref,
    ) = refs[:11]
    g_out, source_ref, fetched_ref = refs[11:14]
    acc_ref = refs[20]
    drive = forward_part(
        near_ref, far_ref, me_ref, table_ref, w_ref, w_long_ref, source_ref, fetched_ref, acc_ref
    )
    decay = decay_ref[...]
    g_out[...] = decay * g_ref[...] + jax.nn.softplus(drive)
    backward_part(
        adj_g_ref[...], adj_v_ref[...], v_ref[...], jax.nn.sigmoid(drive), decay,
        me_ref, table_ref, w_ref, w_long_ref, *refs[14:],
    )


def receive_part(
    moment, placed_ref, pair_ref, cross_ref, own_ref, wanted_ref, adj_v_ref, v_ref, g_ref,
    spikes_ref, acc_ref,
):
    rows = v_ref.shape[0]
    half = lane_half(rows)
    acc_ref[...] = jnp.zeros_like(acc_ref)
    tiles = placed_ref.shape[0]
    for first in range(0, tiles, 3):
        count = min(3, tiles - first)
        codes = wanted_ref[first, 0:1, :]
        for at in range(1, count):
            codes = codes + wanted_ref[first + at, 0:1, :] * 256**at
        code = codes[0, 0]
        for at in range(count):
            arrived = placed_ref[first + at].astype(f32)
            for slot in range(CAP):
                acc_ref[slot, (code >> (8 * at + 4 * slot)) & 15] += arrived
    adj_act = own_ref[...] + (pair_ref[...].astype(f32) + cross_ref[...].astype(f32))
    adj_act = adj_act + jnp.concatenate(folded(acc_ref, half), axis=1)
    slope = surrogate(v_ref[...])
    slope = 2.0 * slope * (1.0 - slope)
    return (
        adj_v_ref[...] * (0.9 - 0.1 * g_ref[...])
        + adj_act * spikes_ref[moment] * slope
    )


def backward_kernel(moment, *refs):
    received = refs[:9]
    (
        adj_g_ref, v_ref, gate_ref, decay_ref, me_ref, table_ref, w_ref, w_long_ref,
    ) = refs[9:17]
    adj_v_out = refs[17]
    acc_ref = refs[24]
    adj_volt = receive_part(moment, *received, acc_ref)
    adj_v_out[...] = adj_volt
    backward_part(
        adj_g_ref[...], adj_volt, v_ref[...], gate_ref[...], decay_ref[...],
        me_ref, table_ref, w_ref, w_long_ref, *refs[18:],
    )


def last_kernel(*refs):
    refs[9][...] = receive_part(0, *refs[:9], refs[10])


def grad_kernel(*refs):
    sources, fetched, adjs, gathered = (refs[k * STEPS : (k + 1) * STEPS] for k in range(4))
    cond_ref, local_ref, long_ref, cond_out = refs[4 * STEPS :]
    cond_out[...] = cond_ref[...]
    for group in range(adjs[0].shape[0]):
        columns = slice(group * WIDE, (group + 1) * WIDE)
        adj = stacked([ref[group] for ref in adjs])
        for side in range(3):
            source = stacked([ref[group, :, side * WIDE : side * WIDE + SIDE] for ref in sources])
            local_ref[side * SIDE : (side + 1) * SIDE, columns] = product_over(
                source, adj
            ).astype(bf16)
    for group in range(gathered[0].shape[0]):
        columns = slice(group * WIDE, (group + 1) * WIDE)
        total = product_over(
            stacked([ref[group] for ref in fetched]), stacked([ref[group] for ref in gathered])
        )
        long_ref[:, columns] = (total[:BLK] + total[BLK:]).astype(bf16)


def call(kernel, outs, args, scratch=(), hbm_outs=(), cost=None):
    vmem = pl.BlockSpec(memory_space=pltpu.VMEM)
    hbm = pl.BlockSpec(memory_space=pltpu.HBM)
    return pl.pallas_call(
        kernel,
        out_shape=[jax.ShapeDtypeStruct(shape, dtype) for shape, dtype in outs],
        in_specs=[vmem] * len(args),
        out_specs=[hbm if k in hbm_outs else vmem for k in range(len(outs))],
        scratch_shapes=scratch,
        compiler_params=pltpu.CompilerParams(vmem_limit_bytes=24 * 2**20),
        cost_estimate=cost,
    )(*args)


def local(
    v_init, g_init, spikes, decay, w_local, w_long, lr_src_tile, lr_src_block, lr_tgt_block,
    adj_v_end, adj_g_end,
):
    rows, neurons = v_init.shape
    blocks = neurons // BLK
    tiles = lax.axis_size("azim")
    chips = tiles // 2
    entries = lr_src_tile.shape[0]
    cores = [list(range(core, tiles, 2)) for core in range(2)]
    pair = [(i, i ^ 1) for i in range(tiles)]
    cross = [(i, i + 1) for i in range(1, tiles - 1, 2)]
    cross = cross + [(target, source) for source, target in cross]

    def spread(values, beside=()):
        near = lax.all_to_all(
            values, "azim", split_axis=0, concat_axis=0, tiled=True, axis_index_groups=cores
        )
        near, *beside = lax.optimization_barrier((near, *beside))
        return near, lax.ppermute(near, "azim", pair), *beside

    state = ((rows, neurons), f32)
    source = ((blocks // GROUP, GROUP * rows, 3 * WIDE), bf16)
    fetched = ((entries // GROUP, GROUP * rows, LANES), bf16)
    block_sum = pltpu.VMEM((CAP, blocks, rows, LANES), f32)
    back_scratch = [
        block_sum,
        pltpu.VMEM((CAP, tiles, rows, LANES), f32),
        pltpu.VMEM((tiles, rows, LANES), bf16),
        pltpu.SemaphoreType.DMA,
    ]
    back_outs = [
        ((blocks // GROUP, GROUP * rows, WIDE), bf16),
        ((entries // GROUP, GROUP * rows, WIDE), bf16),
        state,
        ((rows, neurons), bf16),
        ((rows, neurons), bf16),
        ((tiles, rows, LANES), bf16),
    ]
    activity = (spikes[0].astype(f32) * surrogate(v_init)).astype(bf16)
    out = jnp.broadcast_to(activity[None], (chips, rows, neurons))
    entry_rows = jnp.concatenate([lr_src_tile.T, lr_src_block.T, lr_tgt_block.T])
    pack = jnp.concatenate(
        [v_init, g_init, spikes.astype(f32).reshape(STEPS * rows, neurons), decay]
    )
    w_all = w_local.reshape(9 * BLK, neurons)
    beside = call(
        hold_kernel,
        [
            ((8, LANES), jnp.int32), ((1, entries), jnp.int32), state, state,
            ((1, neurons), f32), ((STEPS, rows, neurons), f32),
            (w_all.shape, bf16), (w_long.shape, bf16),
        ],
        (entry_rows, pack, w_all, w_long),
        cost=pl.CostEstimate(flops=0, bytes_accessed=4 * 2**20, transcendentals=0),
    )
    near, far, me, table, v_start, g_start, decay, spikes, w_all, w_long = spread(out, beside)
    voltages, conducts, gates, sources, fetches = [v_start], [g_start], [], [], []
    for moment in range(STEPS - 1):
        if moment > 0:
            near, far = spread(out)
        width = neurons + LANES if moment == 0 else neurons
        outs = [state, state, state, source, fetched, ((chips, rows, width), bf16)]
        scratch = [block_sum]
        if moment == 0:
            scratch.insert(0, pltpu.VMEM((chips, rows, LANES), f32))
        if moment == 1:
            outs.append(((tiles, rows, LANES), jnp.int32))
        results = call(
            functools.partial(forward_kernel, moment),
            outs,
            (near, far, me, table, w_all, w_long, voltages[-1], conducts[-1], decay, spikes),
            scratch,
        )
        if moment == 1:
            wanted = results[6]
        voltage, conduct, gate, source_t, fetched_t, out = results[:6]
        voltages.append(voltage)
        conducts.append(conduct)
        gates.append(gate)
        sources.append(source_t)
        fetches.append(fetched_t)
    near, far = spread(out)
    conduct, source_t, fetched_t, *back = call(
        turn_kernel,
        [state, source, fetched] + back_outs,
        (
            near, far, me, table, w_all, w_long, voltages[-1], conducts[-1], decay, adj_v_end,
            adj_g_end,
        ),
        back_scratch,
        hbm_outs=(8,),
    )
    conducts.append(conduct)
    sources.append(source_t)
    fetches.append(fetched_t)
    adj_volt = adj_v_end
    adjs, gathers = [], []
    for moment in reversed(range(STEPS)):
        adj_t, gathered_t, adj_cond, to_pair, to_cross, placed = back
        adjs.insert(0, adj_t)
        gathers.insert(0, gathered_t)
        arrived = lax.all_to_all(placed, "azim", split_axis=0, concat_axis=0, tiled=True)
        from_pair = lax.ppermute(to_pair, "azim", pair)
        from_cross = lax.ppermute(to_cross, "azim", cross)
        (own,) = call(own_kernel, [state], (adj_t, w_all))
        received = (
            arrived, from_pair, from_cross, own, wanted, adj_volt, voltages[moment],
            conducts[moment + 1], spikes,
        )
        if moment > 0:
            adj_volt, *back = call(
                functools.partial(backward_kernel, moment),
                [state] + back_outs,
                received
                + (
                    adj_cond, voltages[moment - 1], gates[moment - 1], decay, me, table, w_all,
                    w_long,
                ),
                back_scratch,
                hbm_outs=(6,),
            )
    grad_local, grad_long, adj_cond = call(
        grad_kernel,
        [((9 * BLK, neurons), bf16), ((BLK, entries * BLK), bf16), state],
        (*sources, *fetches, *adjs, *gathers, adj_cond),
    )
    (adj_volt,) = call(last_kernel, [state], received, [block_sum])
    return (adj_volt, adj_cond, grad_local.reshape(9, BLK, neurons), grad_long)


def solution(mesh):
    return jax.shard_map(
        local,
        mesh=mesh,
        in_specs=(
            P("groups", "azim"),
            P("groups", "azim"),
            P(None, "groups", "azim"),
            P("groups", "azim"),
            P("groups", None, "azim"),
            P("groups", "azim"),
            P("azim", "groups"),
            P("azim", "groups"),
            P("azim", "groups"),
            P("groups", "azim"),
            P("groups", "azim"),
        ),
        out_specs=(
            P("groups", "azim"),
            P("groups", "azim"),
            P("groups", None, "azim"),
            P("groups", "azim"),
        ),
        check_vma=False,
    )
```

time: 112 us -> 105 us (0.938)
  blocking collectives: 44.6 us -> 30.3 us
  starting transfers between devices: 21.7 us -> 28.7 us
  local copies, waits for them, and re-layouts: 6.05 us -> 1.58 us
  waiting for transfers between devices: 26.2 us -> 28.9 us
  other arithmetic: 0.7 us -> 3.31 us
    all_to_all x4 -> x3, blocking collectives: 44.6 us -> 30.3 us  [spread(): lax.all_to_all(values, 'azim', split_axis=0, concat_axis=0, tiled=True, a...]
    all_to_all x0 -> x1, starting transfers between devices: none -> 7.28 us  [spread(): lax.all_to_all(values, 'azim', split_axis=0, concat_axis=0, tiled=True, a...]
    unnamed x27 -> x8, local copies, waits for them, and re-layouts: 6.04 us -> 0.92 us
    all_to_all x0 -> x1, waiting for transfers between devices: none -> 3.88 us  [spread(): lax.all_to_all(values, 'azim', split_axis=0, concat_axis=0, tiled=True, a...]
    concatenate x0 -> x2, other arithmetic: none -> 1.51 us  [the longest x1 0.81 us: local(): jnp.concatenate([v_init, g_init, spikes.astype(f32).reshape(STEPS * rows,...]
    pallas_call x10 -> x14, Pallas kernels: 11.1 us -> 10.2 us  [call(): pl.pallas_call(kernel, out_shape=[jax.ShapeDtypeStruct(shape, dtype) for...]
  transfers between devices with their start and end apart: 16 -> 17, of which waited for: 11 -> 9; matrix products, arithmetic and copies ran while one was open for 0% -> 2% of each run, Pallas kernels for 1% -> 3%
where the time goes in v2:
time: 105 us; the launch traced here: 104 us
  blocking collectives  30.3 us (29%)
  waiting for transfers between devices  28.9 us (28%)
  starting transfers between devices  28.7 us (27%)
  Pallas kernels  10.2 us (10%)
  other arithmetic  3.31 us (3%)
  local copies, waits for them, and re-layouts  1.58 us (2%)
    all_to_all x3, blocking collectives, spread(): lax.all_to_all(values, 'azim', split_axis=0, concat_axis=0, tiled=True, a...  30.3 us
    all_to_all x4, waiting for transfers between devices, local(): lax.all_to_all(placed, 'azim', split_axis=0, concat_axis=0, tiled=True)  19.5 us
    all_to_all x4, starting transfers between devices, local(): lax.all_to_all(placed, 'azim', split_axis=0, concat_axis=0, tiled=True)  17.3 us
    pallas_call x14, Pallas kernels, call(): pl.pallas_call(kernel, out_shape=[jax.ShapeDtypeStruct(shape, dtype) for...  10.2 us
    all_to_all x1, starting transfers between devices, spread(): lax.all_to_all(values, 'azim', split_axis=0, concat_axis=0, tiled=True, a...  7.28 us
    ppermute x4, waiting for transfers between devices, spread(): return (near, lax.ppermute(near, 'azim', pair), *beside)  5.4 us
    all_to_all x1, waiting for transfers between devices, spread(): lax.all_to_all(values, 'azim', split_axis=0, concat_axis=0, tiled=True, a...  3.88 us
    ppermute x4, starting transfers between devices, local(): from_cross = lax.ppermute(to_cross, 'azim', cross)  2.6 us
  transfers between devices with their start and end apart: 17, of which 9 were waited for; matrix products, arithmetic and copies ran while one was open for 2% of the time, Pallas kernels for 3%

profile of v2, /device:TPU:0, one launch (start us, length us, event | category | flops | bytes accessed | tf_op | source)
XLA Modules:
  0.0 103.8 jit_solution(12188679892835400872)
XLA Ops:
  0.6 0.9 fusion
  1.5 0.7 broadcast_in_dim.2
  2.2 7.3 %all-to-all-start = ((bf16[8,8,1024]{2,1,0:T(8,128)(2,1)}), bf16[8,8,1024]{2,1,0:T(8,128)(2,1)S(1)}, u32[]{:S(2)}, u32[]{:S(2)}) async-start(bf16[8,8,1024]{2,1,0:T(8,128)(2,1)} %broadcast_in_dim.2), calls=%async_computation | async-start | bytes 262144 | tf_op jit(solution)/shard_map/all_to_all | solution.py:429
  9.5 0.9 convert_bitcast_fusion
  10.4 0.7 pad_add_fusion.entry_ref
  11.1 0.8 pad_maximum_fusion.pack_ref
  11.9 0.9 copy-done.2
  12.8 0.1 shard_map.138
  12.9 3.9 %all-to-all-done.refs_0_ = bf16[8,8,1024]{2,1,0:T(8,128)(2,1)S(1)} async-done(((bf16[8,8,1024]{2,1,0:T(8,128)(2,1)}), bf16[8,8,1024]{2,1,0:T(8,128)(2,1)S(1)}, u32[]{:S(2)}, u32[]{:S(2)}) %all-to-all-start) | async-done | bytes 131104 | tf_op jit(solution)/shard_map/all_to_all | solution.py:429
  16.8 1.3 %collective-permute-done.refs_1_ = bf16[8,8,1024]{2,1,0:T(8,128)(2,1)S(1)} collective-permute-done((bf16[8,8,1024]{2,1,0:T(8,128)(2,1)S(1)}, bf16[8,8,1024]{2,1,0:T(8,128)(2,1)S(1)}, u32[]{:S(2)}, u32[]{:S(2)}) %collective-permute-start) | collective-permute-done | bytes 131104 | tf_op jit(solution)/shard_map/ppermute | solution.py:433
  18.2 0.5 shard_map.139
  18.7 10.2 %all_to_all.40.refs_0_ = bf16[8,8,1152]{2,1,0:T(8,128)(2,1)S(1)} all-to-all(bf16[8,8,1152]{2,1,0:T(8,128)(2,1)S(1)} %get-tuple-element.90), channel_id=1, replica_groups={{0,2,4,6,8,10,12,14},{1,3,5,7,9,11,13,15},{16,18,20,22,24,26,28,30},{17..., dimensions={0} | all-to-all | bytes 294912 | tf_op jit(solution)/shard_map/all_to_all | solution.py:429
  28.9 1.4 %collective-permute-done.1.refs_1_ = bf16[8,8,1152]{2,1,0:T(8,128)(2,1)S(1)} collective-permute-done((bf16[8,8,1152]{2,1,0:T(8,128)(2,1)S(1)}, bf16[8,8,1152]{2,1,0:T(8,128)(2,1)S(1)}, u32[]{:S(2)}, u32[]{:S(2)}) %collective-permute-start.1) | collective-permute-done | bytes 147488 | tf_op jit(solution)/shard_map/ppermute | solution.py:433
  30.3 0.6 shard_map.140
  30.9 10.1 %all_to_all.41.refs_0_ = bf16[8,8,1024]{2,1,0:T(8,128)(2,1)S(1)} all-to-all(bf16[8,8,1024]{2,1,0:T(8,128)(2,1)S(1)} %get-tuple-element.93), channel_id=1, replica_groups={{0,2,4,6,8,10,12,14},{1,3,5,7,9,11,13,15},{16,18,20,22,24,26,28,30},{17..., dimensions={0} | all-to-all | bytes 262144 | tf_op jit(solution)/shard_map/all_to_all | solution.py:429
  41.0 1.3 %collective-permute-done.2.refs_1_ = bf16[8,8,1024]{2,1,0:T(8,128)(2,1)S(1)} collective-permute-done((bf16[8,8,1024]{2,1,0:T(8,128)(2,1)S(1)}, bf16[8,8,1024]{2,1,0:T(8,128)(2,1)S(1)}, u32[]{:S(2)}, u32[]{:S(2)}) %collective-permute-start.2) | collective-permute-done | bytes 131104 | tf_op jit(solution)/shard_map/ppermute | solution.py:433
  42.3 0.5 shard_map.141
  42.8 10.0 %all_to_all.42.refs_0_ = bf16[8,8,1024]{2,1,0:T(8,128)(2,1)S(1)} all-to-all(bf16[8,8,1024]{2,1,0:T(8,128)(2,1)S(1)} %get-tuple-element.96), channel_id=1, replica_groups={{0,2,4,6,8,10,12,14},{1,3,5,7,9,11,13,15},{16,18,20,22,24,26,28,30},{17..., dimensions={0} | all-to-all | bytes 262144 | tf_op jit(solution)/shard_map/all_to_all | solution.py:429
  52.8 1.3 %collective-permute-done.3.refs_1_ = bf16[8,8,1024]{2,1,0:T(8,128)(2,1)S(1)} collective-permute-done((bf16[8,8,1024]{2,1,0:T(8,128)(2,1)S(1)}, bf16[8,8,1024]{2,1,0:T(8,128)(2,1)S(1)}, u32[]{:S(2)}, u32[]{:S(2)}) %collective-permute-start.3) | collective-permute-done | bytes 131104 | tf_op jit(solution)/shard_map/ppermute | solution.py:433
  54.2 1.4 %shard_map.142 = (f32[8,1024]{1,0:T(8,128)S(1)}, bf16[4,32,768]{2,1,0:T(8,128)(2,1)S(1)}, bf16[4,32,128]{2,1,0:T(8,128)(2,1)S(1)}, bf16[4,32,256]{2,1,0:T(8,128)...) custom-call(bf16[8,8,1024]{2,1,0:T(8,128)(2,1)S(1)} %all_to_all.42.r, ...), custom_call_target="tpu_custom_call" | custom-call | tf_op jit(solution)/shard_map/pallas_call | solution.py:403
  55.6 3.5 %all-to-all-start.4 = ((bf16[16,8,128]{2,1,0:T(8,128)(2,1)}), bf16[16,8,128]{2,1,0:T(8,128)(2,1)S(1)}, u32[]{:S(2)}, u32[]{:S(2)}) async-start(bf16[16,8,128]{2,1,0:T(8,128)(2,1)} %get-tuple-element.99), calls=%async_computation.4 | async-start | bytes 65536 | tf_op jit(solution)/shard_map/all_to_all | solution.py:516
  59.1 0.3 collective-permute-start.4
  59.4 0.7 collective-permute-start.5
  60.0 0.3 shard_map.143.refs_3_
  60.3 0.0 collective-permute-done.4.refs_1_
  60.4 5.3 %all-to-all-done.4.refs_0_ = bf16[16,8,128]{2,1,0:T(8,128)(2,1)S(1)} async-done(((bf16[16,8,128]{2,1,0:T(8,128)(2,1)}), bf16[16,8,128]{2,1,0:T(8,128)(2,1)S(1)}, u32[]{:S(2)}, u32[]{:S(2)}) %all-to-all-start.4) | async-done | bytes 32800 | tf_op jit(solution)/shard_map/all_to_all | solution.py:516
  65.7 1.2 %shard_map.144 = (f32[8,1024]{1,0:T(8,128)S(1)}, bf16[4,32,256]{2,1,0:T(8,128)(2,1)S(1)}, bf16[4,32,256]{2,1,0:T(8,128)(2,1)S(1)}, f32[8,1024]{1,0:T(8,128)S(1)}...) custom-call(bf16[16,8,128]{2,1,0:T(8,128)(2,1)S(1)} %all-to-all-done.4.refs_0_, ...), custom_call_target="tpu_custom_call" | custom-call | tf_op jit(solution)/shard_map/pallas_call | solution.py:403
  66.9 4.6 %all-to-all-start.5 = ((bf16[16,8,128]{2,1,0:T(8,128)(2,1)}), bf16[16,8,128]{2,1,0:T(8,128)(2,1)S(1)}, u32[]{:S(2)}, u32[]{:S(2)}) async-start(bf16[16,8,128]{2,1,0:T(8,128)(2,1)} %get-tuple-element.107), calls=%async_computation.5 | async-start | bytes 65536 | tf_op jit(solution)/shard_map/all_to_all | solution.py:516
  71.5 0.4 collective-permute-start.6
  71.9 0.7 collective-permute-start.7
  72.5 0.3 shard_map.145.refs_3_
  72.8 0.0 collective-permute-done.6.refs_1_
  72.8 5.2 %all-to-all-done.5.refs_0_ = bf16[16,8,128]{2,1,0:T(8,128)(2,1)S(1)} async-done(((bf16[16,8,128]{2,1,0:T(8,128)(2,1)}), bf16[16,8,128]{2,1,0:T(8,128)(2,1)S(1)}, u32[]{:S(2)}, u32[]{:S(2)}) %all-to-all-start.5) | async-done | bytes 32800 | tf_op jit(solution)/shard_map/all_to_all | solution.py:516
  78.1 1.2 %shard_map.146 = (f32[8,1024]{1,0:T(8,128)S(1)}, bf16[4,32,256]{2,1,0:T(8,128)(2,1)S(1)}, bf16[4,32,256]{2,1,0:T(8,128)(2,1)S(1)}, f32[8,1024]{1,0:T(8,128)S(1)}...) custom-call(bf16[16,8,128]{2,1,0:T(8,128)(2,1)S(1)} %all-to-all-done.5.refs_0_, ...), custom_call_target="tpu_custom_call" | custom-call | tf_op jit(solution)/shard_map/pallas_call | solution.py:403
  79.3 4.6 %all-to-all-start.6 = ((bf16[16,8,128]{2,1,0:T(8,128)(2,1)}), bf16[16,8,128]{2,1,0:T(8,128)(2,1)S(1)}, u32[]{:S(2)}, u32[]{:S(2)}) async-start(bf16[16,8,128]{2,1,0:T(8,128)(2,1)} %get-tuple-element.114), calls=%async_computation.6 | async-start | bytes 65536 | tf_op jit(solution)/shard_map/all_to_all | solution.py:516
  83.9 0.4 collective-permute-start.8
  84.3 0.7 collective-permute-start.9
  84.9 0.3 shard_map.147.refs_3_
  85.2 0.0 collective-permute-done.8.refs_1_
  85.2 5.2 %all-to-all-done.6.refs_0_ = bf16[16,8,128]{2,1,0:T(8,128)(2,1)S(1)} async-done(((bf16[16,8,128]{2,1,0:T(8,128)(2,1)}), bf16[16,8,128]{2,1,0:T(8,128)(2,1)S(1)}, u32[]{:S(2)}, u32[]{:S(2)}) %all-to-all-start.6) | async-done | bytes 32800 | tf_op jit(solution)/shard_map/all_to_all | solution.py:516
  90.5 1.2 %shard_map.148 = (f32[8,1024]{1,0:T(8,128)S(1)}, bf16[4,32,256]{2,1,0:T(8,128)(2,1)S(1)}, bf16[4,32,256]{2,1,0:T(8,128)(2,1)S(1)}, f32[8,1024]{1,0:T(8,128)S(1)}...) custom-call(bf16[16,8,128]{2,1,0:T(8,128)(2,1)S(1)} %all-to-all-done.6.refs_0_, ...), custom_call_target="tpu_custom_call" | custom-call | tf_op jit(solution)/shard_map/pallas_call | solution.py:403
  91.7 4.6 %all-to-all-start.7 = ((bf16[16,8,128]{2,1,0:T(8,128)(2,1)}), bf16[16,8,128]{2,1,0:T(8,128)(2,1)S(1)}, u32[]{:S(2)}, u32[]{:S(2)}) async-start(bf16[16,8,128]{2,1,0:T(8,128)(2,1)} %get-tuple-element.121), calls=%async_computation.7 | async-start | bytes 65536 | tf_op jit(solution)/shard_map/all_to_all | solution.py:516
  96.3 0.4 collective-permute-start.10
  96.7 0.7 collective-permute-start.11
  97.3 0.3 shard_map.149.refs_3_
  97.6 1.6 %shard_map.151 = (bf16[576,1024]{1,0:T(8,128)(2,1)}, bf16[64,1024]{1,0:T(8,128)(2,1)}, f32[8,1024]{1,0:T(8,128)}) custom-call(bf16[4,32,768]{2,1,0:T(8,128)(2,1)S(1)} %get-tuple-element.126.refs_0_, bf16[4,32,768]{2,1,0:T(8,128)(2,1)S(1)} %get-tuple-element.127.refs_1_, bf16[4,32,768]{2,1,0:T(8,128)(2,1)S(1)} %get-tuple-element.128.refs_2_, ...), custom_call_target="tpu_custom_call" | custom-call | tf_op jit(solution)/shard_map/pallas_call | solution.py:403
  99.2 3.7 %all-to-all-done.7.refs_0_ = bf16[16,8,128]{2,1,0:T(8,128)(2,1)S(1)} async-done(((bf16[16,8,128]{2,1,0:T(8,128)(2,1)}), bf16[16,8,128]{2,1,0:T(8,128)(2,1)S(1)}, u32[]{:S(2)}, u32[]{:S(2)}) %all-to-all-start.7) | async-done | bytes 32800 | tf_op jit(solution)/shard_map/all_to_all | solution.py:516
  102.9 0.9 shard_map.150
  (16 shorter events, 0.0 us)
Async XLA Ops:
  0.6 11.3 %copy-start = (bf16[9,64,1024]{2,1,0:T(8,128)(2,1)S(1)}, bf16[9,64,1024]{2,1,0:T(8,128)(2,1)}, u32[]{:S(2)}) copy-start(bf16[9,64,1024]{2,1,0:T(8,128)(2,1)} %param.15) | copy-start | bytes 3538948
  2.2 14.6 %all-to-all-start = ((bf16[8,8,1024]{2,1,0:T(8,128)(2,1)}), bf16[8,8,1024]{2,1,0:T(8,128)(2,1)S(1)}, u32[]{:S(2)}, u32[]{:S(2)}) async-start(bf16[8,8,1024]{2,1,0:T(8,128)(2,1)} %broadcast_in_dim.2), calls=%async_computation | async-start | bytes 262144 | tf_op jit(solution)/shard_map/all_to_all | solution.py:429
  11.9 0.9 copy-start.2
  16.8 1.3 %collective-permute-start = (bf16[8,8,1024]{2,1,0:T(8,128)(2,1)S(1)}, bf16[8,8,1024]{2,1,0:T(8,128)(2,1)S(1)}, u32[]{:S(2)}, u32[]{:S(2)}) collective-permute-start(bf16[8,8,1024]{2,1,0:T(8,128)(2,1)S(1)} %all-to-all-done.refs_0_), channel_id=1, source_target_pairs={{0,1},{1,0},{2,3},{3,2},{4,5},{5,4},{6,7},{7,6},{8,9},{9,8},{10,11... | collective-permute-start | bytes 393224 | tf_op jit(solution)/shard_map/ppermute | solution.py:433
  28.9 1.4 %collective-permute-start.1 = (bf16[8,8,1152]{2,1,0:T(8,128)(2,1)S(1)}, bf16[8,8,1152]{2,1,0:T(8,128)(2,1)S(1)}, u32[]{:S(2)}, u32[]{:S(2)}) collective-permute-start(bf16[8,8,1152]{2,1,0:T(8,128)(2,1)S(1)} %all_to_all.40.refs_0_), channel_id=1, source_target_pairs={{0,1},{1,0},{2,3},{3,2},{4,5},{5,4},{6,7},{7,6},{8,9},{9,8},{10,11... | collective-permute-start | bytes 442376 | tf_op jit(solution)/shard_map/ppermute | solution.py:433
  30.9 23.3 %copy-start.1 = (f32[8,1024]{1,0:T(8,128)S(1)}, f32[8,1024]{1,0:T(8,128)}, u32[]{:S(2)}) copy-start(f32[8,1024]{1,0:T(8,128)} %refs_5_.1) | copy-start | bytes 98308
  30.9 23.3 %copy-start.3 = (f32[8,1024]{1,0:T(8,128)S(1)}, f32[8,1024]{1,0:T(8,128)}, u32[]{:S(2)}) copy-start(f32[8,1024]{1,0:T(8,128)} %refs_10_.1) | copy-start | bytes 98308
  41.0 1.3 %collective-permute-start.2 = (bf16[8,8,1024]{2,1,0:T(8,128)(2,1)S(1)}, bf16[8,8,1024]{2,1,0:T(8,128)(2,1)S(1)}, u32[]{:S(2)}, u32[]{:S(2)}) collective-permute-start(bf16[8,8,1024]{2,1,0:T(8,128)(2,1)S(1)} %all_to_all.41.refs_0_), channel_id=1, source_target_pairs={{0,1},{1,0},{2,3},{3,2},{4,5},{5,4},{6,7},{7,6},{8,9},{9,8},{10,11... | collective-permute-start | bytes 393224 | tf_op jit(solution)/shard_map/ppermute | solution.py:433
  52.8 1.3 %collective-permute-start.3 = (bf16[8,8,1024]{2,1,0:T(8,128)(2,1)S(1)}, bf16[8,8,1024]{2,1,0:T(8,128)(2,1)S(1)}, u32[]{:S(2)}, u32[]{:S(2)}) collective-permute-start(bf16[8,8,1024]{2,1,0:T(8,128)(2,1)S(1)} %all_to_all.42.refs_0_), channel_id=1, source_target_pairs={{0,1},{1,0},{2,3},{3,2},{4,5},{5,4},{6,7},{7,6},{8,9},{9,8},{10,11... | collective-permute-start | bytes 393224 | tf_op jit(solution)/shard_map/ppermute | solution.py:433
  55.6 10.1 %all-to-all-start.4 = ((bf16[16,8,128]{2,1,0:T(8,128)(2,1)}), bf16[16,8,128]{2,1,0:T(8,128)(2,1)S(1)}, u32[]{:S(2)}, u32[]{:S(2)}) async-start(bf16[16,8,128]{2,1,0:T(8,128)(2,1)} %get-tuple-element.99), calls=%async_computation.4 | async-start | bytes 65536 | tf_op jit(solution)/shard_map/all_to_all | solution.py:516
  59.1 1.2 %collective-permute-start.4 = (bf16[8,1024]{1,0:T(8,128)(2,1)S(1)}, bf16[8,1024]{1,0:T(8,128)(2,1)S(1)}, u32[]{:S(2)}, u32[]{:S(2)}) collective-permute-start(bf16[8,1024]{1,0:T(8,128)(2,1)S(1)} %get-tuple-element.100), channel_id=1, source_target_pairs={{0,1},{1,0},{2,3},{3,2},{4,5},{5,4},{6,7},{7,6},{8,9},{9,8},{10,11... | collective-permute-start | bytes 49160 | tf_op jit(solution)/shard_map/ppermute | solution.py:517
  59.4 1.0 collective-permute-start.5
  66.9 11.2 %all-to-all-start.5 = ((bf16[16,8,128]{2,1,0:T(8,128)(2,1)}), bf16[16,8,128]{2,1,0:T(8,128)(2,1)S(1)}, u32[]{:S(2)}, u32[]{:S(2)}) async-start(bf16[16,8,128]{2,1,0:T(8,128)(2,1)} %get-tuple-element.107), calls=%async_computation.5 | async-start | bytes 65536 | tf_op jit(solution)/shard_map/all_to_all | solution.py:516
  71.5 1.4 %collective-permute-start.6 = (bf16[8,1024]{1,0:T(8,128)(2,1)S(1)}, bf16[8,1024]{1,0:T(8,128)(2,1)S(1)}, u32[]{:S(2)}, u32[]{:S(2)}) collective-permute-start(bf16[8,1024]{1,0:T(8,128)(2,1)S(1)} %get-tuple-element.108), channel_id=1, source_target_pairs={{0,1},{1,0},{2,3},{3,2},{4,5},{5,4},{6,7},{7,6},{8,9},{9,8},{10,11... | collective-permute-start | bytes 49160 | tf_op jit(solution)/shard_map/ppermute | solution.py:517
  71.9 1.0 collective-permute-start.7
  79.3 11.2 %all-to-all-start.6 = ((bf16[16,8,128]{2,1,0:T(8,128)(2,1)}), bf16[16,8,128]{2,1,0:T(8,128)(2,1)S(1)}, u32[]{:S(2)}, u32[]{:S(2)}) async-start(bf16[16,8,128]{2,1,0:T(8,128)(2,1)} %get-tuple-element.114), calls=%async_computation.6 | async-start | bytes 65536 | tf_op jit(solution)/shard_map/all_to_all | solution.py:516
  83.9 1.4 %collective-permute-start.8 = (bf16[8,1024]{1,0:T(8,128)(2,1)S(1)}, bf16[8,1024]{1,0:T(8,128)(2,1)S(1)}, u32[]{:S(2)}, u32[]{:S(2)}) collective-permute-start(bf16[8,1024]{1,0:T(8,128)(2,1)S(1)} %get-tuple-element.115), channel_id=1, source_target_pairs={{0,1},{1,0},{2,3},{3,2},{4,5},{5,4},{6,7},{7,6},{8,9},{9,8},{10,11... | collective-permute-start | bytes 49160 | tf_op jit(solution)/shard_map/ppermute | solution.py:517
  84.3 1.0 collective-permute-start.9
  91.7 11.2 %all-to-all-start.7 = ((bf16[16,8,128]{2,1,0:T(8,128)(2,1)}), bf16[16,8,128]{2,1,0:T(8,128)(2,1)S(1)}, u32[]{:S(2)}, u32[]{:S(2)}) async-start(bf16[16,8,128]{2,1,0:T(8,128)(2,1)} %get-tuple-element.121), calls=%async_computation.7 | async-start | bytes 65536 | tf_op jit(solution)/shard_map/all_to_all | solution.py:516
  96.3 2.9 %collective-permute-start.10 = (bf16[8,1024]{1,0:T(8,128)(2,1)S(1)}, bf16[8,1024]{1,0:T(8,128)(2,1)S(1)}, u32[]{:S(2)}, u32[]{:S(2)}) collective-permute-start(bf16[8,1024]{1,0:T(8,128)(2,1)S(1)} %get-tuple-element.122), channel_id=1, source_target_pairs={{0,1},{1,0},{2,3},{3,2},{4,5},{5,4},{6,7},{7,6},{8,9},{9,8},{10,11... | collective-permute-start | bytes 49160 | tf_op jit(solution)/shard_map/ppermute | solution.py:517
  96.7 2.5 %collective-permute-start.11 = (bf16[8,1024]{1,0:T(8,128)(2,1)S(1)}, bf16[8,1024]{1,0:T(8,128)(2,1)S(1)}, u32[]{:S(2)}, u32[]{:S(2)}) collective-permute-start(bf16[8,1024]{1,0:T(8,128)(2,1)S(1)} %get-tuple-element.123), channel_id=1, source_target_pairs={{1,2},{3,4},{5,6},{7,8},{9,10},{11,12},{13,14},{2,1},{4,3},{6,5},{... | collective-permute-start | bytes 49160 | tf_op jit(solution)/shard_map/ppermute | solution.py:518

commit v3 on v2

v3 whole, which is shorter than its diff:
```python
import functools

import jax
import jax.numpy as jnp
from jax import lax
from jax.experimental import pallas as pl
from jax.experimental.pallas import tpu as pltpu
from jax.sharding import PartitionSpec as P

BLK = 64
CAP = 2
STEPS = 4
LANES = 128
GROUP = 4
WIDE = GROUP * BLK
SIDE = 3 * BLK

f32 = jnp.float32
bf16 = jnp.bfloat16


def surrogate(voltage):
    return jax.nn.sigmoid(2.0 * (voltage - 1.0))


def lane_half(rows):
    return lax.broadcasted_iota(jnp.int32, (rows, LANES), 1) // BLK


def half_only(piece, half, which):
    return jnp.where(half == which, piece, 0.0)


def half_pair(first, second, half):
    return jnp.where(half == 0, first, second)


def swapped(piece):
    return pltpu.roll(piece, BLK, 1)


def chunks_of(values):
    return [values[:, c * LANES : (c + 1) * LANES] for c in range(values.shape[1] // LANES)]


def odd_chunks(chunks, half):
    turned = [swapped(piece) for piece in chunks]
    zero = jnp.zeros_like(chunks[0])
    return [
        half_pair(left, right, half) for left, right in zip([zero] + turned, turned + [zero])
    ]


def product(left, right):
    return lax.dot_general(left, right, (((1,), (0,)), ((), ())), preferred_element_type=f32)


def product_back(left, right):
    return lax.dot_general(left, right, (((1,), (1,)), ((), ())), preferred_element_type=f32)


def product_over(left, right):
    return lax.dot_general(left, right, (((0,), (0,)), ((), ())), preferred_element_type=f32)


def stacked(pieces):
    return jnp.concatenate(pieces, axis=0)


def folded(acc_ref, half):
    totals = []
    for block in range(acc_ref.shape[1]):
        piece = half_pair(acc_ref[0, block], acc_ref[1, block], half)
        totals.append(piece + swapped(piece))
    return [half_pair(totals[b], totals[b + 1], half) for b in range(0, len(totals), 2)]


def in_group(tile):
    return (tile ^ (tile >> 1)) & 1


def source_code(tile, block, target, me):
    far = in_group(tile) ^ in_group(me)
    chunk = (tile >> 1) * 8 + (block >> 1)
    return ((chunk * 2 + far) * 2 + (block & 1)) * 16 + target


def source_of(code):
    return code >> 9, (code >> 6) & 7, (code >> 5) & 1, (code >> 4) & 1, code & 15


def slot_code(tile, rank, target):
    return (tile * CAP + rank) * 16 + target


def slot_of(code):
    return code >> 5, (code >> 4) & 1, code & 15


def start_kernel(*refs):
    heads, rest = refs[:3], refs[3:]
    count = (len(rest) - 8) // 2
    held, (out_ref, me_ref, table_ref), kept = rest[:count], rest[count : count + 3], rest[count + 3 :]
    rows_of, ask_ref, sems = kept[count : count + 3], kept[count + 3], kept[count + 4]
    kept = kept[:count]
    copies = [
        pltpu.make_async_copy(source, target, sems.at[number])
        for number, (source, target) in enumerate(zip((*heads, *held), (*rows_of, *kept)))
    ]
    for copy in copies[3:6] + copies[:3] + copies[6:]:
        copy.start()
    chips = out_ref.shape[0]
    v_ref, spikes_ref = kept[:2]
    rows, neurons = v_ref.shape
    entries = table_ref.shape[1]
    for copy in copies[3:5]:
        copy.wait()
    activity = (spikes_ref[0].astype(f32) * surrogate(v_ref[...])).astype(bf16)
    for chip in range(chips):
        out_ref[chip, :, :neurons] = activity
    me = lax.axis_index("azim")
    me_ref[...] = jnp.full(me_ref.shape, me, jnp.int32)
    ask_ref[...] = jnp.zeros_like(ask_ref)
    across = lax.broadcasted_iota(jnp.int32, (entries, entries), 1)
    down = lax.broadcasted_iota(jnp.int32, (entries, entries), 0)
    lane = lax.broadcasted_iota(jnp.int32, (rows, LANES), 1)
    for copy in copies[:3]:
        copy.wait()
    tiles, block, target = (ref[...] for ref in rows_of)
    tiles_down = jnp.sum(
        jnp.where(across == down, tiles.astype(f32), 0.0), axis=1, keepdims=True
    ).astype(jnp.int32)
    earlier = (tiles_down == tiles) & (down < across)
    rank = jnp.sum(jnp.where(earlier, 1.0, 0.0), axis=0, keepdims=True).astype(jnp.int32)
    table = jnp.concatenate(
        [source_code(tiles, block, target, me), slot_code(tiles, rank, target)], axis=0
    )
    table_ref[...] = table
    for entry in range(entries):
        tile, slot, _ = slot_of(table[1, entry])
        _, chunk, _, side, _ = source_of(table[0, entry])
        asked = (2 * chunk + side).astype(f32)
        place = CAP * (tile & 1) + slot
        ask_ref[tile >> 1] = jnp.where(lane == place, asked, ask_ref[tile >> 1])
    for chip in range(chips):
        out_ref[chip, :, neurons:] = ask_ref[chip].astype(bf16)
    for copy in copies[5:]:
        copy.wait()


def tile_drive(values, weights, source_ref, half):
    rows = values.shape[0]
    even = chunks_of(values)
    odd = odd_chunks(even, half)
    even = even + [jnp.zeros((rows, LANES), f32)]
    drive = []
    for group in range((len(even) - 1) * 2 // GROUP):
        pieces = []
        for block in range(GROUP * group, GROUP * (group + 1)):
            line = even if block % 2 else odd
            pieces.append((line[block // 2], line[block // 2 + 1]))
        source = jnp.concatenate(
            [stacked([piece[k] for piece in pieces]) for k in range(2)], axis=1
        ).astype(bf16)
        source_ref[group] = source
        total = product(source[:, :SIDE], weights(slice(group * WIDE, (group + 1) * WIDE)))
        for pair in range(GROUP // 2):
            lanes = slice(pair * LANES, (pair + 1) * LANES)
            at = 2 * pair * rows
            drive.append(
                half_pair(
                    total[at : at + rows, lanes], total[at + rows : at + 2 * rows, lanes], half
                )
            )
    return drive


def near_kernel(near_ref, me_ref, w_ref, drive_out, source_ref):
    chips = near_ref.shape[0]
    neurons = w_ref.shape[2]
    half = lane_half(near_ref.shape[1])
    me = me_ref[...][0, 0]
    chip = me >> 1
    core = me & 1
    own = near_ref[chip, :, :neurons].astype(f32)
    beyond = chip - 1 + 2 * core
    cross = near_ref[jnp.clip(beyond, 0, chips - 1), :, :neurons].astype(f32)
    cross = jnp.where((beyond >= 0) & (beyond < chips), cross, 0.0)
    first = tile_drive(own, lambda columns: w_ref[1, :, columns], source_ref.at[0], half)
    second = tile_drive(
        cross, lambda columns: w_ref[2 * core, :, columns], source_ref.at[1], half
    )
    drive_out[...] = jnp.concatenate([a + b for a, b in zip(first, second)], axis=1)


def forward_part(
    near_ref, far_ref, partial_ref, me_ref, table_ref, w_ref, w_long_ref, source_ref, fetched_ref,
    acc_ref,
):
    rows = near_ref.shape[1]
    neurons = w_ref.shape[2]
    entries = table_ref.shape[1]
    half = lane_half(rows)
    table = table_ref[...]
    me = me_ref[...][0, 0]
    acc_ref[...] = jnp.zeros_like(acc_ref)
    for group in range(entries // GROUP):
        columns = slice(group * WIDE, (group + 1) * WIDE)
        pieces, targets = [], []
        for entry in range(GROUP * group, GROUP * (group + 1)):
            place, chunk, far, side, target = source_of(table[0, entry])
            targets.append(target)
            lanes = pl.ds(pl.multiple_of(chunk * LANES, LANES), LANES)
            piece = jnp.where(far == 0, near_ref[place, :, lanes], far_ref[place, :, lanes])
            pieces.append(half_only(piece.astype(f32), half, side))
        fetched = stacked(pieces).astype(bf16)
        fetched_ref[group] = fetched
        weights = w_long_ref[:, columns]
        total = product(fetched, stacked([weights, weights]))
        for at, target in enumerate(targets):
            lanes = slice(at // 2 * LANES, (at // 2 + 1) * LANES)
            acc_ref[at % 2, target] += total[at * rows : (at + 1) * rows, lanes]
    mate = far_ref[me >> 1, :, :neurons].astype(f32)
    drive = tile_drive(
        mate, lambda columns: w_ref[2 - 2 * (me & 1), :, columns], source_ref, half
    )
    extra = folded(acc_ref, half)
    return partial_ref[...] + jnp.concatenate([a + b for a, b in zip(drive, extra)], axis=1)


def forward_kernel(moment, *refs):
    (
        near_ref, far_ref, partial_ref, me_ref, table_ref, w_ref, w_long_ref, v_ref, g_ref,
        decay_ref, spikes_ref,
    ) = refs[:11]
    v_out, g_out, gate_out, source_ref, fetched_ref, act_ref = refs[11:17]
    acc_ref = refs[-1]
    rows, neurons = v_ref.shape
    chips = act_ref.shape[0]
    drive = forward_part(
        near_ref, far_ref, partial_ref, me_ref, table_ref, w_ref, w_long_ref, source_ref,
        fetched_ref, acc_ref,
    )
    voltage = v_ref[...]
    conduct = decay_ref[...] * g_ref[...] + jax.nn.softplus(drive)
    voltage = (
        voltage + 0.1 * (conduct * (3.0 - voltage) - voltage) - spikes_ref[moment].astype(f32)
    )
    v_out[...] = voltage
    g_out[...] = conduct
    gate_out[...] = jax.nn.sigmoid(drive)
    activity = (spikes_ref[moment + 1].astype(f32) * surrogate(voltage)).astype(bf16)
    for chip in range(chips):
        act_ref[chip] = activity
    if moment == 0:
        wanted_ref = refs[17]
        core = me_ref[...][0, 0] & 1
        mine = in_group(me_ref[...][0, 0])
        for chip in range(chips):
            near_core = mine ^ (chip & 1)
            for ref, place in ((near_ref, near_core), (far_ref, 1 - near_core)):
                place = 2 * chip + place
                asked = ref[chip, :, neurons:].astype(f32)
                asked = jnp.where(core == 1, pltpu.roll(asked, LANES - CAP, 1), asked)
                asked = asked + 16.0 * pltpu.roll(asked, LANES - 1, 1)
                wanted_ref[place] = asked.astype(jnp.int32)


def toward_tile(side, adj_ref, w_ref):
    groups, rows, _ = adj_ref.shape
    rows = rows // GROUP
    blocks = groups * GROUP
    half = lane_half(rows)
    zero = jnp.zeros((rows, LANES), f32)
    even = [zero] * (blocks // 2 + 1)
    odd = [zero] * (blocks // 2 + 1)
    for group in range(groups):
        columns = slice(group * WIDE, (group + 1) * WIDE)
        back = product_back(adj_ref[group], w_ref[side, :, columns])
        for at in range(GROUP):
            block = GROUP * group + at
            line = even if block % 2 else odd
            lower = back[at * rows : (at + 1) * rows, :LANES]
            upper = back[at * rows : (at + 1) * rows, LANES:]
            upper = jnp.concatenate([upper, jnp.zeros_like(upper)], axis=1)
            line[block // 2] = line[block // 2] + lower
            line[block // 2 + 1] = line[block // 2 + 1] + upper
    turned = [swapped(piece) for piece in odd]
    return jnp.concatenate(
        [even[c] + half_pair(turned[c], turned[c + 1], half) for c in range(blocks // 2)], axis=1
    )


def backward_part(
    adj_cond, adj_volt, voltage, gate, decay, me_ref, table_ref, w_ref, w_long_ref,
    adj_ref, gathered_ref, cond_out, pair_out, cross_out, placed_out, acc_ref, slot_ref,
    stage_ref, sem,
):
    rows, neurons = voltage.shape
    blocks = neurons // BLK
    entries = table_ref.shape[1]
    half = lane_half(rows)
    table = table_ref[...]
    core = me_ref[...][0, 0] & 1
    total_g = adj_cond + adj_volt * 0.1 * (3.0 - voltage)
    adj_drive = (total_g * gate).astype(bf16).astype(f32)
    cond_out[...] = decay * total_g
    chunks = chunks_of(adj_drive)
    zero = jnp.zeros((rows, LANES), f32)
    for number, piece in enumerate(chunks):
        turned = swapped(piece)
        acc_ref[0, 2 * number] = half_pair(piece, turned, half)
        acc_ref[0, 2 * number + 1] = half_pair(turned, piece, half)
    slot_ref[...] = jnp.zeros_like(slot_ref)
    for group in range(entries // GROUP):
        columns = slice(group * WIDE, (group + 1) * WIDE)
        left, right, slots = [], [], []
        for at in range(GROUP):
            tile, rank, target = slot_of(table[1, GROUP * group + at])
            slots.append((rank, tile))
            piece = half_only(acc_ref[0, target], half, at % 2)
            left.append(piece if at < 2 else zero)
            right.append(zero if at < 2 else piece)
        gathered = jnp.concatenate([stacked(left), stacked(right)], axis=1).astype(bf16)
        gathered_ref[group] = gathered
        weights = w_long_ref[:, columns]
        back = product_back(gathered, stacked([weights, weights]))
        for at, slot in enumerate(slots):
            slot_ref[slot] = back[at * rows : (at + 1) * rows]
    for tile in range(stage_ref.shape[0]):
        stage_ref[tile] = half_pair(slot_ref[0, tile], slot_ref[1, tile], half).astype(bf16)
    copy = pltpu.make_async_copy(stage_ref, placed_out, sem)
    copy.start()
    for group in range(blocks // GROUP):
        left = stacked([half_only(chunks[2 * group], half, k) for k in range(2)] + [zero, zero])
        right = stacked(
            [zero, zero] + [half_only(chunks[2 * group + 1], half, k) for k in range(2)]
        )
        adj_ref[group] = jnp.concatenate([left, right], axis=1).astype(bf16)
    cross_out[...] = toward_tile(2 * core, adj_ref, w_ref).astype(bf16)
    pair_out[...] = toward_tile(2 - 2 * core, adj_ref, w_ref).astype(bf16)
    copy.wait()


def own_kernel(
    moment, adj_ref, w_ref, adj_v_ref, v_ref, g_ref, spikes_ref, base_out, gain_out
):
    slope = surrogate(v_ref[...])
    gain = spikes_ref[moment].astype(f32) * (2.0 * slope * (1.0 - slope))
    gain_out[...] = gain
    base_out[...] = (
        adj_v_ref[...] * (0.9 - 0.1 * g_ref[...]) + toward_tile(1, adj_ref, w_ref) * gain
    )


def turn_kernel(*refs):
    (
        near_ref, far_ref, partial_ref, me_ref, table_ref, w_ref, w_long_ref, v_ref, g_ref,
        decay_ref, adj_v_ref, adj_g_ref,
    ) = refs[:12]
    g_out, source_ref, fetched_ref = refs[12:15]
    acc_ref = refs[21]
    drive = forward_part(
        near_ref, far_ref, partial_ref, me_ref, table_ref, w_ref, w_long_ref, source_ref,
        fetched_ref, acc_ref,
    )
    decay = decay_ref[...]
    g_out[...] = decay * g_ref[...] + jax.nn.softplus(drive)
    backward_part(
        adj_g_ref[...], adj_v_ref[...], v_ref[...], jax.nn.sigmoid(drive), decay,
        me_ref, table_ref, w_ref, w_long_ref, *refs[15:],
    )


def receive_part(placed_ref, pair_ref, cross_ref, base_ref, gain_ref, wanted_ref, acc_ref):
    half = lane_half(base_ref.shape[0])
    acc_ref[...] = jnp.zeros_like(acc_ref)
    tiles = placed_ref.shape[0]
    for first in range(0, tiles, 3):
        count = min(3, tiles - first)
        codes = wanted_ref[first, 0:1, :]
        for at in range(1, count):
            codes = codes + wanted_ref[first + at, 0:1, :] * 256**at
        code = codes[0, 0]
        for at in range(count):
            arrived = placed_ref[first + at].astype(f32)
            for slot in range(CAP):
                acc_ref[slot, (code >> (8 * at + 4 * slot)) & 15] += arrived
    rest = pair_ref[...].astype(f32) + cross_ref[...].astype(f32)
    rest = rest + jnp.concatenate(folded(acc_ref, half), axis=1)
    return base_ref[...] + rest * gain_ref[...]


def backward_kernel(*refs):
    adj_g_ref, v_ref, gate_ref, decay_ref, me_ref, table_ref, w_ref, w_long_ref = refs[6:14]
    adj_v_out = refs[14]
    acc_ref = refs[21]
    adj_volt = receive_part(*refs[:6], acc_ref)
    adj_v_out[...] = adj_volt
    backward_part(
        adj_g_ref[...], adj_volt, v_ref[...], gate_ref[...], decay_ref[...],
        me_ref, table_ref, w_ref, w_long_ref, *refs[15:],
    )


def last_kernel(*refs):
    refs[6][...] = receive_part(*refs[:6], refs[7])


def grad_kernel(*refs):
    near, far, fetched, adjs, gathered = (refs[k * STEPS : (k + 1) * STEPS] for k in range(5))
    me_ref, cond_ref, local_ref, long_ref, cond_out = refs[5 * STEPS :]
    cond_out[...] = cond_ref[...]
    core = me_ref[...][0, 0] & 1
    for group in range(adjs[0].shape[0]):
        columns = slice(group * WIDE, (group + 1) * WIDE)
        adj = stacked([ref[group] for ref in adjs])
        for side, sources in (
            (1, [ref[0, group] for ref in near]),
            (2 * core, [ref[1, group] for ref in near]),
            (2 - 2 * core, [ref[group] for ref in far]),
        ):
            total = product_over(stacked(sources)[:, :SIDE], adj)
            local_ref[side, :, columns] = total.astype(bf16)
    for group in range(gathered[0].shape[0]):
        columns = slice(group * WIDE, (group + 1) * WIDE)
        total = product_over(
            stacked([ref[group] for ref in fetched]), stacked([ref[group] for ref in gathered])
        )
        long_ref[:, columns] = (total[:BLK] + total[BLK:]).astype(bf16)


def call(kernel, outs, args, scratch=(), hbm_outs=(), hbm_args=False):
    vmem = pl.BlockSpec(memory_space=pltpu.VMEM)
    hbm = pl.BlockSpec(memory_space=pltpu.HBM)
    if hbm_args:
        args = [pltpu.with_memory_space_constraint(array, pltpu.HBM) for array in args]
    return pl.pallas_call(
        kernel,
        out_shape=[jax.ShapeDtypeStruct(shape, dtype) for shape, dtype in outs],
        in_specs=[hbm if hbm_args else vmem] * len(args),
        out_specs=[hbm if k in hbm_outs else vmem for k in range(len(outs))],
        scratch_shapes=scratch,
        compiler_params=pltpu.CompilerParams(vmem_limit_bytes=24 * 2**20),
    )(*args)


def local(
    v_init, g_init, spikes, decay, w_local, w_long, lr_src_tile, lr_src_block, lr_tgt_block,
    adj_v_end, adj_g_end,
):
    rows, neurons = v_init.shape
    blocks = neurons // BLK
    tiles = lax.axis_size("azim")
    chips = tiles // 2
    entries = lr_src_tile.shape[0]
    members = [[tile for tile in range(tiles) if in_group(tile) == k] for k in range(2)]
    pair = [(i, i ^ 1) for i in range(tiles)]
    cross = [(i, i + 1) for i in range(1, tiles - 1, 2)]
    cross = cross + [(target, source) for source, target in cross]

    def spread(values):
        near = lax.all_to_all(
            values, "azim", split_axis=0, concat_axis=0, tiled=True, axis_index_groups=members
        )
        return near, lax.ppermute(near, "azim", pair)

    state = ((rows, neurons), f32)
    source = ((blocks // GROUP, GROUP * rows, WIDE), bf16)
    sources = ((2, *source[0]), bf16)
    fetched = ((entries // GROUP, GROUP * rows, LANES), bf16)
    block_sum = pltpu.VMEM((CAP, blocks, rows, LANES), f32)
    back_scratch = [
        block_sum,
        pltpu.VMEM((CAP, tiles, rows, LANES), f32),
        pltpu.VMEM((tiles, rows, LANES), bf16),
        pltpu.SemaphoreType.DMA,
    ]
    back_outs = [
        ((blocks // GROUP, GROUP * rows, WIDE), bf16),
        ((entries // GROUP, GROUP * rows, WIDE), bf16),
        state,
        ((rows, neurons), bf16),
        ((rows, neurons), bf16),
        ((tiles, rows, LANES), bf16),
    ]
    held = (
        v_init, spikes, w_local.reshape(3, SIDE, neurons), w_long, g_init, decay, adj_v_end,
        adj_g_end,
    )
    entry_row = pltpu.VMEM((1, entries), jnp.int32)
    out, me, table, v_start, spikes, w_all, w_long, g_start, decay, adj_volt, adj_cond = call(
        start_kernel,
        [
            ((chips, rows, neurons + LANES), bf16), ((8, LANES), jnp.int32),
            ((2, entries), jnp.int32),
        ]
        + [(array.shape, array.dtype) for array in held],
        (lr_src_tile.T, lr_src_block.T, lr_tgt_block.T, *held),
        [
            entry_row, entry_row, entry_row, pltpu.VMEM((chips, rows, LANES), f32),
            pltpu.SemaphoreType.DMA((3 + len(held),)),
        ],
        hbm_args=True,
    )
    voltages, conducts, gates, nears, fars, fetches = [v_start], [g_start], [], [], [], []
    for moment in range(STEPS - 1):
        near, far = spread(out)
        partial, near_t = call(near_kernel, [state, sources], (near, me, w_all))
        nears.append(near_t)
        outs = [state, state, state, source, fetched, ((chips, rows, neurons), bf16)]
        if moment == 0:
            outs.append(((tiles, rows, LANES), jnp.int32))
        results = call(
            functools.partial(forward_kernel, moment),
            outs,
            (
                near, far, partial, me, table, w_all, w_long, voltages[-1], conducts[-1], decay,
                spikes,
            ),
            [block_sum],
        )
        if moment == 0:
            wanted = results[6]
        voltage, conduct, gate, far_t, fetched_t, out = results[:6]
        voltages.append(voltage)
        conducts.append(conduct)
        gates.append(gate)
        fars.append(far_t)
        fetches.append(fetched_t)
    near, far = spread(out)
    partial, near_t = call(near_kernel, [state, sources], (near, me, w_all))
    nears.append(near_t)
    conduct, far_t, fetched_t, *back = call(
        turn_kernel,
        [state, source, fetched] + back_outs,
        (
            near, far, partial, me, table, w_all, w_long, voltages[-1], conducts[-1], decay,
            adj_volt, adj_cond,
        ),
        back_scratch,
        hbm_outs=(8,),
    )
    conducts.append(conduct)
    fars.append(far_t)
    fetches.append(fetched_t)
    adjs, gathers = [], []
    for moment in reversed(range(STEPS)):
        adj_t, gathered_t, adj_cond, to_pair, to_cross, placed = back
        adjs.insert(0, adj_t)
        gathers.insert(0, gathered_t)
        arrived = lax.all_to_all(placed, "azim", split_axis=0, concat_axis=0, tiled=True)
        from_cross = lax.ppermute(to_cross, "azim", cross)
        from_pair = lax.ppermute(to_pair, "azim", pair)
        base, gain = call(
            functools.partial(own_kernel, moment),
            [state, state],
            (adj_t, w_all, adj_volt, voltages[moment], conducts[moment + 1], spikes),
        )
        received = (arrived, from_pair, from_cross, base, gain, wanted)
        if moment > 0:
            adj_volt, *back = call(
                backward_kernel,
                [state] + back_outs,
                received
                + (
                    adj_cond, voltages[moment - 1], gates[moment - 1], decay, me, table, w_all,
                    w_long,
                ),
                back_scratch,
                hbm_outs=(6,),
            )
    grad_local, grad_long, adj_cond = call(
        grad_kernel,
        [((3, SIDE, neurons), bf16), ((BLK, entries * BLK), bf16), state],
        (*nears, *fars, *fetches, *adjs, *gathers, me, adj_cond),
    )
    (adj_volt,) = call(last_kernel, [state], received, [block_sum])
    return (adj_volt, adj_cond, grad_local.reshape(9, BLK, neurons), grad_long)


def solution(mesh):
    return jax.shard_map(
        local,
        mesh=mesh,
        in_specs=(
            P("groups", "azim"),
            P("groups", "azim"),
            P(None, "groups", "azim"),
            P("groups", "azim"),
            P("groups", None, "azim"),
            P("groups", "azim"),
            P("azim", "groups"),
            P("azim", "groups"),
            P("azim", "groups"),
            P("groups", "azim"),
            P("groups", "azim"),
        ),
        out_specs=(
            P("groups", "azim"),
            P("groups", "azim"),
            P("groups", None, "azim"),
            P("groups", "azim"),
        ),
        check_vma=False,
    )
```

time: 105 us -> 104 us (level)
  blocking collectives: 30.3 us -> 43.8 us
  waiting for transfers between devices: 28.9 us -> 22.1 us
  starting transfers between devices: 28.7 us -> 23.6 us
  other arithmetic: 3.31 us -> 0 us
  Pallas kernels: 10.2 us -> 12.8 us
  local copies, waits for them, and re-layouts: 1.58 us -> 0 us
    all_to_all x3 -> x4, blocking collectives: 30.3 us -> 43.8 us  [spread(): lax.all_to_all(values, 'azim', split_axis=0, concat_axis=0, tiled=True, a...]
    all_to_all x1 -> x0, starting transfers between devices: 7.28 us -> none  [spread(): lax.all_to_all(values, 'azim', split_axis=0, concat_axis=0, tiled=True, a...]
    all_to_all x1 -> x0, waiting for transfers between devices: 3.88 us -> none  [spread(): lax.all_to_all(values, 'azim', split_axis=0, concat_axis=0, tiled=True, a...]
    ppermute x4, waiting for transfers between devices: 5.4 us -> 2.61 us  [spread(): return (near, lax.ppermute(near, 'azim', pair))]
    pallas_call x14 -> x18, Pallas kernels: 10.2 us -> 12.8 us  [call(): pl.pallas_call(kernel, out_shape=[jax.ShapeDtypeStruct(shape, dtype) for...]
    ppermute x4, starting transfers between devices: 0.01 us -> 2.13 us  [spread(): return (near, lax.ppermute(near, 'azim', pair))]
    concatenate x2 -> x0, other arithmetic: 1.51 us -> none  [the longest x1 0.81 us: local(): jnp.concatenate([v_init, g_init, spikes.astype(f32).reshape(STEPS * rows,...]
  transfers between devices with their start and end apart: 17 -> 16, of which waited for: 9 -> 8; matrix products, arithmetic and copies ran while one was open for 2% -> 0% of each run, Pallas kernels for 3% -> 4%
where the time goes in v3:
time: 104 us; the launch traced here: 103 us
  blocking collectives  43.8 us (42%)
  starting transfers between devices  23.6 us (23%)
  waiting for transfers between devices  22.1 us (21%)
  Pallas kernels  12.8 us (12%)
    all_to_all x4, blocking collectives, spread(): lax.all_to_all(values, 'azim', split_axis=0, concat_axis=0, tiled=True, a...  43.8 us
    all_to_all x4, waiting for transfers between devices, local(): lax.all_to_all(placed, 'azim', split_axis=0, concat_axis=0, tiled=True)  19.4 us
    all_to_all x4, starting transfers between devices, local(): lax.all_to_all(placed, 'azim', split_axis=0, concat_axis=0, tiled=True)  17.3 us
    pallas_call x18, Pallas kernels, call(): pl.pallas_call(kernel, out_shape=[jax.ShapeDtypeStruct(shape, dtype) for...  12.8 us
    ppermute x4, waiting for transfers between devices, spread(): return (near, lax.ppermute(near, 'azim', pair))  2.61 us
    ppermute x4, starting transfers between devices, local(): from_cross = lax.ppermute(to_cross, 'azim', cross)  2.6 us
    ppermute x4, starting transfers between devices, spread(): return (near, lax.ppermute(near, 'azim', pair))  2.13 us
  transfers between devices with their start and end apart: 16, of which 8 were waited for; matrix products, arithmetic and copies ran while one was open for 0% of the time, Pallas kernels for 4%

profile of v3, /device:TPU:0, one launch (start us, length us, event | category | flops | bytes accessed | tf_op | source)
XLA Modules:
  0.0 103.1 jit_solution(15075923611426538600)
XLA Ops:
  0.6 1.5 %shard_map.138 = (bf16[8,8,1152]{2,1,0:T(8,128)(2,1)S(1)}, s32[8,128]{1,0:T(8,128)S(1)}, s32[2,16]{1,0:T(2,128)S(1)}, f32[8,1024]{1,0:T(8,128)S(1)}, s32[4,8,102...) custom-call(s32[1,16]{1,0:T(1,128)} %bitcast.6, ...), custom_call_target="tpu_custom_call" | custom-call | tf_op jit(solution)/shard_map/pallas_call | solution.py:438
  2.2 13.7 %all_to_all.40.near_ref.refs_0_ = bf16[8,8,1152]{2,1,0:T(8,128)(2,1)S(1)} all-to-all(bf16[8,8,1152]{2,1,0:T(8,128)(2,1)S(1)} %get-tuple-element.83), channel_id=1, replica_groups={{0,3,4,7,8,11,12,15},{1,2,5,6,9,10,13,14},{16,19,20,23,24,27,28,31},{17..., dimensions={0} | all-to-all | bytes 294912 | tf_op jit(solution)/shard_map/all_to_all | solution.py:463
  15.8 0.7 collective-permute-start
  16.6 0.3 shard_map.139
  16.9 0.7 collective-permute-done.refs_1_
  17.6 0.5 shard_map.140
  18.1 10.1 %all_to_all.41.near_ref.refs_0_ = bf16[8,8,1024]{2,1,0:T(8,128)(2,1)S(1)} all-to-all(bf16[8,8,1024]{2,1,0:T(8,128)(2,1)S(1)} %get-tuple-element.93), channel_id=1, replica_groups={{0,3,4,7,8,11,12,15},{1,2,5,6,9,10,13,14},{16,19,20,23,24,27,28,31},{17..., dimensions={0} | all-to-all | bytes 262144 | tf_op jit(solution)/shard_map/all_to_all | solution.py:463
  28.2 0.5 collective-permute-start.1
  28.7 0.3 shard_map.141
  29.0 0.6 collective-permute-done.1.refs_1_
  29.7 0.5 shard_map.142
  30.1 10.0 %all_to_all.42.near_ref.refs_0_ = bf16[8,8,1024]{2,1,0:T(8,128)(2,1)S(1)} all-to-all(bf16[8,8,1024]{2,1,0:T(8,128)(2,1)S(1)} %get-tuple-element.97), channel_id=1, replica_groups={{0,3,4,7,8,11,12,15},{1,2,5,6,9,10,13,14},{16,19,20,23,24,27,28,31},{17..., dimensions={0} | all-to-all | bytes 262144 | tf_op jit(solution)/shard_map/all_to_all | solution.py:463
  40.1 0.5 collective-permute-start.2
  40.6 0.3 shard_map.143
  40.9 0.6 collective-permute-done.2.refs_1_
  41.6 0.5 shard_map.144
  42.1 10.0 %all_to_all.43.near_ref.refs_0_ = bf16[8,8,1024]{2,1,0:T(8,128)(2,1)S(1)} all-to-all(bf16[8,8,1024]{2,1,0:T(8,128)(2,1)S(1)} %get-tuple-element.101), channel_id=1, replica_groups={{0,3,4,7,8,11,12,15},{1,2,5,6,9,10,13,14},{16,19,20,23,24,27,28,31},{17..., dimensions={0} | all-to-all | bytes 262144 | tf_op jit(solution)/shard_map/all_to_all | solution.py:463
  52.1 0.5 collective-permute-start.3
  52.5 0.3 shard_map.145
  52.9 0.6 collective-permute-done.3.refs_1_
  53.5 1.4 %shard_map.146 = (f32[8,1024]{1,0:T(8,128)S(1)}, bf16[4,32,256]{2,1,0:T(8,128)(2,1)S(1)}, bf16[4,32,128]{2,1,0:T(8,128)(2,1)S(1)}, bf16[4,32,256]{2,1,0:T(8,128)...) custom-call(bf16[8,8,1024]{2,1,0:T(8,128)(2,1)S(1)} %all_to_all.43.n, ...), custom_call_target="tpu_custom_call" | custom-call | tf_op jit(solution)/shard_map/pallas_call | solution.py:438
  54.9 3.5 %all-to-all-start.4 = ((bf16[16,8,128]{2,1,0:T(8,128)(2,1)}), bf16[16,8,128]{2,1,0:T(8,128)(2,1)S(1)}, u32[]{:S(2)}, u32[]{:S(2)}) async-start(bf16[16,8,128]{2,1,0:T(8,128)(2,1)} %get-tuple-element.107), calls=%async_computation.4 | async-start | bytes 65536 | tf_op jit(solution)/shard_map/all_to_all | solution.py:552
  58.4 0.3 collective-permute-start.4
  58.7 0.7 collective-permute-start.5
  59.4 0.3 shard_map.147
  59.7 0.0 collective-permute-done.5.refs_2_
  59.7 5.3 %all-to-all-done.4.refs_0_ = bf16[16,8,128]{2,1,0:T(8,128)(2,1)S(1)} async-done(((bf16[16,8,128]{2,1,0:T(8,128)(2,1)}), bf16[16,8,128]{2,1,0:T(8,128)(2,1)S(1)}, u32[]{:S(2)}, u32[]{:S(2)}) %all-to-all-start.4) | async-done | bytes 32800 | tf_op jit(solution)/shard_map/all_to_all | solution.py:552
  65.0 1.2 %shard_map.148 = (f32[8,1024]{1,0:T(8,128)S(1)}, bf16[4,32,256]{2,1,0:T(8,128)(2,1)S(1)}, bf16[4,32,256]{2,1,0:T(8,128)(2,1)S(1)}, f32[8,1024]{1,0:T(8,128)S(1)}...) custom-call(bf16[16,8,128]{2,1,0:T(8,128)(2,1)S(1)} %all-to-all-done.4.refs_0_, ...), custom_call_target="tpu_custom_call" | custom-call | tf_op jit(solution)/shard_map/pallas_call | solution.py:438
  66.2 4.6 %all-to-all-start.5 = ((bf16[16,8,128]{2,1,0:T(8,128)(2,1)}), bf16[16,8,128]{2,1,0:T(8,128)(2,1)S(1)}, u32[]{:S(2)}, u32[]{:S(2)}) async-start(bf16[16,8,128]{2,1,0:T(8,128)(2,1)} %get-tuple-element.117), calls=%async_computation.5 | async-start | bytes 65536 | tf_op jit(solution)/shard_map/all_to_all | solution.py:552
  70.8 0.4 collective-permute-start.6
  71.2 0.7 collective-permute-start.7
  71.8 0.3 shard_map.149
  72.1 0.0 collective-permute-done.7.refs_2_
  72.2 5.2 %all-to-all-done.5.refs_0_ = bf16[16,8,128]{2,1,0:T(8,128)(2,1)S(1)} async-done(((bf16[16,8,128]{2,1,0:T(8,128)(2,1)}), bf16[16,8,128]{2,1,0:T(8,128)(2,1)S(1)}, u32[]{:S(2)}, u32[]{:S(2)}) %all-to-all-start.5) | async-done | bytes 32800 | tf_op jit(solution)/shard_map/all_to_all | solution.py:552
  77.4 1.2 %shard_map.150 = (f32[8,1024]{1,0:T(8,128)S(1)}, bf16[4,32,256]{2,1,0:T(8,128)(2,1)S(1)}, bf16[4,32,256]{2,1,0:T(8,128)(2,1)S(1)}, f32[8,1024]{1,0:T(8,128)S(1)}...) custom-call(bf16[16,8,128]{2,1,0:T(8,128)(2,1)S(1)} %all-to-all-done.5.refs_0_, ...), custom_call_target="tpu_custom_call" | custom-call | tf_op jit(solution)/shard_map/pallas_call | solution.py:438
  78.6 4.6 %all-to-all-start.6 = ((bf16[16,8,128]{2,1,0:T(8,128)(2,1)}), bf16[16,8,128]{2,1,0:T(8,128)(2,1)S(1)}, u32[]{:S(2)}, u32[]{:S(2)}) async-start(bf16[16,8,128]{2,1,0:T(8,128)(2,1)} %get-tuple-element.126), calls=%async_computation.6 | async-start | bytes 65536 | tf_op jit(solution)/shard_map/all_to_all | solution.py:552
  83.2 0.4 collective-permute-start.8
  83.6 0.7 collective-permute-start.9
  84.2 0.3 shard_map.151
  84.6 5.2 %all-to-all-done.6.refs_0_ = bf16[16,8,128]{2,1,0:T(8,128)(2,1)S(1)} async-done(((bf16[16,8,128]{2,1,0:T(8,128)(2,1)}), bf16[16,8,128]{2,1,0:T(8,128)(2,1)S(1)}, u32[]{:S(2)}, u32[]{:S(2)}) %all-to-all-start.6) | async-done | bytes 32800 | tf_op jit(solution)/shard_map/all_to_all | solution.py:552
  89.8 1.2 %shard_map.152 = (f32[8,1024]{1,0:T(8,128)S(1)}, bf16[4,32,256]{2,1,0:T(8,128)(2,1)S(1)}, bf16[4,32,256]{2,1,0:T(8,128)(2,1)S(1)}, f32[8,1024]{1,0:T(8,128)S(1)}...) custom-call(bf16[16,8,128]{2,1,0:T(8,128)(2,1)S(1)} %all-to-all-done.6.refs_0_, ...), custom_call_target="tpu_custom_call" | custom-call | tf_op jit(solution)/shard_map/pallas_call | solution.py:438
  91.0 4.6 %all-to-all-start.7 = ((bf16[16,8,128]{2,1,0:T(8,128)(2,1)}), bf16[16,8,128]{2,1,0:T(8,128)(2,1)S(1)}, u32[]{:S(2)}, u32[]{:S(2)}) async-start(bf16[16,8,128]{2,1,0:T(8,128)(2,1)} %get-tuple-element.135), calls=%async_computation.7 | async-start | bytes 65536 | tf_op jit(solution)/shard_map/all_to_all | solution.py:552
  95.6 0.4 collective-permute-start.10
  96.0 0.7 collective-permute-start.11
  96.7 0.3 shard_map.153
  97.0 1.6 %shard_map.155 = (bf16[3,192,1024]{2,1,0:T(8,128)(2,1)}, bf16[64,1024]{1,0:T(8,128)(2,1)}, f32[8,1024]{1,0:T(8,128)}) custom-call(bf16[2,4,32,256]{3,2,1,0:T(8,128)(2,1)S(1)} %get-tuple-element.142.refs_0_, bf16[2,4,32,256]{3,2,1,0:T(8,128)(2,1)S(1)} %get-tuple-element.143.refs_1_, bf16[2,4,32,256]{3,2,1,0:T(8,128)(2,1)S(1)} %get-tuple-element.144.refs_2_, ...), custom_call_target="tpu_custom_call" | custom-call | tf_op jit(solution)/shard_map/pallas_call | solution.py:438
  98.5 3.7 %all-to-all-done.7.refs_0_ = bf16[16,8,128]{2,1,0:T(8,128)(2,1)S(1)} async-done(((bf16[16,8,128]{2,1,0:T(8,128)(2,1)}), bf16[16,8,128]{2,1,0:T(8,128)(2,1)S(1)}, u32[]{:S(2)}, u32[]{:S(2)}) %all-to-all-start.7) | async-done | bytes 32800 | tf_op jit(solution)/shard_map/all_to_all | solution.py:552
  102.2 0.9 shard_map.154
  (6 shorter events, 0.0 us)
Async XLA Ops:
  15.8 1.8 %collective-permute-start = (bf16[8,8,1152]{2,1,0:T(8,128)(2,1)S(1)}, bf16[8,8,1152]{2,1,0:T(8,128)(2,1)S(1)}, u32[]{:S(2)}, u32[]{:S(2)}) collective-permute-start(bf16[8,8,1152]{2,1,0:T(8,128)(2,1)S(1)} %all_to_all.40.near_ref.refs_0_), channel_id=1, source_target_pairs={{0,1},{1,0},{2,3},{3,2},{4,5},{5,4},{6,7},{7,6},{8,9},{9,8},{10,11... | collective-permute-start | bytes 442376 | tf_op jit(solution)/shard_map/ppermute | solution.py:466
  28.2 1.4 %collective-permute-start.1 = (bf16[8,8,1024]{2,1,0:T(8,128)(2,1)S(1)}, bf16[8,8,1024]{2,1,0:T(8,128)(2,1)S(1)}, u32[]{:S(2)}, u32[]{:S(2)}) collective-permute-start(bf16[8,8,1024]{2,1,0:T(8,128)(2,1)S(1)} %all_to_all.41.near_ref.refs_0_), channel_id=1, source_target_pairs={{0,1},{1,0},{2,3},{3,2},{4,5},{5,4},{6,7},{7,6},{8,9},{9,8},{10,11... | collective-permute-start | bytes 393224 | tf_op jit(solution)/shard_map/ppermute | solution.py:466
  40.1 1.4 %collective-permute-start.2 = (bf16[8,8,1024]{2,1,0:T(8,128)(2,1)S(1)}, bf16[8,8,1024]{2,1,0:T(8,128)(2,1)S(1)}, u32[]{:S(2)}, u32[]{:S(2)}) collective-permute-start(bf16[8,8,1024]{2,1,0:T(8,128)(2,1)S(1)} %all_to_all.42.near_ref.refs_0_), channel_id=1, source_target_pairs={{0,1},{1,0},{2,3},{3,2},{4,5},{5,4},{6,7},{7,6},{8,9},{9,8},{10,11... | collective-permute-start | bytes 393224 | tf_op jit(solution)/shard_map/ppermute | solution.py:466
  52.1 1.4 %collective-permute-start.3 = (bf16[8,8,1024]{2,1,0:T(8,128)(2,1)S(1)}, bf16[8,8,1024]{2,1,0:T(8,128)(2,1)S(1)}, u32[]{:S(2)}, u32[]{:S(2)}) collective-permute-start(bf16[8,8,1024]{2,1,0:T(8,128)(2,1)S(1)} %all_to_all.43.near_ref.refs_0_), channel_id=1, source_target_pairs={{0,1},{1,0},{2,3},{3,2},{4,5},{5,4},{6,7},{7,6},{8,9},{9,8},{10,11... | collective-permute-start | bytes 393224 | tf_op jit(solution)/shard_map/ppermute | solution.py:466
  54.9 10.1 %all-to-all-start.4 = ((bf16[16,8,128]{2,1,0:T(8,128)(2,1)}), bf16[16,8,128]{2,1,0:T(8,128)(2,1)S(1)}, u32[]{:S(2)}, u32[]{:S(2)}) async-start(bf16[16,8,128]{2,1,0:T(8,128)(2,1)} %get-tuple-element.107), calls=%async_computation.4 | async-start | bytes 65536 | tf_op jit(solution)/shard_map/all_to_all | solution.py:552
  58.4 1.3 %collective-permute-start.4 = (bf16[8,1024]{1,0:T(8,128)(2,1)S(1)}, bf16[8,1024]{1,0:T(8,128)(2,1)S(1)}, u32[]{:S(2)}, u32[]{:S(2)}) collective-permute-start(bf16[8,1024]{1,0:T(8,128)(2,1)S(1)} %get-tuple-element.108), channel_id=1, source_target_pairs={{0,1},{1,0},{2,3},{3,2},{4,5},{5,4},{6,7},{7,6},{8,9},{9,8},{10,11... | collective-permute-start | bytes 49160 | tf_op jit(solution)/shard_map/ppermute | solution.py:554
  58.7 1.0 collective-permute-start.5
  66.2 11.2 %all-to-all-start.5 = ((bf16[16,8,128]{2,1,0:T(8,128)(2,1)}), bf16[16,8,128]{2,1,0:T(8,128)(2,1)S(1)}, u32[]{:S(2)}, u32[]{:S(2)}) async-start(bf16[16,8,128]{2,1,0:T(8,128)(2,1)} %get-tuple-element.117), calls=%async_computation.5 | async-start | bytes 65536 | tf_op jit(solution)/shard_map/all_to_all | solution.py:552
  70.8 1.4 %collective-permute-start.6 = (bf16[8,1024]{1,0:T(8,128)(2,1)S(1)}, bf16[8,1024]{1,0:T(8,128)(2,1)S(1)}, u32[]{:S(2)}, u32[]{:S(2)}) collective-permute-start(bf16[8,1024]{1,0:T(8,128)(2,1)S(1)} %get-tuple-element.118), channel_id=1, source_target_pairs={{0,1},{1,0},{2,3},{3,2},{4,5},{5,4},{6,7},{7,6},{8,9},{9,8},{10,11... | collective-permute-start | bytes 49160 | tf_op jit(solution)/shard_map/ppermute | solution.py:554
  71.2 1.0 collective-permute-start.7
  78.6 11.2 %all-to-all-start.6 = ((bf16[16,8,128]{2,1,0:T(8,128)(2,1)}), bf16[16,8,128]{2,1,0:T(8,128)(2,1)S(1)}, u32[]{:S(2)}, u32[]{:S(2)}) async-start(bf16[16,8,128]{2,1,0:T(8,128)(2,1)} %get-tuple-element.126), calls=%async_computation.6 | async-start | bytes 65536 | tf_op jit(solution)/shard_map/all_to_all | solution.py:552
  83.2 1.4 %collective-permute-start.8 = (bf16[8,1024]{1,0:T(8,128)(2,1)S(1)}, bf16[8,1024]{1,0:T(8,128)(2,1)S(1)}, u32[]{:S(2)}, u32[]{:S(2)}) collective-permute-start(bf16[8,1024]{1,0:T(8,128)(2,1)S(1)} %get-tuple-element.127), channel_id=1, source_target_pairs={{0,1},{1,0},{2,3},{3,2},{4,5},{5,4},{6,7},{7,6},{8,9},{9,8},{10,11... | collective-permute-start | bytes 49160 | tf_op jit(solution)/shard_map/ppermute | solution.py:554
  83.6 1.0 collective-permute-start.9
  91.0 11.2 %all-to-all-start.7 = ((bf16[16,8,128]{2,1,0:T(8,128)(2,1)}), bf16[16,8,128]{2,1,0:T(8,128)(2,1)S(1)}, u32[]{:S(2)}, u32[]{:S(2)}) async-start(bf16[16,8,128]{2,1,0:T(8,128)(2,1)} %get-tuple-element.135), calls=%async_computation.7 | async-start | bytes 65536 | tf_op jit(solution)/shard_map/all_to_all | solution.py:552
  95.6 2.9 %collective-permute-start.10 = (bf16[8,1024]{1,0:T(8,128)(2,1)S(1)}, bf16[8,1024]{1,0:T(8,128)(2,1)S(1)}, u32[]{:S(2)}, u32[]{:S(2)}) collective-permute-start(bf16[8,1024]{1,0:T(8,128)(2,1)S(1)} %get-tuple-element.136), channel_id=1, source_target_pairs={{0,1},{1,0},{2,3},{3,2},{4,5},{5,4},{6,7},{7,6},{8,9},{9,8},{10,11... | collective-permute-start | bytes 49160 | tf_op jit(solution)/shard_map/ppermute | solution.py:554
  96.0 2.5 %collective-permute-start.11 = (bf16[8,1024]{1,0:T(8,128)(2,1)S(1)}, bf16[8,1024]{1,0:T(8,128)(2,1)S(1)}, u32[]{:S(2)}, u32[]{:S(2)}) collective-permute-start(bf16[8,1024]{1,0:T(8,128)(2,1)S(1)} %get-tuple-element.137), channel_id=1, source_target_pairs={{1,2},{3,4},{5,6},{7,8},{9,10},{11,12},{13,14},{2,1},{4,3},{6,5},{... | collective-permute-start | bytes 49160 | tf_op jit(solution)/shard_map/ppermute | solution.py:553

commit v4 on v3

--- a/solution.py
+++ b/solution.py
@@ -67,85 +67,92 @@
     return jnp.concatenate(pieces, axis=0)
 
 
-def folded(acc_ref, half):
-    totals = []
-    for block in range(acc_ref.shape[1]):
-        piece = half_pair(acc_ref[0, block], acc_ref[1, block], half)
-        totals.append(piece + swapped(piece))
-    return [half_pair(totals[b], totals[b + 1], half) for b in range(0, len(totals), 2)]
+def folded(acc_refs, half):
+    chunks = []
+    for block in range(0, acc_refs[0].shape[0], 2):
+        (low, low_next), (high, high_next) = (
+            (sum(ref[block] for ref in refs), sum(ref[block + 1] for ref in refs))
+            for refs in (acc_refs[0::2], acc_refs[1::2])
+        )
+        chunks.append(half_pair(low, high_next, half) + swapped(half_pair(low_next, high, half)))
+    return chunks
 
 
 def in_group(tile):
     return (tile ^ (tile >> 1)) & 1
 
 
-def source_code(tile, block, target, me):
-    far = in_group(tile) ^ in_group(me)
-    chunk = (tile >> 1) * 8 + (block >> 1)
-    return ((chunk * 2 + far) * 2 + (block & 1)) * 16 + target
-
-
-def source_of(code):
-    return code >> 9, (code >> 6) & 7, (code >> 5) & 1, (code >> 4) & 1, code & 15
-
-
-def slot_code(tile, rank, target):
-    return (tile * CAP + rank) * 16 + target
-
-
-def slot_of(code):
-    return code >> 5, (code >> 4) & 1, code & 15
+FIELDS = 7
+ACCS = 4
+
+
+def source_of(entry_ref, entry):
+    return tuple(entry_ref[FIELDS * entry + field] for field in range(5))
+
+
+def slot_of(entry_ref, entry):
+    return tuple(entry_ref[FIELDS * entry + field] for field in range(4, 7))
 
 
 def start_kernel(*refs):
     heads, rest = refs[:3], refs[3:]
-    count = (len(rest) - 8) // 2
-    held, (out_ref, me_ref, table_ref), kept = rest[:count], rest[count : count + 3], rest[count + 3 :]
-    rows_of, ask_ref, sems = kept[count : count + 3], kept[count + 3], kept[count + 4]
-    kept = kept[:count]
+    count = (len(rest) - 9) // 2
+    held, (out_ref, me_ref, entry_ref) = rest[:count], rest[count : count + 3]
+    kept = rest[count + 3 : 2 * count + 3]
+    tile_ref, block_ref, target_ref, used_ref, ask_ref, sems = rest[2 * count + 3 :]
+    lists = (tile_ref, block_ref, target_ref)
     copies = [
         pltpu.make_async_copy(source, target, sems.at[number])
-        for number, (source, target) in enumerate(zip((*heads, *held), (*rows_of, *kept)))
+        for number, (source, target) in enumerate(zip((*heads, *held), (*lists, *kept)))
     ]
     for copy in copies[3:6] + copies[:3] + copies[6:]:
         copy.start()
     chips = out_ref.shape[0]
     v_ref, spikes_ref = kept[:2]
     rows, neurons = v_ref.shape
-    entries = table_ref.shape[1]
+    entries = tile_ref.shape[1]
+    me = lax.axis_index("azim")
+    me_ref[0] = me
+    lane = lax.broadcasted_iota(jnp.int32, (rows, LANES), 1)
+    ask_ref[...] = jnp.zeros_like(ask_ref)
+    for tile in range(2 * chips):
+        used_ref[tile] = 0
+    for copy in copies[:3]:
+        copy.wait()
+    for entry in range(entries):
+        tile = tile_ref[0, entry]
+        block = block_ref[0, entry]
+        rank = used_ref[tile]
+        used_ref[tile] = rank + 1
+        fields = (
+            tile >> 1, (block >> 1) * LANES, in_group(tile) ^ in_group(me), block & 1,
+            target_ref[0, entry], tile, rank,
+        )
+        for number, field in enumerate(fields):
+            entry_ref[FIELDS * entry + number] = field
+        place = CAP * (tile & 1) + rank
+        ask_ref[tile >> 1] = jnp.where(lane == place, block.astype(f32), ask_ref[tile >> 1])
     for copy in copies[3:5]:
         copy.wait()
     activity = (spikes_ref[0].astype(f32) * surrogate(v_ref[...])).astype(bf16)
     for chip in range(chips):
         out_ref[chip, :, :neurons] = activity
-    me = lax.axis_index("azim")
-    me_ref[...] = jnp.full(me_ref.shape, me, jnp.int32)
-    ask_ref[...] = jnp.zeros_like(ask_ref)
-    across = lax.broadcasted_iota(jnp.int32, (entries, entries), 1)
-    down = lax.broadcasted_iota(jnp.int32, (entries, entries), 0)
-    lane = lax.broadcasted_iota(jnp.int32, (rows, LANES), 1)
-    for copy in copies[:3]:
-        copy.wait()
-    tiles, block, target = (ref[...] for ref in rows_of)
-    tiles_down = jnp.sum(
-        jnp.where(across == down, tiles.astype(f32), 0.0), axis=1, keepdims=True
-    ).astype(jnp.int32)
-    earlier = (tiles_down == tiles) & (down < across)
-    rank = jnp.sum(jnp.where(earlier, 1.0, 0.0), axis=0, keepdims=True).astype(jnp.int32)
-    table = jnp.concatenate(
-        [source_code(tiles, block, target, me), slot_code(tiles, rank, target)], axis=0
-    )
-    table_ref[...] = table
-    for entry in range(entries):
-        tile, slot, _ = slot_of(table[1, entry])
-        _, chunk, _, side, _ = source_of(table[0, entry])
-        asked = (2 * chunk + side).astype(f32)
-        place = CAP * (tile & 1) + slot
-        ask_ref[tile >> 1] = jnp.where(lane == place, asked, ask_ref[tile >> 1])
-    for chip in range(chips):
         out_ref[chip, :, neurons:] = ask_ref[chip].astype(bf16)
     for copy in copies[5:]:
         copy.wait()
+
+
+def wanted_kernel(near_ref, far_ref, me_ref, wanted_ref):
+    chips, _, width = near_ref.shape
+    me = me_ref[0]
+    for chip in range(chips):
+        near_core = in_group(me) ^ (chip & 1)
+        for ref, core in ((near_ref, near_core), (far_ref, 1 - near_core)):
+            asked = ref[chip, :, width - LANES :].astype(f32)
+            asked = jnp.where((me & 1) == 1, pltpu.roll(asked, LANES - CAP, 1), asked)
+            asked = asked.astype(jnp.int32)
+            for slot in range(CAP):
+                wanted_ref[CAP * (2 * chip + core) + slot] = asked[0, slot]
 
 
 def tile_drive(values, weights, source_ref, half):
@@ -179,7 +186,7 @@
     chips = near_ref.shape[0]
     neurons = w_ref.shape[2]
     half = lane_half(near_ref.shape[1])
-    me = me_ref[...][0, 0]
+    me = me_ref[0]
     chip = me >> 1
     core = me & 1
     own = near_ref[chip, :, :neurons].astype(f32)
@@ -194,23 +201,23 @@
 
 
 def forward_part(
-    near_ref, far_ref, partial_ref, me_ref, table_ref, w_ref, w_long_ref, source_ref, fetched_ref,
-    acc_ref,
+    near_ref, far_ref, partial_ref, me_ref, entry_ref, w_ref, w_long_ref, source_ref, fetched_ref,
+    acc_refs,
 ):
     rows = near_ref.shape[1]
     neurons = w_ref.shape[2]
-    entries = table_ref.shape[1]
+    entries = fetched_ref.shape[0] * GROUP
     half = lane_half(rows)
-    table = table_ref[...]
-    me = me_ref[...][0, 0]
-    acc_ref[...] = jnp.zeros_like(acc_ref)
+    me = me_ref[0]
+    for ref in acc_refs:
+        ref[...] = jnp.zeros_like(ref)
     for group in range(entries // GROUP):
         columns = slice(group * WIDE, (group + 1) * WIDE)
         pieces, targets = [], []
         for entry in range(GROUP * group, GROUP * (group + 1)):
-            place, chunk, far, side, target = source_of(table[0, entry])
+            place, lane, far, side, target = source_of(entry_ref, entry)
             targets.append(target)
-            lanes = pl.ds(pl.multiple_of(chunk * LANES, LANES), LANES)
+            lanes = pl.ds(pl.multiple_of(lane, LANES), LANES)
             piece = jnp.where(far == 0, near_ref[place, :, lanes], far_ref[place, :, lanes])
             pieces.append(half_only(piece.astype(f32), half, side))
         fetched = stacked(pieces).astype(bf16)
@@ -219,27 +226,29 @@
         total = product(fetched, stacked([weights, weights]))
         for at, target in enumerate(targets):
             lanes = slice(at // 2 * LANES, (at // 2 + 1) * LANES)
-            acc_ref[at % 2, target] += total[at * rows : (at + 1) * rows, lanes]
+            acc_refs[(at + 2 * group) % len(acc_refs)][target] += total[
+                at * rows : (at + 1) * rows, lanes
+            ]
     mate = far_ref[me >> 1, :, :neurons].astype(f32)
     drive = tile_drive(
         mate, lambda columns: w_ref[2 - 2 * (me & 1), :, columns], source_ref, half
     )
-    extra = folded(acc_ref, half)
+    extra = folded(acc_refs, half)
     return partial_ref[...] + jnp.concatenate([a + b for a, b in zip(drive, extra)], axis=1)
 
 
 def forward_kernel(moment, *refs):
     (
-        near_ref, far_ref, partial_ref, me_ref, table_ref, w_ref, w_long_ref, v_ref, g_ref,
+        near_ref, far_ref, partial_ref, me_ref, entry_ref, w_ref, w_long_ref, v_ref, g_ref,
         decay_ref, spikes_ref,
     ) = refs[:11]
     v_out, g_out, gate_out, source_ref, fetched_ref, act_ref = refs[11:17]
-    acc_ref = refs[-1]
+    acc_refs = refs[17:]
     rows, neurons = v_ref.shape
     chips = act_ref.shape[0]
     drive = forward_part(
-        near_ref, far_ref, partial_ref, me_ref, table_ref, w_ref, w_long_ref, source_ref,
-        fetched_ref, acc_ref,
+        near_ref, far_ref, partial_ref, me_ref, entry_ref, w_ref, w_long_ref, source_ref,
+        fetched_ref, acc_refs,
     )
     voltage = v_ref[...]
     conduct = decay_ref[...] * g_ref[...] + jax.nn.softplus(drive)
@@ -252,18 +261,6 @@
     activity = (spikes_ref[moment + 1].astype(f32) * surrogate(voltage)).astype(bf16)
     for chip in range(chips):
         act_ref[chip] = activity
-    if moment == 0:
-        wanted_ref = refs[17]
-        core = me_ref[...][0, 0] & 1
-        mine = in_group(me_ref[...][0, 0])
-        for chip in range(chips):
-            near_core = mine ^ (chip & 1)
-            for ref, place in ((near_ref, near_core), (far_ref, 1 - near_core)):
-                place = 2 * chip + place
-                asked = ref[chip, :, neurons:].astype(f32)
-                asked = jnp.where(core == 1, pltpu.roll(asked, LANES - CAP, 1), asked)
-                asked = asked + 16.0 * pltpu.roll(asked, LANES - 1, 1)
-                wanted_ref[place] = asked.astype(jnp.int32)
 
 
 def toward_tile(side, adj_ref, w_ref):
@@ -292,16 +289,15 @@
 
 
 def backward_part(
-    adj_cond, adj_volt, voltage, gate, decay, me_ref, table_ref, w_ref, w_long_ref,
-    adj_ref, gathered_ref, cond_out, pair_out, cross_out, placed_out, acc_ref, slot_ref,
+    adj_cond, adj_volt, voltage, gate, decay, me_ref, entry_ref, w_ref, w_long_ref,
+    adj_ref, gathered_ref, cond_out, pair_out, cross_out, placed_out, block_ref, slot_ref,
     stage_ref, sem,
 ):
     rows, neurons = voltage.shape
     blocks = neurons // BLK
-    entries = table_ref.shape[1]
+    entries = gathered_ref.shape[0] * GROUP
     half = lane_half(rows)
-    table = table_ref[...]
-    core = me_ref[...][0, 0] & 1
+    core = me_ref[0] & 1
     total_g = adj_cond + adj_volt * 0.1 * (3.0 - voltage)
     adj_drive = (total_g * gate).astype(bf16).astype(f32)
     cond_out[...] = decay * total_g
@@ -309,16 +305,16 @@
     zero = jnp.zeros((rows, LANES), f32)
     for number, piece in enumerate(chunks):
         turned = swapped(piece)
-        acc_ref[0, 2 * number] = half_pair(piece, turned, half)
-        acc_ref[0, 2 * number + 1] = half_pair(turned, piece, half)
+        block_ref[2 * number] = half_pair(piece, turned, half)
+        block_ref[2 * number + 1] = half_pair(turned, piece, half)
     slot_ref[...] = jnp.zeros_like(slot_ref)
     for group in range(entries // GROUP):
         columns = slice(group * WIDE, (group + 1) * WIDE)
         left, right, slots = [], [], []
         for at in range(GROUP):
-            tile, rank, target = slot_of(table[1, GROUP * group + at])
+            target, tile, rank = slot_of(entry_ref, GROUP * group + at)
             slots.append((rank, tile))
-            piece = half_only(acc_ref[0, target], half, at % 2)
+            piece = half_only(block_ref[target], half, at % 2)
             left.append(piece if at < 2 else zero)
             right.append(zero if at < 2 else piece)
         gathered = jnp.concatenate([stacked(left), stacked(right)], axis=1).astype(bf16)
@@ -355,63 +351,58 @@
 
 def turn_kernel(*refs):
     (
-        near_ref, far_ref, partial_ref, me_ref, table_ref, w_ref, w_long_ref, v_ref, g_ref,
+        near_ref, far_ref, partial_ref, me_ref, entry_ref, w_ref, w_long_ref, v_ref, g_ref,
         decay_ref, adj_v_ref, adj_g_ref,
     ) = refs[:12]
     g_out, source_ref, fetched_ref = refs[12:15]
-    acc_ref = refs[21]
+    acc_refs = refs[25:]
     drive = forward_part(
-        near_ref, far_ref, partial_ref, me_ref, table_ref, w_ref, w_long_ref, source_ref,
-        fetched_ref, acc_ref,
+        near_ref, far_ref, partial_ref, me_ref, entry_ref, w_ref, w_long_ref, source_ref,
+        fetched_ref, acc_refs,
     )
     decay = decay_ref[...]
     g_out[...] = decay * g_ref[...] + jax.nn.softplus(drive)
     backward_part(
         adj_g_ref[...], adj_v_ref[...], v_ref[...], jax.nn.sigmoid(drive), decay,
-        me_ref, table_ref, w_ref, w_long_ref, *refs[15:],
-    )
-
-
-def receive_part(placed_ref, pair_ref, cross_ref, base_ref, gain_ref, wanted_ref, acc_ref):
+        me_ref, entry_ref, w_ref, w_long_ref, *refs[15:25],
+    )
+
+
+def receive_part(placed_ref, pair_ref, cross_ref, base_ref, gain_ref, wanted_ref, acc_refs):
     half = lane_half(base_ref.shape[0])
-    acc_ref[...] = jnp.zeros_like(acc_ref)
+    for ref in acc_refs:
+        ref[...] = jnp.zeros_like(ref)
     tiles = placed_ref.shape[0]
-    for first in range(0, tiles, 3):
-        count = min(3, tiles - first)
-        codes = wanted_ref[first, 0:1, :]
-        for at in range(1, count):
-            codes = codes + wanted_ref[first + at, 0:1, :] * 256**at
-        code = codes[0, 0]
-        for at in range(count):
-            arrived = placed_ref[first + at].astype(f32)
-            for slot in range(CAP):
-                acc_ref[slot, (code >> (8 * at + 4 * slot)) & 15] += arrived
+    for tile in range(tiles):
+        arrived = placed_ref[tile].astype(f32)
+        for slot in range(CAP):
+            number = (slot + CAP * tile) % len(acc_refs)
+            acc_refs[number][wanted_ref[CAP * tile + slot]] += arrived
     rest = pair_ref[...].astype(f32) + cross_ref[...].astype(f32)
-    rest = rest + jnp.concatenate(folded(acc_ref, half), axis=1)
+    rest = rest + jnp.concatenate(folded(acc_refs, half), axis=1)
     return base_ref[...] + rest * gain_ref[...]
 
 
 def backward_kernel(*refs):
-    adj_g_ref, v_ref, gate_ref, decay_ref, me_ref, table_ref, w_ref, w_long_ref = refs[6:14]
+    adj_g_ref, v_ref, gate_ref, decay_ref, me_ref, entry_ref, w_ref, w_long_ref = refs[6:14]
     adj_v_out = refs[14]
-    acc_ref = refs[21]
-    adj_volt = receive_part(*refs[:6], acc_ref)
+    adj_volt = receive_part(*refs[:6], refs[25:])
     adj_v_out[...] = adj_volt
     backward_part(
         adj_g_ref[...], adj_volt, v_ref[...], gate_ref[...], decay_ref[...],
-        me_ref, table_ref, w_ref, w_long_ref, *refs[15:],
+        me_ref, entry_ref, w_ref, w_long_ref, *refs[15:25],
     )
 
 
 def last_kernel(*refs):
-    refs[6][...] = receive_part(*refs[:6], refs[7])
+    refs[6][...] = receive_part(*refs[:6], refs[7:])
 
 
 def grad_kernel(*refs):
     near, far, fetched, adjs, gathered = (refs[k * STEPS : (k + 1) * STEPS] for k in range(5))
     me_ref, cond_ref, local_ref, long_ref, cond_out = refs[5 * STEPS :]
     cond_out[...] = cond_ref[...]
-    core = me_ref[...][0, 0] & 1
+    core = me_ref[0] & 1
     for group in range(adjs[0].shape[0]):
         columns = slice(group * WIDE, (group + 1) * WIDE)
         adj = stacked([ref[group] for ref in adjs])
@@ -431,15 +422,25 @@
 
 
 def call(kernel, outs, args, scratch=(), hbm_outs=(), hbm_args=False):
-    vmem = pl.BlockSpec(memory_space=pltpu.VMEM)
-    hbm = pl.BlockSpec(memory_space=pltpu.HBM)
+    def spec(space):
+        return pl.BlockSpec(memory_space=space)
+
+    vmem, hbm, smem = (spec(space) for space in (pltpu.VMEM, pltpu.HBM, pltpu.SMEM))
     if hbm_args:
         args = [pltpu.with_memory_space_constraint(array, pltpu.HBM) for array in args]
+    in_specs = [smem if array.ndim == 1 else hbm if hbm_args else vmem for array in args]
+    out_specs = [
+        smem if len(shape) == 1 else hbm if number in hbm_outs else vmem
+        for number, (shape, _) in enumerate(outs)
+    ]
     return pl.pallas_call(
         kernel,
-        out_shape=[jax.ShapeDtypeStruct(shape, dtype) for shape, dtype in outs],
-        in_specs=[hbm if hbm_args else vmem] * len(args),
-        out_specs=[hbm if k in hbm_outs else vmem for k in range(len(outs))],
+        out_shape=[
+            pltpu.SMEM(shape, dtype) if len(shape) == 1 else jax.ShapeDtypeStruct(shape, dtype)
+            for shape, dtype in outs
+        ],
+        in_specs=in_specs,
+        out_specs=out_specs,
         scratch_shapes=scratch,
         compiler_params=pltpu.CompilerParams(vmem_limit_bytes=24 * 2**20),
     )(*args)
@@ -469,12 +470,14 @@
     source = ((blocks // GROUP, GROUP * rows, WIDE), bf16)
     sources = ((2, *source[0]), bf16)
     fetched = ((entries // GROUP, GROUP * rows, LANES), bf16)
-    block_sum = pltpu.VMEM((CAP, blocks, rows, LANES), f32)
+    block_row = pltpu.VMEM((blocks, rows, LANES), f32)
+    sums = [block_row] * ACCS
     back_scratch = [
-        block_sum,
+        block_row,
         pltpu.VMEM((CAP, tiles, rows, LANES), f32),
         pltpu.VMEM((tiles, rows, LANES), bf16),
         pltpu.SemaphoreType.DMA,
+        *sums,
     ]
     back_outs = [
         ((blocks // GROUP, GROUP * rows, WIDE), bf16),
@@ -488,17 +491,18 @@
         v_init, spikes, w_local.reshape(3, SIDE, neurons), w_long, g_init, decay, adj_v_end,
         adj_g_end,
     )
-    entry_row = pltpu.VMEM((1, entries), jnp.int32)
-    out, me, table, v_start, spikes, w_all, w_long, g_start, decay, adj_volt, adj_cond = call(
+    entry_row = pltpu.SMEM((1, entries), jnp.int32)
+    out, me, entry_list, v_start, spikes, w_all, w_long, g_start, decay, adj_volt, adj_cond = call(
         start_kernel,
         [
-            ((chips, rows, neurons + LANES), bf16), ((8, LANES), jnp.int32),
-            ((2, entries), jnp.int32),
+            ((chips, rows, neurons + LANES), bf16), ((1,), jnp.int32),
+            ((FIELDS * entries,), jnp.int32),
         ]
         + [(array.shape, array.dtype) for array in held],
         (lr_src_tile.T, lr_src_block.T, lr_tgt_block.T, *held),
         [
-            entry_row, entry_row, entry_row, pltpu.VMEM((chips, rows, LANES), f32),
+            entry_row, entry_row, entry_row, pltpu.SMEM((tiles,), jnp.int32),
+            pltpu.VMEM((chips, rows, LANES), f32),
             pltpu.SemaphoreType.DMA((3 + len(held),)),
         ],
         hbm_args=True,
@@ -509,20 +513,18 @@
         partial, near_t = call(near_kernel, [state, sources], (near, me, w_all))
         nears.append(near_t)
         outs = [state, state, state, source, fetched, ((chips, rows, neurons), bf16)]
-        if moment == 0:
-            outs.append(((tiles, rows, LANES), jnp.int32))
         results = call(
             functools.partial(forward_kernel, moment),
             outs,
             (
-                near, far, partial, me, table, w_all, w_long, voltages[-1], conducts[-1], decay,
+                near, far, partial, me, entry_list, w_all, w_long, voltages[-1], conducts[-1], decay,
                 spikes,
             ),
-            [block_sum],
+            sums,
         )
         if moment == 0:
-            wanted = results[6]
-        voltage, conduct, gate, far_t, fetched_t, out = results[:6]
+            (wanted,) = call(wanted_kernel, [((CAP * tiles,), jnp.int32)], (near, far, me))
+        voltage, conduct, gate, far_t, fetched_t, out = results
         voltages.append(voltage)
         conducts.append(conduct)
         gates.append(gate)
@@ -535,7 +537,7 @@
         turn_kernel,
         [state, source, fetched] + back_outs,
         (
-            near, far, partial, me, table, w_all, w_long, voltages[-1], conducts[-1], decay,
+            near, far, partial, me, entry_list, w_all, w_long, voltages[-1], conducts[-1], decay,
             adj_volt, adj_cond,
         ),
         back_scratch,
@@ -564,7 +566,7 @@
                 [state] + back_outs,
                 received
                 + (
-                    adj_cond, voltages[moment - 1], gates[moment - 1], decay, me, table, w_all,
+                    adj_cond, voltages[moment - 1], gates[moment - 1], decay, me, entry_list, w_all,
                     w_long,
                 ),
                 back_scratch,
@@ -575,7 +577,7 @@
         [((3, SIDE, neurons), bf16), ((BLK, entries * BLK), bf16), state],
         (*nears, *fars, *fetches, *adjs, *gathers, me, adj_cond),
     )
-    (adj_volt,) = call(last_kernel, [state], received, [block_sum])
+    (adj_volt,) = call(last_kernel, [state], received, sums)
     return (adj_volt, adj_cond, grad_local.reshape(9, BLK, neurons), grad_long)
 
 

time: 104 us -> 103 us (level)
    pallas_call x18 -> x19, Pallas kernels: 12.8 us -> 11.9 us  [call(): pl.pallas_call(kernel, out_shape=[pltpu.SMEM(shape, dtype) if len(shape)...]
where the time goes in v4:
time: 103 us; the launch traced here: 102 us
  blocking collectives  43.8 us (43%)
  starting transfers between devices  23.6 us (23%)
  waiting for transfers between devices  22 us (21%)
  Pallas kernels  11.9 us (12%)
    all_to_all x4, blocking collectives, spread(): lax.all_to_all(values, 'azim', split_axis=0, concat_axis=0, tiled=True, a...  43.8 us
    all_to_all x4, waiting for transfers between devices, local(): lax.all_to_all(placed, 'azim', split_axis=0, concat_axis=0, tiled=True)  19.3 us
    all_to_all x4, starting transfers between devices, local(): lax.all_to_all(placed, 'azim', split_axis=0, concat_axis=0, tiled=True)  17.3 us
    pallas_call x19, Pallas kernels, call(): pl.pallas_call(kernel, out_shape=[pltpu.SMEM(shape, dtype) if len(shape)...  11.9 us
    ppermute x4, waiting for transfers between devices, spread(): return (near, lax.ppermute(near, 'azim', pair))  2.73 us
    ppermute x4, starting transfers between devices, local(): from_cross = lax.ppermute(to_cross, 'azim', cross)  2.6 us
    ppermute x4, starting transfers between devices, spread(): return (near, lax.ppermute(near, 'azim', pair))  2.13 us
  transfers between devices with their start and end apart: 16, of which 8 were waited for; matrix products, arithmetic and copies ran while one was open for 0% of the time, Pallas kernels for 4%

profile of v4, /device:TPU:0, one launch (start us, length us, event | category | flops | bytes accessed | tf_op | source)
XLA Modules:
  0.0 102.1 jit_solution(12038425372655524366)
XLA Ops:
  0.6 1.5 %shard_map.138 = (bf16[8,8,1152]{2,1,0:T(8,128)(2,1)S(1)}, s32[1]{0:T(128)S(4)}, s32[112]{0:T(128)S(4)}, f32[8,1024]{1,0:T(8,128)S(1)}, s32[4,8,1024]{2,1,0:T(8,...) custom-call(s32[1,16]{1,0:T(1,128)} %bitcast.6, ...), custom_call_target="tpu_custom_call" | custom-call | tf_op jit(solution)/shard_map/pallas_call | solution.py:436
  2.1 13.7 %all_to_all.40.near_ref.refs_0_ = bf16[8,8,1152]{2,1,0:T(8,128)(2,1)S(1)} all-to-all(bf16[8,8,1152]{2,1,0:T(8,128)(2,1)S(1)} %get-tuple-element.82), channel_id=1, replica_groups={{0,3,4,7,8,11,12,15},{1,2,5,6,9,10,13,14},{16,19,20,23,24,27,28,31},{17..., dimensions={0} | all-to-all | bytes 294912 | tf_op jit(solution)/shard_map/all_to_all | solution.py:464
  15.8 0.7 collective-permute-start
  16.5 0.3 shard_map.139
  16.8 0.7 collective-permute-done.refs_1_.far_ref
  17.5 0.3 shard_map.140
  17.9 10.1 %all_to_all.41.near_ref.refs_0_ = bf16[8,8,1024]{2,1,0:T(8,128)(2,1)S(1)} all-to-all(bf16[8,8,1024]{2,1,0:T(8,128)(2,1)S(1)} %get-tuple-element.92), channel_id=1, replica_groups={{0,3,4,7,8,11,12,15},{1,2,5,6,9,10,13,14},{16,19,20,23,24,27,28,31},{17..., dimensions={0} | all-to-all | bytes 262144 | tf_op jit(solution)/shard_map/all_to_all | solution.py:464
  28.0 0.5 collective-permute-start.1
  28.4 0.3 shard_map.141
  28.8 0.7 collective-permute-done.1.refs_1_
  29.4 0.3 shard_map.142
  29.8 10.0 %all_to_all.42.near_ref.refs_0_ = bf16[8,8,1024]{2,1,0:T(8,128)(2,1)S(1)} all-to-all(bf16[8,8,1024]{2,1,0:T(8,128)(2,1)S(1)} %get-tuple-element.96), channel_id=1, replica_groups={{0,3,4,7,8,11,12,15},{1,2,5,6,9,10,13,14},{16,19,20,23,24,27,28,31},{17..., dimensions={0} | all-to-all | bytes 262144 | tf_op jit(solution)/shard_map/all_to_all | solution.py:464
  39.8 0.5 collective-permute-start.2
  40.2 0.3 shard_map.143
  40.5 0.7 collective-permute-done.2.refs_1_
  41.2 0.3 shard_map.144
  41.5 10.0 %all_to_all.43.near_ref.refs_0_ = bf16[8,8,1024]{2,1,0:T(8,128)(2,1)S(1)} all-to-all(bf16[8,8,1024]{2,1,0:T(8,128)(2,1)S(1)} %get-tuple-element.100), channel_id=1, replica_groups={{0,3,4,7,8,11,12,15},{1,2,5,6,9,10,13,14},{16,19,20,23,24,27,28,31},{17..., dimensions={0} | all-to-all | bytes 262144 | tf_op jit(solution)/shard_map/all_to_all | solution.py:464
  51.5 0.5 collective-permute-start.3
  52.0 0.3 shard_map.145
  52.3 0.7 collective-permute-done.3.refs_1_
  53.0 1.2 %shard_map.146 = (f32[8,1024]{1,0:T(8,128)S(1)}, bf16[4,32,256]{2,1,0:T(8,128)(2,1)S(1)}, bf16[4,32,128]{2,1,0:T(8,128)(2,1)S(1)}, bf16[4,32,256]{2,1,0:T(8,128)...) custom-call(bf16[8,8,1024]{2,1,0:T(8,128)(2,1)S(1)} %all_to_all.43.n, ...), custom_call_target="tpu_custom_call" | custom-call | tf_op jit(solution)/shard_map/pallas_call | solution.py:436
  54.2 3.5 %all-to-all-start.4 = ((bf16[16,8,128]{2,1,0:T(8,128)(2,1)}), bf16[16,8,128]{2,1,0:T(8,128)(2,1)S(1)}, u32[]{:S(2)}, u32[]{:S(2)}) async-start(bf16[16,8,128]{2,1,0:T(8,128)(2,1)} %get-tuple-element.106), calls=%async_computation.4 | async-start | bytes 65536 | tf_op jit(solution)/shard_map/all_to_all | solution.py:554
  57.7 0.3 collective-permute-start.4
  58.1 0.7 collective-permute-start.5
  58.7 0.2 shard_map.148.refs_5_
  58.9 0.3 shard_map.147
  59.2 0.0 collective-permute-done.4.refs_1_
  59.3 5.1 %all-to-all-done.4.refs_0_ = bf16[16,8,128]{2,1,0:T(8,128)(2,1)S(1)} async-done(((bf16[16,8,128]{2,1,0:T(8,128)(2,1)}), bf16[16,8,128]{2,1,0:T(8,128)(2,1)S(1)}, u32[]{:S(2)}, u32[]{:S(2)}) %all-to-all-start.4) | async-done | bytes 32800 | tf_op jit(solution)/shard_map/all_to_all | solution.py:554
  64.3 1.1 %shard_map.149 = (f32[8,1024]{1,0:T(8,128)S(1)}, bf16[4,32,256]{2,1,0:T(8,128)(2,1)S(1)}, bf16[4,32,256]{2,1,0:T(8,128)(2,1)S(1)}, f32[8,1024]{1,0:T(8,128)S(1)}...) custom-call(bf16[16,8,128]{2,1,0:T(8,128)(2,1)S(1)} %all-to-all-done.4.refs_0_, ...), custom_call_target="tpu_custom_call" | custom-call | tf_op jit(solution)/shard_map/pallas_call | solution.py:436
  65.4 4.6 %all-to-all-start.5 = ((bf16[16,8,128]{2,1,0:T(8,128)(2,1)}), bf16[16,8,128]{2,1,0:T(8,128)(2,1)S(1)}, u32[]{:S(2)}, u32[]{:S(2)}) async-start(bf16[16,8,128]{2,1,0:T(8,128)(2,1)} %get-tuple-element.115), calls=%async_computation.5 | async-start | bytes 65536 | tf_op jit(solution)/shard_map/all_to_all | solution.py:554
  70.0 0.4 collective-permute-start.6
  70.4 0.7 collective-permute-start.7
  71.1 0.3 shard_map.150
  71.4 5.2 %all-to-all-done.5.refs_0_ = bf16[16,8,128]{2,1,0:T(8,128)(2,1)S(1)} async-done(((bf16[16,8,128]{2,1,0:T(8,128)(2,1)}), bf16[16,8,128]{2,1,0:T(8,128)(2,1)S(1)}, u32[]{:S(2)}, u32[]{:S(2)}) %all-to-all-start.5) | async-done | bytes 32800 | tf_op jit(solution)/shard_map/all_to_all | solution.py:554
  76.7 1.1 %shard_map.151 = (f32[8,1024]{1,0:T(8,128)S(1)}, bf16[4,32,256]{2,1,0:T(8,128)(2,1)S(1)}, bf16[4,32,256]{2,1,0:T(8,128)(2,1)S(1)}, f32[8,1024]{1,0:T(8,128)S(1)}...) custom-call(bf16[16,8,128]{2,1,0:T(8,128)(2,1)S(1)} %all-to-all-done.5.refs_0_, ...), custom_call_target="tpu_custom_call" | custom-call | tf_op jit(solution)/shard_map/pallas_call | solution.py:436
  77.7 4.6 %all-to-all-start.6 = ((bf16[16,8,128]{2,1,0:T(8,128)(2,1)}), bf16[16,8,128]{2,1,0:T(8,128)(2,1)S(1)}, u32[]{:S(2)}, u32[]{:S(2)}) async-start(bf16[16,8,128]{2,1,0:T(8,128)(2,1)} %get-tuple-element.124), calls=%async_computation.6 | async-start | bytes 65536 | tf_op jit(solution)/shard_map/all_to_all | solution.py:554
  82.3 0.4 collective-permute-start.8
  82.8 0.7 collective-permute-start.9
  83.4 0.3 shard_map.152
  83.7 5.2 %all-to-all-done.6.refs_0_ = bf16[16,8,128]{2,1,0:T(8,128)(2,1)S(1)} async-done(((bf16[16,8,128]{2,1,0:T(8,128)(2,1)}), bf16[16,8,128]{2,1,0:T(8,128)(2,1)S(1)}, u32[]{:S(2)}, u32[]{:S(2)}) %all-to-all-start.6) | async-done | bytes 32800 | tf_op jit(solution)/shard_map/all_to_all | solution.py:554
  89.0 1.1 %shard_map.153 = (f32[8,1024]{1,0:T(8,128)S(1)}, bf16[4,32,256]{2,1,0:T(8,128)(2,1)S(1)}, bf16[4,32,256]{2,1,0:T(8,128)(2,1)S(1)}, f32[8,1024]{1,0:T(8,128)S(1)}...) custom-call(bf16[16,8,128]{2,1,0:T(8,128)(2,1)S(1)} %all-to-all-done.6.refs_0_, ...), custom_call_target="tpu_custom_call" | custom-call | tf_op jit(solution)/shard_map/pallas_call | solution.py:436
  90.1 4.6 %all-to-all-start.7 = ((bf16[16,8,128]{2,1,0:T(8,128)(2,1)}), bf16[16,8,128]{2,1,0:T(8,128)(2,1)S(1)}, u32[]{:S(2)}, u32[]{:S(2)}) async-start(bf16[16,8,128]{2,1,0:T(8,128)(2,1)} %get-tuple-element.133), calls=%async_computation.7 | async-start | bytes 65536 | tf_op jit(solution)/shard_map/all_to_all | solution.py:554
  94.7 0.4 collective-permute-start.10
  95.1 0.7 collective-permute-start.11
  95.7 0.3 shard_map.154
  96.0 1.6 %shard_map.156 = (bf16[3,192,1024]{2,1,0:T(8,128)(2,1)}, bf16[64,1024]{1,0:T(8,128)(2,1)}, f32[8,1024]{1,0:T(8,128)}) custom-call(bf16[2,4,32,256]{3,2,1,0:T(8,128)(2,1)S(1)} %get-tuple-element.140.refs_0_, bf16[2,4,32,256]{3,2,1,0:T(8,128)(2,1)S(1)} %get-tuple-element.141.refs_1_, bf16[2,4,32,256]{3,2,1,0:T(8,128)(2,1)S(1)} %get-tuple-element.142.refs_2_, ...), custom_call_target="tpu_custom_call" | custom-call | tf_op jit(solution)/shard_map/pallas_call | solution.py:436
  97.6 3.7 %all-to-all-done.7.refs_0_ = bf16[16,8,128]{2,1,0:T(8,128)(2,1)S(1)} async-done(((bf16[16,8,128]{2,1,0:T(8,128)(2,1)}), bf16[16,8,128]{2,1,0:T(8,128)(2,1)S(1)}, u32[]{:S(2)}, u32[]{:S(2)}) %all-to-all-start.7) | async-done | bytes 32800 | tf_op jit(solution)/shard_map/all_to_all | solution.py:554
  101.3 0.8 shard_map.155
  (7 shorter events, 0.0 us)
Async XLA Ops:
  15.8 1.7 %collective-permute-start = (bf16[8,8,1152]{2,1,0:T(8,128)(2,1)S(1)}, bf16[8,8,1152]{2,1,0:T(8,128)(2,1)S(1)}, u32[]{:S(2)}, u32[]{:S(2)}) collective-permute-start(bf16[8,8,1152]{2,1,0:T(8,128)(2,1)S(1)} %all_to_all.40.near_ref.refs_0_), channel_id=1, source_target_pairs={{0,1},{1,0},{2,3},{3,2},{4,5},{5,4},{6,7},{7,6},{8,9},{9,8},{10,11... | collective-permute-start | bytes 442376 | tf_op jit(solution)/shard_map/ppermute | solution.py:467
  28.0 1.4 %collective-permute-start.1 = (bf16[8,8,1024]{2,1,0:T(8,128)(2,1)S(1)}, bf16[8,8,1024]{2,1,0:T(8,128)(2,1)S(1)}, u32[]{:S(2)}, u32[]{:S(2)}) collective-permute-start(bf16[8,8,1024]{2,1,0:T(8,128)(2,1)S(1)} %all_to_all.41.near_ref.refs_0_), channel_id=1, source_target_pairs={{0,1},{1,0},{2,3},{3,2},{4,5},{5,4},{6,7},{7,6},{8,9},{9,8},{10,11... | collective-permute-start | bytes 393224 | tf_op jit(solution)/shard_map/ppermute | solution.py:467
  39.8 1.4 %collective-permute-start.2 = (bf16[8,8,1024]{2,1,0:T(8,128)(2,1)S(1)}, bf16[8,8,1024]{2,1,0:T(8,128)(2,1)S(1)}, u32[]{:S(2)}, u32[]{:S(2)}) collective-permute-start(bf16[8,8,1024]{2,1,0:T(8,128)(2,1)S(1)} %all_to_all.42.near_ref.refs_0_), channel_id=1, source_target_pairs={{0,1},{1,0},{2,3},{3,2},{4,5},{5,4},{6,7},{7,6},{8,9},{9,8},{10,11... | collective-permute-start | bytes 393224 | tf_op jit(solution)/shard_map/ppermute | solution.py:467
  51.5 1.4 %collective-permute-start.3 = (bf16[8,8,1024]{2,1,0:T(8,128)(2,1)S(1)}, bf16[8,8,1024]{2,1,0:T(8,128)(2,1)S(1)}, u32[]{:S(2)}, u32[]{:S(2)}) collective-permute-start(bf16[8,8,1024]{2,1,0:T(8,128)(2,1)S(1)} %all_to_all.43.near_ref.refs_0_), channel_id=1, source_target_pairs={{0,1},{1,0},{2,3},{3,2},{4,5},{5,4},{6,7},{7,6},{8,9},{9,8},{10,11... | collective-permute-start | bytes 393224 | tf_op jit(solution)/shard_map/ppermute | solution.py:467
  54.2 10.1 %all-to-all-start.4 = ((bf16[16,8,128]{2,1,0:T(8,128)(2,1)}), bf16[16,8,128]{2,1,0:T(8,128)(2,1)S(1)}, u32[]{:S(2)}, u32[]{:S(2)}) async-start(bf16[16,8,128]{2,1,0:T(8,128)(2,1)} %get-tuple-element.106), calls=%async_computation.4 | async-start | bytes 65536 | tf_op jit(solution)/shard_map/all_to_all | solution.py:554
  57.7 1.5 %collective-permute-start.4 = (bf16[8,1024]{1,0:T(8,128)(2,1)S(1)}, bf16[8,1024]{1,0:T(8,128)(2,1)S(1)}, u32[]{:S(2)}, u32[]{:S(2)}) collective-permute-start(bf16[8,1024]{1,0:T(8,128)(2,1)S(1)} %get-tuple-element.107), channel_id=1, source_target_pairs={{0,1},{1,0},{2,3},{3,2},{4,5},{5,4},{6,7},{7,6},{8,9},{9,8},{10,11... | collective-permute-start | bytes 49160 | tf_op jit(solution)/shard_map/ppermute | solution.py:556
  58.1 1.2 %collective-permute-start.5 = (bf16[8,1024]{1,0:T(8,128)(2,1)S(1)}, bf16[8,1024]{1,0:T(8,128)(2,1)S(1)}, u32[]{:S(2)}, u32[]{:S(2)}) collective-permute-start(bf16[8,1024]{1,0:T(8,128)(2,1)S(1)} %get-tuple-element.108), channel_id=1, source_target_pairs={{1,2},{3,4},{5,6},{7,8},{9,10},{11,12},{13,14},{2,1},{4,3},{6,5},{... | collective-permute-start | bytes 49160 | tf_op jit(solution)/shard_map/ppermute | solution.py:555
  65.4 11.2 %all-to-all-start.5 = ((bf16[16,8,128]{2,1,0:T(8,128)(2,1)}), bf16[16,8,128]{2,1,0:T(8,128)(2,1)S(1)}, u32[]{:S(2)}, u32[]{:S(2)}) async-start(bf16[16,8,128]{2,1,0:T(8,128)(2,1)} %get-tuple-element.115), calls=%async_computation.5 | async-start | bytes 65536 | tf_op jit(solution)/shard_map/all_to_all | solution.py:554
  70.0 1.4 %collective-permute-start.6 = (bf16[8,1024]{1,0:T(8,128)(2,1)S(1)}, bf16[8,1024]{1,0:T(8,128)(2,1)S(1)}, u32[]{:S(2)}, u32[]{:S(2)}) collective-permute-start(bf16[8,1024]{1,0:T(8,128)(2,1)S(1)} %get-tuple-element.116), channel_id=1, source_target_pairs={{0,1},{1,0},{2,3},{3,2},{4,5},{5,4},{6,7},{7,6},{8,9},{9,8},{10,11... | collective-permute-start | bytes 49160 | tf_op jit(solution)/shard_map/ppermute | solution.py:556
  70.4 1.0 collective-permute-start.7
  77.7 11.2 %all-to-all-start.6 = ((bf16[16,8,128]{2,1,0:T(8,128)(2,1)}), bf16[16,8,128]{2,1,0:T(8,128)(2,1)S(1)}, u32[]{:S(2)}, u32[]{:S(2)}) async-start(bf16[16,8,128]{2,1,0:T(8,128)(2,1)} %get-tuple-element.124), calls=%async_computation.6 | async-start | bytes 65536 | tf_op jit(solution)/shard_map/all_to_all | solution.py:554
  82.3 1.4 %collective-permute-start.8 = (bf16[8,1024]{1,0:T(8,128)(2,1)S(1)}, bf16[8,1024]{1,0:T(8,128)(2,1)S(1)}, u32[]{:S(2)}, u32[]{:S(2)}) collective-permute-start(bf16[8,1024]{1,0:T(8,128)(2,1)S(1)} %get-tuple-element.125), channel_id=1, source_target_pairs={{0,1},{1,0},{2,3},{3,2},{4,5},{5,4},{6,7},{7,6},{8,9},{9,8},{10,11... | collective-permute-start | bytes 49160 | tf_op jit(solution)/shard_map/ppermute | solution.py:556
  82.8 1.0 collective-permute-start.9
  90.1 11.2 %all-to-all-start.7 = ((bf16[16,8,128]{2,1,0:T(8,128)(2,1)}), bf16[16,8,128]{2,1,0:T(8,128)(2,1)S(1)}, u32[]{:S(2)}, u32[]{:S(2)}) async-start(bf16[16,8,128]{2,1,0:T(8,128)(2,1)} %get-tuple-element.133), calls=%async_computation.7 | async-start | bytes 65536 | tf_op jit(solution)/shard_map/all_to_all | solution.py:554
  94.7 2.9 %collective-permute-start.10 = (bf16[8,1024]{1,0:T(8,128)(2,1)S(1)}, bf16[8,1024]{1,0:T(8,128)(2,1)S(1)}, u32[]{:S(2)}, u32[]{:S(2)}) collective-permute-start(bf16[8,1024]{1,0:T(8,128)(2,1)S(1)} %get-tuple-element.134), channel_id=1, source_target_pairs={{0,1},{1,0},{2,3},{3,2},{4,5},{5,4},{6,7},{7,6},{8,9},{9,8},{10,11... | collective-permute-start | bytes 49160 | tf_op jit(solution)/shard_map/ppermute | solution.py:556
  95.1 2.5 %collective-permute-start.11 = (bf16[8,1024]{1,0:T(8,128)(2,1)S(1)}, bf16[8,1024]{1,0:T(8,128)(2,1)S(1)}, u32[]{:S(2)}, u32[]{:S(2)}) collective-permute-start(bf16[8,1024]{1,0:T(8,128)(2,1)S(1)} %get-tuple-element.135), channel_id=1, source_target_pairs={{1,2},{3,4},{5,6},{7,8},{9,10},{11,12},{13,14},{2,1},{4,3},{6,5},{... | collective-permute-start | bytes 49160 | tf_op jit(solution)/shard_map/ppermute | solution.py:555

commit v5 on v4

--- a/solution.py
+++ b/solution.py
@@ -290,7 +290,7 @@
 
 def backward_part(
     adj_cond, adj_volt, voltage, gate, decay, me_ref, entry_ref, w_ref, w_long_ref,
-    adj_ref, gathered_ref, cond_out, pair_out, cross_out, placed_out, block_ref, slot_ref,
+    adj_ref, gathered_ref, cond_out, cross_out, pair_out, placed_out, block_ref, slot_ref,
     stage_ref, sem,
 ):
     rows, neurons = voltage.shape
@@ -548,7 +548,7 @@
     fetches.append(fetched_t)
     adjs, gathers = [], []
     for moment in reversed(range(STEPS)):
-        adj_t, gathered_t, adj_cond, to_pair, to_cross, placed = back
+        adj_t, gathered_t, adj_cond, to_cross, to_pair, placed = back
         adjs.insert(0, adj_t)
         gathers.insert(0, gathered_t)
         arrived = lax.all_to_all(placed, "azim", split_axis=0, concat_axis=0, tiled=True)
@@ -559,7 +559,7 @@
             [state, state],
             (adj_t, w_all, adj_volt, voltages[moment], conducts[moment + 1], spikes),
         )
-        received = (arrived, from_pair, from_cross, base, gain, wanted)
+        received = (arrived, from_cross, from_pair, base, gain, wanted)
         if moment > 0:
             adj_volt, *back = call(
                 backward_kernel,

time: 103 us -> 102 us (level)
  waiting for transfers between devices: 22 us -> 10.3 us
  starting transfers between devices: 23.6 us -> 34.9 us
    all_to_all x4, waiting for transfers between devices: 19.3 us -> 6.18 us  [local(): lax.all_to_all(placed, 'azim', split_axis=0, concat_axis=0, tiled=True)]
    ppermute x4, starting transfers between devices: 1.57 us -> 13.3 us  [local(): from_pair = lax.ppermute(to_pair, 'azim', pair)]
    ppermute x4, waiting for transfers between devices: 0.01 us -> 1.39 us  [local(): from_pair = lax.ppermute(to_pair, 'azim', pair)]
  transfers between devices with their start and end apart: 16 -> 16, of which waited for: 8 -> 11; matrix products, arithmetic and copies ran while one was open for 0% -> 0% of each run, Pallas kernels for 4% -> 4%
where the time goes in v5:
time: 102 us
  blocking collectives  43.8 us (43%)
  starting transfers between devices  34.9 us (34%)
  Pallas kernels  11.9 us (12%)
  waiting for transfers between devices  10.3 us (10%)
    all_to_all x4, blocking collectives, spread(): lax.all_to_all(values, 'azim', split_axis=0, concat_axis=0, tiled=True, a...  43.8 us
    all_to_all x4, starting transfers between devices, local(): lax.all_to_all(placed, 'azim', split_axis=0, concat_axis=0, tiled=True)  16.8 us
    ppermute x4, starting transfers between devices, local(): from_pair = lax.ppermute(to_pair, 'azim', pair)  13.3 us
    pallas_call x19, Pallas kernels, call(): pl.pallas_call(kernel, out_shape=[pltpu.SMEM(shape, dtype) if len(shape)...  11.9 us
    all_to_all x4, waiting for transfers between devices, local(): lax.all_to_all(placed, 'azim', split_axis=0, concat_axis=0, tiled=True)  6.18 us
    ppermute x4, waiting for transfers between devices, spread(): return (near, lax.ppermute(near, 'azim', pair))  2.73 us
    ppermute x4, starting transfers between devices, local(): from_cross = lax.ppermute(to_cross, 'azim', cross)  2.65 us
    ppermute x4, starting transfers between devices, spread(): return (near, lax.ppermute(near, 'azim', pair))  2.13 us
  transfers between devices with their start and end apart: 16, of which 11 were waited for; matrix products, arithmetic and copies ran while one was open for 0% of the time, Pallas kernels for 4%

profile of v5, /device:TPU:0, one launch (start us, length us, event | category | flops | bytes accessed | tf_op | source)
XLA Modules:
  0.0 101.6 jit_solution(14732304042561627362)
XLA Ops:
  0.6 1.5 %shard_map.138 = (bf16[8,8,1152]{2,1,0:T(8,128)(2,1)S(1)}, s32[1]{0:T(128)S(4)}, s32[112]{0:T(128)S(4)}, f32[8,1024]{1,0:T(8,128)S(1)}, s32[4,8,1024]{2,1,0:T(8,...) custom-call(s32[1,16]{1,0:T(1,128)} %bitcast.6, ...), custom_call_target="tpu_custom_call" | custom-call | tf_op jit(solution)/shard_map/pallas_call | solution.py:436
  2.1 13.7 %all_to_all.40.near_ref.refs_0_ = bf16[8,8,1152]{2,1,0:T(8,128)(2,1)S(1)} all-to-all(bf16[8,8,1152]{2,1,0:T(8,128)(2,1)S(1)} %get-tuple-element.82), channel_id=1, replica_groups={{0,3,4,7,8,11,12,15},{1,2,5,6,9,10,13,14},{16,19,20,23,24,27,28,31},{17..., dimensions={0} | all-to-all | bytes 294912 | tf_op jit(solution)/shard_map/all_to_all | solution.py:464
  15.8 0.7 collective-permute-start
  16.5 0.3 shard_map.139
  16.8 0.7 collective-permute-done.refs_1_.far_ref
  17.5 0.3 shard_map.140
  17.9 10.1 %all_to_all.41.near_ref.refs_0_ = bf16[8,8,1024]{2,1,0:T(8,128)(2,1)S(1)} all-to-all(bf16[8,8,1024]{2,1,0:T(8,128)(2,1)S(1)} %get-tuple-element.92), channel_id=1, replica_groups={{0,3,4,7,8,11,12,15},{1,2,5,6,9,10,13,14},{16,19,20,23,24,27,28,31},{17..., dimensions={0} | all-to-all | bytes 262144 | tf_op jit(solution)/shard_map/all_to_all | solution.py:464
  28.0 0.5 collective-permute-start.1
  28.4 0.3 shard_map.141
  28.8 0.7 collective-permute-done.1.refs_1_
  29.4 0.3 shard_map.142
  29.8 10.0 %all_to_all.42.near_ref.refs_0_ = bf16[8,8,1024]{2,1,0:T(8,128)(2,1)S(1)} all-to-all(bf16[8,8,1024]{2,1,0:T(8,128)(2,1)S(1)} %get-tuple-element.96), channel_id=1, replica_groups={{0,3,4,7,8,11,12,15},{1,2,5,6,9,10,13,14},{16,19,20,23,24,27,28,31},{17..., dimensions={0} | all-to-all | bytes 262144 | tf_op jit(solution)/shard_map/all_to_all | solution.py:464
  39.8 0.5 collective-permute-start.2
  40.2 0.3 shard_map.143
  40.5 0.7 collective-permute-done.2.refs_1_
  41.2 0.3 shard_map.144
  41.5 10.0 %all_to_all.43.near_ref.refs_0_ = bf16[8,8,1024]{2,1,0:T(8,128)(2,1)S(1)} all-to-all(bf16[8,8,1024]{2,1,0:T(8,128)(2,1)S(1)} %get-tuple-element.100), channel_id=1, replica_groups={{0,3,4,7,8,11,12,15},{1,2,5,6,9,10,13,14},{16,19,20,23,24,27,28,31},{17..., dimensions={0} | all-to-all | bytes 262144 | tf_op jit(solution)/shard_map/all_to_all | solution.py:464
  51.5 0.5 collective-permute-start.3
  52.0 0.3 shard_map.145
  52.3 0.7 collective-permute-done.3.refs_1_
  53.0 1.2 %shard_map.146 = (f32[8,1024]{1,0:T(8,128)S(1)}, bf16[4,32,256]{2,1,0:T(8,128)(2,1)S(1)}, bf16[4,32,128]{2,1,0:T(8,128)(2,1)S(1)}, bf16[4,32,256]{2,1,0:T(8,128)...) custom-call(bf16[8,8,1024]{2,1,0:T(8,128)(2,1)S(1)} %all_to_all.43.n, ...), custom_call_target="tpu_custom_call" | custom-call | tf_op jit(solution)/shard_map/pallas_call | solution.py:436
  54.2 3.5 %all-to-all-start.4 = ((bf16[16,8,128]{2,1,0:T(8,128)(2,1)}), bf16[16,8,128]{2,1,0:T(8,128)(2,1)S(1)}, u32[]{:S(2)}, u32[]{:S(2)}) async-start(bf16[16,8,128]{2,1,0:T(8,128)(2,1)} %get-tuple-element.106), calls=%async_computation.4 | async-start | bytes 65536 | tf_op jit(solution)/shard_map/all_to_all | solution.py:554
  57.7 0.7 collective-permute-start.4
  58.4 3.2 %collective-permute-start.5 = (bf16[8,1024]{1,0:T(8,128)(2,1)S(1)}, bf16[8,1024]{1,0:T(8,128)(2,1)S(1)}, u32[]{:S(2)}, u32[]{:S(2)}) collective-permute-start(bf16[8,1024]{1,0:T(8,128)(2,1)S(1)} %get-tuple-element.108), channel_id=1, source_target_pairs={{0,1},{1,0},{2,3},{3,2},{4,5},{5,4},{6,7},{7,6},{8,9},{9,8},{10,11... | collective-permute-start | bytes 49160 | tf_op jit(solution)/shard_map/ppermute | solution.py:556
  61.8 0.3 shard_map.147
  62.2 0.3 collective-permute-done.5.refs_2_
  62.5 1.9 %all-to-all-done.4.refs_0_ = bf16[16,8,128]{2,1,0:T(8,128)(2,1)S(1)} async-done(((bf16[16,8,128]{2,1,0:T(8,128)(2,1)}), bf16[16,8,128]{2,1,0:T(8,128)(2,1)S(1)}, u32[]{:S(2)}, u32[]{:S(2)}) %all-to-all-start.4) | async-done | bytes 32800 | tf_op jit(solution)/shard_map/all_to_all | solution.py:554
  64.3 1.1 %shard_map.149 = (f32[8,1024]{1,0:T(8,128)S(1)}, bf16[4,32,256]{2,1,0:T(8,128)(2,1)S(1)}, bf16[4,32,256]{2,1,0:T(8,128)(2,1)S(1)}, f32[8,1024]{1,0:T(8,128)S(1)}...) custom-call(bf16[16,8,128]{2,1,0:T(8,128)(2,1)S(1)} %all-to-all-done.4.refs_0_, ...), custom_call_target="tpu_custom_call" | custom-call | tf_op jit(solution)/shard_map/pallas_call | solution.py:436
  65.4 4.4 %all-to-all-start.5 = ((bf16[16,8,128]{2,1,0:T(8,128)(2,1)}), bf16[16,8,128]{2,1,0:T(8,128)(2,1)S(1)}, u32[]{:S(2)}, u32[]{:S(2)}) async-start(bf16[16,8,128]{2,1,0:T(8,128)(2,1)} %get-tuple-element.115), calls=%async_computation.5 | async-start | bytes 65536 | tf_op jit(solution)/shard_map/all_to_all | solution.py:554
  69.9 0.7 collective-permute-start.6
  70.5 3.3 %collective-permute-start.7 = (bf16[8,1024]{1,0:T(8,128)(2,1)S(1)}, bf16[8,1024]{1,0:T(8,128)(2,1)S(1)}, u32[]{:S(2)}, u32[]{:S(2)}) collective-permute-start(bf16[8,1024]{1,0:T(8,128)(2,1)S(1)} %get-tuple-element.117), channel_id=1, source_target_pairs={{0,1},{1,0},{2,3},{3,2},{4,5},{5,4},{6,7},{7,6},{8,9},{9,8},{10,11... | collective-permute-start | bytes 49160 | tf_op jit(solution)/shard_map/ppermute | solution.py:556
  73.9 0.3 shard_map.150
  74.2 0.5 collective-permute-done.7.refs_2_
  74.7 1.8 %all-to-all-done.5.refs_0_ = bf16[16,8,128]{2,1,0:T(8,128)(2,1)S(1)} async-done(((bf16[16,8,128]{2,1,0:T(8,128)(2,1)}), bf16[16,8,128]{2,1,0:T(8,128)(2,1)S(1)}, u32[]{:S(2)}, u32[]{:S(2)}) %all-to-all-start.5) | async-done | bytes 32800 | tf_op jit(solution)/shard_map/all_to_all | solution.py:554
  76.5 1.1 %shard_map.151 = (f32[8,1024]{1,0:T(8,128)S(1)}, bf16[4,32,256]{2,1,0:T(8,128)(2,1)S(1)}, bf16[4,32,256]{2,1,0:T(8,128)(2,1)S(1)}, f32[8,1024]{1,0:T(8,128)S(1)}...) custom-call(bf16[16,8,128]{2,1,0:T(8,128)(2,1)S(1)} %all-to-all-done.5.refs_0_, ...), custom_call_target="tpu_custom_call" | custom-call | tf_op jit(solution)/shard_map/pallas_call | solution.py:436
  77.6 4.4 %all-to-all-start.6 = ((bf16[16,8,128]{2,1,0:T(8,128)(2,1)}), bf16[16,8,128]{2,1,0:T(8,128)(2,1)S(1)}, u32[]{:S(2)}, u32[]{:S(2)}) async-start(bf16[16,8,128]{2,1,0:T(8,128)(2,1)} %get-tuple-element.124), calls=%async_computation.6 | async-start | bytes 65536 | tf_op jit(solution)/shard_map/all_to_all | solution.py:554
  82.1 0.7 collective-permute-start.8
  82.7 3.3 %collective-permute-start.9 = (bf16[8,1024]{1,0:T(8,128)(2,1)S(1)}, bf16[8,1024]{1,0:T(8,128)(2,1)S(1)}, u32[]{:S(2)}, u32[]{:S(2)}) collective-permute-start(bf16[8,1024]{1,0:T(8,128)(2,1)S(1)} %get-tuple-element.126), channel_id=1, source_target_pairs={{0,1},{1,0},{2,3},{3,2},{4,5},{5,4},{6,7},{7,6},{8,9},{9,8},{10,11... | collective-permute-start | bytes 49160 | tf_op jit(solution)/shard_map/ppermute | solution.py:556
  86.1 0.3 shard_map.152
  86.4 0.5 collective-permute-done.9.refs_2_
  86.9 1.8 %all-to-all-done.6.refs_0_ = bf16[16,8,128]{2,1,0:T(8,128)(2,1)S(1)} async-done(((bf16[16,8,128]{2,1,0:T(8,128)(2,1)}), bf16[16,8,128]{2,1,0:T(8,128)(2,1)S(1)}, u32[]{:S(2)}, u32[]{:S(2)}) %all-to-all-start.6) | async-done | bytes 32800 | tf_op jit(solution)/shard_map/all_to_all | solution.py:554
  88.7 1.1 %shard_map.153 = (f32[8,1024]{1,0:T(8,128)S(1)}, bf16[4,32,256]{2,1,0:T(8,128)(2,1)S(1)}, bf16[4,32,256]{2,1,0:T(8,128)(2,1)S(1)}, f32[8,1024]{1,0:T(8,128)S(1)}...) custom-call(bf16[16,8,128]{2,1,0:T(8,128)(2,1)S(1)} %all-to-all-done.6.refs_0_, ...), custom_call_target="tpu_custom_call" | custom-call | tf_op jit(solution)/shard_map/pallas_call | solution.py:436
  89.8 4.4 %all-to-all-start.7 = ((bf16[16,8,128]{2,1,0:T(8,128)(2,1)}), bf16[16,8,128]{2,1,0:T(8,128)(2,1)S(1)}, u32[]{:S(2)}, u32[]{:S(2)}) async-start(bf16[16,8,128]{2,1,0:T(8,128)(2,1)} %get-tuple-element.133), calls=%async_computation.7 | async-start | bytes 65536 | tf_op jit(solution)/shard_map/all_to_all | solution.py:554
  94.2 0.7 collective-permute-start.10
  94.9 3.3 %collective-permute-start.11 = (bf16[8,1024]{1,0:T(8,128)(2,1)S(1)}, bf16[8,1024]{1,0:T(8,128)(2,1)S(1)}, u32[]{:S(2)}, u32[]{:S(2)}) collective-permute-start(bf16[8,1024]{1,0:T(8,128)(2,1)S(1)} %get-tuple-element.135), channel_id=1, source_target_pairs={{0,1},{1,0},{2,3},{3,2},{4,5},{5,4},{6,7},{7,6},{8,9},{9,8},{10,11... | collective-permute-start | bytes 49160 | tf_op jit(solution)/shard_map/ppermute | solution.py:556
  98.5 1.6 %shard_map.156 = (bf16[3,192,1024]{2,1,0:T(8,128)(2,1)}, bf16[64,1024]{1,0:T(8,128)(2,1)}, f32[8,1024]{1,0:T(8,128)}) custom-call(bf16[2,4,32,256]{3,2,1,0:T(8,128)(2,1)S(1)} %get-tuple-element.140.refs_0_, bf16[2,4,32,256]{3,2,1,0:T(8,128)(2,1)S(1)} %get-tuple-element.141.refs_1_, bf16[2,4,32,256]{3,2,1,0:T(8,128)(2,1)S(1)} %get-tuple-element.142.refs_2_, ...), custom_call_target="tpu_custom_call" | custom-call | tf_op jit(solution)/shard_map/pallas_call | solution.py:436
  100.1 0.8 all-to-all-done.7.refs_0_
  100.9 0.8 shard_map.155
  (7 shorter events, 0.5 us)
Async XLA Ops:
  15.8 1.7 %collective-permute-start = (bf16[8,8,1152]{2,1,0:T(8,128)(2,1)S(1)}, bf16[8,8,1152]{2,1,0:T(8,128)(2,1)S(1)}, u32[]{:S(2)}, u32[]{:S(2)}) collective-permute-start(bf16[8,8,1152]{2,1,0:T(8,128)(2,1)S(1)} %all_to_all.40.near_ref.refs_0_), channel_id=1, source_target_pairs={{0,1},{1,0},{2,3},{3,2},{4,5},{5,4},{6,7},{7,6},{8,9},{9,8},{10,11... | collective-permute-start | bytes 442376 | tf_op jit(solution)/shard_map/ppermute | solution.py:467
  28.0 1.4 %collective-permute-start.1 = (bf16[8,8,1024]{2,1,0:T(8,128)(2,1)S(1)}, bf16[8,8,1024]{2,1,0:T(8,128)(2,1)S(1)}, u32[]{:S(2)}, u32[]{:S(2)}) collective-permute-start(bf16[8,8,1024]{2,1,0:T(8,128)(2,1)S(1)} %all_to_all.41.near_ref.refs_0_), channel_id=1, source_target_pairs={{0,1},{1,0},{2,3},{3,2},{4,5},{5,4},{6,7},{7,6},{8,9},{9,8},{10,11... | collective-permute-start | bytes 393224 | tf_op jit(solution)/shard_map/ppermute | solution.py:467
  39.8 1.4 %collective-permute-start.2 = (bf16[8,8,1024]{2,1,0:T(8,128)(2,1)S(1)}, bf16[8,8,1024]{2,1,0:T(8,128)(2,1)S(1)}, u32[]{:S(2)}, u32[]{:S(2)}) collective-permute-start(bf16[8,8,1024]{2,1,0:T(8,128)(2,1)S(1)} %all_to_all.42.near_ref.refs_0_), channel_id=1, source_target_pairs={{0,1},{1,0},{2,3},{3,2},{4,5},{5,4},{6,7},{7,6},{8,9},{9,8},{10,11... | collective-permute-start | bytes 393224 | tf_op jit(solution)/shard_map/ppermute | solution.py:467
  51.5 1.4 %collective-permute-start.3 = (bf16[8,8,1024]{2,1,0:T(8,128)(2,1)S(1)}, bf16[8,8,1024]{2,1,0:T(8,128)(2,1)S(1)}, u32[]{:S(2)}, u32[]{:S(2)}) collective-permute-start(bf16[8,8,1024]{2,1,0:T(8,128)(2,1)S(1)} %all_to_all.43.near_ref.refs_0_), channel_id=1, source_target_pairs={{0,1},{1,0},{2,3},{3,2},{4,5},{5,4},{6,7},{7,6},{8,9},{9,8},{10,11... | collective-permute-start | bytes 393224 | tf_op jit(solution)/shard_map/ppermute | solution.py:467
  54.2 10.1 %all-to-all-start.4 = ((bf16[16,8,128]{2,1,0:T(8,128)(2,1)}), bf16[16,8,128]{2,1,0:T(8,128)(2,1)S(1)}, u32[]{:S(2)}, u32[]{:S(2)}) async-start(bf16[16,8,128]{2,1,0:T(8,128)(2,1)} %get-tuple-element.106), calls=%async_computation.4 | async-start | bytes 65536 | tf_op jit(solution)/shard_map/all_to_all | solution.py:554
  57.7 4.4 %collective-permute-start.4 = (bf16[8,1024]{1,0:T(8,128)(2,1)S(1)}, bf16[8,1024]{1,0:T(8,128)(2,1)S(1)}, u32[]{:S(2)}, u32[]{:S(2)}) collective-permute-start(bf16[8,1024]{1,0:T(8,128)(2,1)S(1)} %get-tuple-element.107), channel_id=1, source_target_pairs={{1,2},{3,4},{5,6},{7,8},{9,10},{11,12},{13,14},{2,1},{4,3},{6,5},{... | collective-permute-start | bytes 49160 | tf_op jit(solution)/shard_map/ppermute | solution.py:555
  58.4 4.1 %collective-permute-start.5 = (bf16[8,1024]{1,0:T(8,128)(2,1)S(1)}, bf16[8,1024]{1,0:T(8,128)(2,1)S(1)}, u32[]{:S(2)}, u32[]{:S(2)}) collective-permute-start(bf16[8,1024]{1,0:T(8,128)(2,1)S(1)} %get-tuple-element.108), channel_id=1, source_target_pairs={{0,1},{1,0},{2,3},{3,2},{4,5},{5,4},{6,7},{7,6},{8,9},{9,8},{10,11... | collective-permute-start | bytes 49160 | tf_op jit(solution)/shard_map/ppermute | solution.py:556
  65.4 11.1 %all-to-all-start.5 = ((bf16[16,8,128]{2,1,0:T(8,128)(2,1)}), bf16[16,8,128]{2,1,0:T(8,128)(2,1)S(1)}, u32[]{:S(2)}, u32[]{:S(2)}) async-start(bf16[16,8,128]{2,1,0:T(8,128)(2,1)} %get-tuple-element.115), calls=%async_computation.5 | async-start | bytes 65536 | tf_op jit(solution)/shard_map/all_to_all | solution.py:554
  69.9 4.3 %collective-permute-start.6 = (bf16[8,1024]{1,0:T(8,128)(2,1)S(1)}, bf16[8,1024]{1,0:T(8,128)(2,1)S(1)}, u32[]{:S(2)}, u32[]{:S(2)}) collective-permute-start(bf16[8,1024]{1,0:T(8,128)(2,1)S(1)} %get-tuple-element.116), channel_id=1, source_target_pairs={{1,2},{3,4},{5,6},{7,8},{9,10},{11,12},{13,14},{2,1},{4,3},{6,5},{... | collective-permute-start | bytes 49160 | tf_op jit(solution)/shard_map/ppermute | solution.py:555
  70.5 4.2 %collective-permute-start.7 = (bf16[8,1024]{1,0:T(8,128)(2,1)S(1)}, bf16[8,1024]{1,0:T(8,128)(2,1)S(1)}, u32[]{:S(2)}, u32[]{:S(2)}) collective-permute-start(bf16[8,1024]{1,0:T(8,128)(2,1)S(1)} %get-tuple-element.117), channel_id=1, source_target_pairs={{0,1},{1,0},{2,3},{3,2},{4,5},{5,4},{6,7},{7,6},{8,9},{9,8},{10,11... | collective-permute-start | bytes 49160 | tf_op jit(solution)/shard_map/ppermute | solution.py:556
  77.6 11.1 %all-to-all-start.6 = ((bf16[16,8,128]{2,1,0:T(8,128)(2,1)}), bf16[16,8,128]{2,1,0:T(8,128)(2,1)S(1)}, u32[]{:S(2)}, u32[]{:S(2)}) async-start(bf16[16,8,128]{2,1,0:T(8,128)(2,1)} %get-tuple-element.124), calls=%async_computation.6 | async-start | bytes 65536 | tf_op jit(solution)/shard_map/all_to_all | solution.py:554
  82.1 4.3 %collective-permute-start.8 = (bf16[8,1024]{1,0:T(8,128)(2,1)S(1)}, bf16[8,1024]{1,0:T(8,128)(2,1)S(1)}, u32[]{:S(2)}, u32[]{:S(2)}) collective-permute-start(bf16[8,1024]{1,0:T(8,128)(2,1)S(1)} %get-tuple-element.125), channel_id=1, source_target_pairs={{1,2},{3,4},{5,6},{7,8},{9,10},{11,12},{13,14},{2,1},{4,3},{6,5},{... | collective-permute-start | bytes 49160 | tf_op jit(solution)/shard_map/ppermute | solution.py:555
  82.7 4.2 %collective-permute-start.9 = (bf16[8,1024]{1,0:T(8,128)(2,1)S(1)}, bf16[8,1024]{1,0:T(8,128)(2,1)S(1)}, u32[]{:S(2)}, u32[]{:S(2)}) collective-permute-start(bf16[8,1024]{1,0:T(8,128)(2,1)S(1)} %get-tuple-element.126), channel_id=1, source_target_pairs={{0,1},{1,0},{2,3},{3,2},{4,5},{5,4},{6,7},{7,6},{8,9},{9,8},{10,11... | collective-permute-start | bytes 49160 | tf_op jit(solution)/shard_map/ppermute | solution.py:556
  89.8 11.1 %all-to-all-start.7 = ((bf16[16,8,128]{2,1,0:T(8,128)(2,1)}), bf16[16,8,128]{2,1,0:T(8,128)(2,1)S(1)}, u32[]{:S(2)}, u32[]{:S(2)}) async-start(bf16[16,8,128]{2,1,0:T(8,128)(2,1)} %get-tuple-element.133), calls=%async_computation.7 | async-start | bytes 65536 | tf_op jit(solution)/shard_map/all_to_all | solution.py:554
  94.2 5.9 %collective-permute-start.10 = (bf16[8,1024]{1,0:T(8,128)(2,1)S(1)}, bf16[8,1024]{1,0:T(8,128)(2,1)S(1)}, u32[]{:S(2)}, u32[]{:S(2)}) collective-permute-start(bf16[8,1024]{1,0:T(8,128)(2,1)S(1)} %get-tuple-element.134), channel_id=1, source_target_pairs={{1,2},{3,4},{5,6},{7,8},{9,10},{11,12},{13,14},{2,1},{4,3},{6,5},{... | collective-permute-start | bytes 49160 | tf_op jit(solution)/shard_map/ppermute | solution.py:555
  94.9 5.2 %collective-permute-start.11 = (bf16[8,1024]{1,0:T(8,128)(2,1)S(1)}, bf16[8,1024]{1,0:T(8,128)(2,1)S(1)}, u32[]{:S(2)}, u32[]{:S(2)}) collective-permute-start(bf16[8,1024]{1,0:T(8,128)(2,1)S(1)} %get-tuple-element.135), channel_id=1, source_target_pairs={{0,1},{1,0},{2,3},{3,2},{4,5},{5,4},{6,7},{7,6},{8,9},{9,8},{10,11... | collective-permute-start | bytes 49160 | tf_op jit(solution)/shard_map/ppermute | solution.py:556

commit v6 on v2

v6 whole, which is shorter than its diff:
```python
import functools

import jax
import jax.numpy as jnp
from jax import lax
from jax.experimental import pallas as pl
from jax.experimental.pallas import tpu as pltpu
from jax.sharding import PartitionSpec as P

BLK = 64
CAP = 2
STEPS = 4
LANES = 128
GROUP = 4
WIDE = GROUP * BLK
SIDE = 3 * BLK

f32 = jnp.float32
bf16 = jnp.bfloat16


def surrogate(voltage):
    return jax.nn.sigmoid(2.0 * (voltage - 1.0))


def lane_half(rows):
    return lax.broadcasted_iota(jnp.int32, (rows, LANES), 1) // BLK


def half_only(piece, half, which):
    return jnp.where(half == which, piece, 0.0)


def half_pair(first, second, half):
    return jnp.where(half == 0, first, second)


def swapped(piece):
    return pltpu.roll(piece, BLK, 1)


def chunks_of(values):
    return [values[:, c * LANES : (c + 1) * LANES] for c in range(values.shape[1] // LANES)]


def odd_chunks(chunks, half):
    turned = [swapped(piece) for piece in chunks]
    zero = jnp.zeros_like(chunks[0])
    return [
        half_pair(left, right, half) for left, right in zip([zero] + turned, turned + [zero])
    ]


def product(left, right):
    return lax.dot_general(left, right, (((1,), (0,)), ((), ())), preferred_element_type=f32)


def product_back(left, right):
    return lax.dot_general(left, right, (((1,), (1,)), ((), ())), preferred_element_type=f32)


def product_over(left, right):
    return lax.dot_general(left, right, (((0,), (0,)), ((), ())), preferred_element_type=f32)


def stacked(pieces):
    return jnp.concatenate(pieces, axis=0)


def folded(acc_refs, half):
    chunks = []
    for block in range(0, acc_refs[0].shape[0], 2):
        (low, low_next), (high, high_next) = (
            (sum(ref[block] for ref in refs), sum(ref[block + 1] for ref in refs))
            for refs in (acc_refs[0::2], acc_refs[1::2])
        )
        chunks.append(half_pair(low, high_next, half) + swapped(half_pair(low_next, high, half)))
    return chunks


def in_group(tile):
    return (tile ^ (tile >> 1)) & 1


ACCS = 4


def sublane_half(rows, lanes):
    return lax.broadcasted_iota(jnp.int32, (rows, lanes), 0) // (rows // 2)


def turned(values):
    return pltpu.roll(values, values.shape[0] // 2, 0)


def row_halves(upper, lower):
    return jnp.where(sublane_half(*upper.shape) == 0, upper, lower)


def tile_rows(lanes, rows=GROUP * 8):
    return (lax.broadcasted_iota(jnp.int32, (rows, lanes), 0) // 4) % 2


def copied(pairs, sems):
    copies = [
        pltpu.make_async_copy(source, target, sems.at[number])
        for number, (source, target) in enumerate(pairs)
    ]
    for copy in copies:
        copy.start()
    return copies


def start_kernel(*refs):
    ins, (keep_out, send_out), scratch = refs[:9], refs[9:11], refs[11:]
    kept, sems = scratch[:-1], scratch[-1]
    copies = copied(zip(ins, kept), sems)
    v, spikes, g, adj_v, adj_g, decay, tile_ref, block_ref, target_ref = kept
    rows, neurons = v.shape
    entries = tile_ref.shape[1]
    half = in_group(lax.axis_index("azim"))
    for copy in copies:
        copy.wait()
    across = lax.broadcasted_iota(jnp.int32, (entries, entries), 1)
    down = lax.broadcasted_iota(jnp.int32, (entries, entries), 0)
    tiles = tile_ref[...]
    tiles_down = jnp.sum(
        jnp.where(across == down, tiles.astype(f32), 0.0), axis=1, keepdims=True
    ).astype(jnp.int32)
    earlier = (tiles_down == tiles) & (down < across)
    rank = jnp.sum(jnp.where(earlier, 1.0, 0.0), axis=0, keepdims=True).astype(jnp.int32)
    code = ((tiles * CAP + rank) * 16 + target_ref[...]) * 16 + block_ref[...]
    pairs = ((v[...], g[...]), (adj_v[...], adj_g[...])) + tuple(
        (spikes[k].astype(f32), spikes[k + 1].astype(f32)) for k in range(0, STEPS, 2)
    )
    for number, (first, second) in enumerate(pairs):
        straight = row_halves(first, turned(second))
        crossed = row_halves(turned(first), second)
        keep_out[number] = jnp.where(half == 0, straight, crossed)
        send_out[number] = jnp.where(half == 0, crossed, straight)
    for out in (keep_out, send_out):
        out[len(pairs)] = jnp.zeros((rows, neurons), f32)
        out[len(pairs), 0:1, :] = decay[...]
        out[len(pairs), 1:2, :entries] = code.astype(f32)


def hold_kernel(w_ref, w_long_ref, w_out, w_long_out, sems):
    for copy in copied(((w_ref, w_out), (w_long_ref, w_long_out)), sems):
        copy.wait()


def merge_kernel(
    keep_ref, got_ref, out_ref, v_out, g_out, adj_v_out, adj_g_out, spikes_out, decay_out,
    entry_out, fields_ref, sem,
):
    core = lax.axis_index("azim") & 1
    rows, neurons = v_out.shape
    first = [jnp.where(core == 0, keep_ref[k], got_ref[k]) for k in range(keep_ref.shape[0])]
    second = [jnp.where(core == 0, got_ref[k], keep_ref[k]) for k in range(keep_ref.shape[0])]
    lanes = fields_ref.shape[1] // 2
    for at, block in enumerate((keep_ref[len(first) - 1], got_ref[len(first) - 1])):
        code = block[1:2, :lanes].astype(jnp.int32)
        columns = slice(at * lanes, (at + 1) * lanes)
        fields = (
            code >> 10, ((code & 15) >> 1) * LANES, (code >> 9) & 1, code & 1, (code >> 4) & 15,
            code >> 9, (code >> 8) & 1, code & 15,
        )
        fields_ref[:, columns] = jnp.concatenate(fields, axis=0)
    copy = pltpu.make_async_copy(fields_ref, entry_out, sem)
    copy.start()
    merged = []
    for low, high in zip(first[:-1], second[:-1]):
        merged += [row_halves(low, turned(high)), row_halves(turned(low), high)]
    v, g, adj_v, adj_g, *spikes = merged
    activity = (spikes[0] * surrogate(v)).astype(bf16)
    for chip in range(out_ref.shape[0]):
        out_ref[chip] = activity
    v_out[...] = v
    g_out[...] = g
    adj_v_out[...] = adj_v
    adj_g_out[...] = adj_g
    for moment, spiking in enumerate(spikes):
        spikes_out[moment] = spiking
    decay_out[...] = row_halves(
        jnp.broadcast_to(first[-1][0:1, :], (rows, neurons)),
        jnp.broadcast_to(second[-1][0:1, :], (rows, neurons)),
    )
    copy.wait()


def entry_index(entry_ref, role, entry):
    return role * (entry_ref.shape[1] // 2) + entry


def forward_part(
    near_ref, entry_ref, w_ref, w_mate_ref, w_long_ref, w_long_mate_ref, source_ref, fetched_ref,
    acc_refs,
):
    chips, rows, _ = near_ref.shape
    neurons = w_ref.shape[2]
    blocks = neurons // BLK
    half = lane_half(rows)
    me = lax.axis_index("azim")
    chip = me >> 1
    core = me & 1
    for ref in acc_refs:
        ref[...] = jnp.zeros_like(ref)
    groups = fetched_ref.shape[0] // 2
    row_half = sublane_half(rows, LANES)
    for role, long_ref in enumerate((w_long_ref, w_long_mate_ref)):
        own_row = core if role == 0 else 1 - core
        for group in range(groups):
            pieces, targets = [], []
            for entry in range(GROUP * group, GROUP * (group + 1)):
                at = entry_index(entry_ref, role, entry)
                lanes = pl.ds(pl.multiple_of(entry_ref[1, at], LANES), LANES)
                piece = near_ref[entry_ref[0, at], :, lanes].astype(f32)
                piece = jnp.where(entry_ref[2, at] == own_row, piece, turned(piece))
                chosen = (row_half == own_row) & (half == entry_ref[3, at])
                pieces.append(jnp.where(chosen, piece, 0.0))
                targets.append(entry_ref[4, at])
            fetched = stacked(pieces).astype(bf16)
            fetched_ref[role * groups + group] = fetched
            weights = long_ref[:, group * WIDE : (group + 1) * WIDE]
            total = product(fetched, stacked([weights, weights]))
            for at, target in enumerate(targets):
                lanes = slice(at // 2 * LANES, (at // 2 + 1) * LANES)
                acc_refs[(at + 2 * group) % len(acc_refs)][target] += total[
                    at * rows : (at + 1) * rows, lanes
                ]
    own = near_ref[chip, :, :neurons].astype(f32)
    left = near_ref[jnp.maximum(chip - 1, 0), :, :neurons].astype(f32)
    right = near_ref[jnp.minimum(chip + 1, chips - 1), :, :neurons].astype(f32)
    left = jnp.where(chip > 0, turned(left), 0.0)
    right = jnp.where(chip < chips - 1, turned(right), 0.0)
    sides = (row_halves(left, turned(own)), own, row_halves(turned(own), right))
    for side, values in enumerate(sides):
        even = chunks_of(values)
        odd = odd_chunks(even, half)
        even = even + [jnp.zeros((rows, LANES), f32)]
        for group in range(blocks // GROUP):
            pieces = []
            for block in range(GROUP * group, GROUP * (group + 1)):
                line = even if block % 2 else odd
                pieces.append((line[block // 2], line[block // 2 + 1]))
            source_ref[side, group] = jnp.concatenate(
                [stacked([piece[k] for piece in pieces]) for k in range(2)], axis=1
            ).astype(bf16)
    own_rows = tile_rows(WIDE) == core
    drive = []
    for group in range(blocks // GROUP):
        columns = slice(group * WIDE, (group + 1) * WIDE)
        totals = []
        for ref in (w_ref, w_mate_ref):
            total = product(source_ref[0, group][:, :SIDE], ref[0, :, columns])
            for side in range(1, 3):
                total = total + product(source_ref[side, group][:, :SIDE], ref[side, :, columns])
            totals.append(total)
        total = jnp.where(own_rows, *totals)
        for pair in range(GROUP // 2):
            lanes = slice(pair * LANES, (pair + 1) * LANES)
            at = 2 * pair * rows
            drive.append(
                half_pair(
                    total[at : at + rows, lanes], total[at + rows : at + 2 * rows, lanes], half
                )
            )
    extra = folded(acc_refs, half)
    return jnp.concatenate([a + b for a, b in zip(drive, extra)], axis=1)


def forward_kernel(moment, *refs):
    near_ref, entry_ref, w_ref, w_mate_ref, w_long_ref, w_long_mate_ref = refs[:6]
    v_ref, g_ref, decay_ref, spikes_ref = refs[6:10]
    v_out, g_out, gate_out, source_ref, fetched_ref, act_ref = refs[10:16]
    acc_refs = refs[16 : 16 + ACCS] if moment != 1 else refs[17 : 17 + ACCS]
    chips = act_ref.shape[0]
    rows, neurons = v_ref.shape
    if moment == 1:
        asked_ref = refs[16]
        for chip in range(chips):
            asked = near_ref[chip, :, neurons:].astype(f32)
            asked_ref[chip : chip + 1, :] = asked[0:1, :].astype(jnp.int32)
    drive = forward_part(
        near_ref, entry_ref, w_ref, w_mate_ref, w_long_ref, w_long_mate_ref, source_ref,
        fetched_ref, acc_refs,
    )
    voltage = v_ref[...]
    conduct = decay_ref[...] * g_ref[...] + jax.nn.softplus(drive)
    voltage = voltage + 0.1 * (conduct * (3.0 - voltage) - voltage) - spikes_ref[moment]
    v_out[...] = voltage
    g_out[...] = conduct
    gate_out[...] = jax.nn.sigmoid(drive)
    activity = (spikes_ref[moment + 1] * surrogate(voltage)).astype(bf16)
    for chip in range(chips):
        act_ref[chip, :, :neurons] = activity
    if moment == 0:
        ask_ref = refs[-1]
        core = lax.axis_index("azim") & 1
        lane = lax.broadcasted_iota(jnp.int32, (rows, LANES), 1)
        ask_ref[...] = jnp.zeros_like(ask_ref)
        for role in range(2):
            own_row = core if role == 0 else 1 - core
            for entry in range(fetched_ref.shape[0] // 2 * GROUP):
                at = entry_index(entry_ref, role, entry)
                place = own_row * 4 + entry_ref[2, at] * CAP + entry_ref[6, at]
                chip = entry_ref[0, at]
                ask_ref[chip] = jnp.where(
                    lane == place, entry_ref[7, at].astype(f32), ask_ref[chip]
                )
        for chip in range(chips):
            act_ref[chip, :, neurons:] = ask_ref[chip].astype(bf16)


def toward_side(side, adj_ref, w_ref, w_mate_ref, own_rows):
    groups, rows, _ = adj_ref.shape
    rows = rows // GROUP
    blocks = groups * GROUP
    half = lane_half(rows)
    zero = jnp.zeros((rows, LANES), f32)
    even = [zero] * (blocks // 2 + 1)
    odd = [zero] * (blocks // 2 + 1)
    for group in range(groups):
        columns = slice(group * WIDE, (group + 1) * WIDE)
        adj = adj_ref[group]
        back = jnp.where(
            own_rows,
            product_back(adj, w_ref[side, :, columns]),
            product_back(adj, w_mate_ref[side, :, columns]),
        )
        for at in range(GROUP):
            block = GROUP * group + at
            line = even if block % 2 else odd
            lower = back[at * rows : (at + 1) * rows, :LANES]
            upper = back[at * rows : (at + 1) * rows, LANES:]
            upper = jnp.concatenate([upper, jnp.zeros_like(upper)], axis=1)
            line[block // 2] = line[block // 2] + lower
            line[block // 2 + 1] = line[block // 2 + 1] + upper
    moved = [swapped(piece) for piece in odd]
    return jnp.concatenate(
        [even[c] + half_pair(moved[c], moved[c + 1], half) for c in range(blocks // 2)], axis=1
    )


def backward_part(
    adj_cond, adj_volt, voltage, gate, decay, entry_ref, w_ref, w_mate_ref, w_long_ref,
    w_long_mate_ref, adj_ref, gathered_ref, cond_out, own_out, placed_out, block_ref, slot_ref,
):
    rows, neurons = voltage.shape
    blocks = neurons // BLK
    chips = placed_out.shape[0]
    half = lane_half(rows)
    me = lax.axis_index("azim")
    chip = me >> 1
    core = me & 1
    total_g = adj_cond + adj_volt * 0.1 * (3.0 - voltage)
    adj_drive = (total_g * gate).astype(bf16).astype(f32)
    cond_out[...] = decay * total_g
    chunks = chunks_of(adj_drive)
    zero = jnp.zeros((rows, LANES), f32)
    for number, piece in enumerate(chunks):
        moved = swapped(piece)
        block_ref[2 * number] = half_pair(piece, moved, half)
        block_ref[2 * number + 1] = half_pair(moved, piece, half)
    slot_ref[...] = jnp.zeros_like(slot_ref)
    groups = gathered_ref.shape[0] // 2
    row_half = sublane_half(rows, LANES)
    for role, long_ref in enumerate((w_long_ref, w_long_mate_ref)):
        own_row = core if role == 0 else 1 - core
        for group in range(groups):
            left, right, slots = [], [], []
            for at in range(GROUP):
                entry = entry_index(entry_ref, role, GROUP * group + at)
                slots.append((entry_ref[6, entry], entry_ref[5, entry]))
                chosen = (row_half == own_row) & (half == at % 2)
                piece = jnp.where(chosen, block_ref[entry_ref[4, entry]], 0.0)
                left.append(piece if at < 2 else zero)
                right.append(zero if at < 2 else piece)
            gathered = jnp.concatenate([stacked(left), stacked(right)], axis=1).astype(bf16)
            gathered_ref[role * groups + group] = gathered
            weights = long_ref[:, group * WIDE : (group + 1) * WIDE]
            back = product_back(gathered, stacked([weights, weights]))
            for at, slot in enumerate(slots):
                slot_ref[slot] += back[at * rows : (at + 1) * rows]
    for tile in range(2 * chips):
        lanes = slice(tile % 2 * LANES, (tile % 2 + 1) * LANES)
        placed_out[tile // 2, :, lanes] = half_pair(
            slot_ref[0, tile], slot_ref[1, tile], half
        ).astype(bf16)
    for group in range(blocks // GROUP):
        left = stacked([half_only(chunks[2 * group], half, k) for k in range(2)] + [zero, zero])
        right = stacked(
            [zero, zero] + [half_only(chunks[2 * group + 1], half, k) for k in range(2)]
        )
        adj_ref[group] = jnp.concatenate([left, right], axis=1).astype(bf16)
    own_rows = tile_rows(SIDE) == core
    before, own, after = (
        toward_side(side, adj_ref, w_ref, w_mate_ref, own_rows) for side in range(3)
    )
    own_out[...] = own + row_halves(turned(before), turned(after))
    middle = neurons // 2
    to_left = row_halves(before[:, :middle], turned(before[:, middle:])).astype(bf16)
    to_right = row_halves(turned(after[:, :middle]), after[:, middle:]).astype(bf16)
    unused = jnp.zeros_like(to_left)
    for other in range(chips):
        placed_out[other, :, 2 * LANES :] = unused
    placed_out[jnp.where(chip > 0, chip - 1, chip), :, 2 * LANES :] = to_left
    placed_out[jnp.where(chip < chips - 1, chip + 1, chip), :, 2 * LANES :] = to_right


def turn_kernel(*refs):
    near_ref, entry_ref, w_ref, w_mate_ref, w_long_ref, w_long_mate_ref = refs[:6]
    v_ref, g_ref, decay_ref, adj_v_ref, adj_g_ref, asked_ref = refs[6:12]
    g_out, wanted_out, source_ref, fetched_ref = refs[12:16]
    copy = pltpu.make_async_copy(asked_ref, wanted_out, refs[-1])
    copy.start()
    drive = forward_part(
        near_ref, entry_ref, w_ref, w_mate_ref, w_long_ref, w_long_mate_ref, source_ref,
        fetched_ref, refs[23:-1],
    )
    decay = decay_ref[...]
    g_out[...] = decay * g_ref[...] + jax.nn.softplus(drive)
    backward_part(
        adj_g_ref[...], adj_v_ref[...], v_ref[...], jax.nn.sigmoid(drive), decay,
        entry_ref, w_ref, w_mate_ref, w_long_ref, w_long_mate_ref, *refs[16:23],
    )
    copy.wait()


def receive_part(
    moment, placed_ref, own_ref, wanted_ref, adj_v_ref, v_ref, g_ref, spikes_ref, acc_refs
):
    chips, rows, _ = placed_ref.shape
    half = lane_half(rows)
    row_half = sublane_half(rows, LANES)
    chip = lax.axis_index("azim") >> 1
    for ref in acc_refs:
        ref[...] = jnp.zeros_like(ref)
    for other in range(chips):
        for source in range(2):
            arrived = placed_ref[other, :, source * LANES : (source + 1) * LANES].astype(f32)
            for target, piece in ((source, arrived), (1 - source, turned(arrived))):
                piece = jnp.where(row_half == source, piece, 0.0)
                for slot in range(CAP):
                    number = (slot + CAP * target) % len(acc_refs)
                    block = wanted_ref[other, target * 4 + source * CAP + slot]
                    acc_refs[number][block] += piece
    left = placed_ref[jnp.maximum(chip - 1, 0), :, 2 * LANES :].astype(f32)
    right = placed_ref[jnp.minimum(chip + 1, chips - 1), :, 2 * LANES :].astype(f32)
    left = jnp.where(chip > 0, left, 0.0)
    right = jnp.where(chip < chips - 1, right, 0.0)
    beside = row_halves(
        jnp.concatenate([left, turned(left)], axis=1),
        jnp.concatenate([turned(right), right], axis=1),
    )
    adj_act = own_ref[...] + beside + jnp.concatenate(folded(acc_refs, half), axis=1)
    slope = surrogate(v_ref[...])
    slope = 2.0 * slope * (1.0 - slope)
    return adj_v_ref[...] * (0.9 - 0.1 * g_ref[...]) + adj_act * spikes_ref[moment] * slope


def backward_kernel(moment, *refs):
    adj_g_ref, v_ref, gate_ref, decay_ref, entry_ref = refs[7:12]
    weights = refs[12:16]
    adj_v_out = refs[16]
    adj_volt = receive_part(moment, *refs[:7], refs[24:])
    adj_v_out[...] = adj_volt
    backward_part(
        adj_g_ref[...], adj_volt, v_ref[...], gate_ref[...], decay_ref[...],
        entry_ref, *weights, *refs[17:24],
    )


def last_kernel(*refs):
    refs[8][0] = receive_part(0, *refs[:7], refs[9:])
    refs[8][1] = refs[7][...]


def end_kernel(last_ref, got_ref, *outs):
    me = lax.axis_index("azim")
    core = me & 1
    half = in_group(me)
    for number, out in enumerate(outs):
        keep, got = last_ref[number], got_ref[number]
        keep = jnp.where(half == core, keep, turned(keep))
        got = jnp.where(half == core, turned(got), got)
        out[...] = jnp.where(half == 0, row_halves(keep, got), row_halves(got, keep))


def grad_kernel(*refs):
    sources, fetched, adjs, gathered = (refs[k * STEPS : (k + 1) * STEPS] for k in range(4))
    outs = refs[4 * STEPS :]
    core = lax.axis_index("azim") & 1
    row_tile = tile_rows(WIDE, STEPS * GROUP * 8)
    for role, out in enumerate(outs):
        chosen = row_tile == (core if role == 0 else 1 - core)
        for group in range(adjs[0].shape[0]):
            columns = slice(group * WIDE, (group + 1) * WIDE)
            adj = stacked([ref[group] for ref in adjs])
            adj = jnp.where(chosen, adj.astype(f32), 0.0).astype(bf16)
            for side in range(3):
                source = stacked([ref[side, group] for ref in sources])
                total = product_over(source[:, :SIDE], adj)
                out[side * SIDE : (side + 1) * SIDE, columns] = total.astype(bf16)
        groups = gathered[0].shape[0] // 2
        for group in range(groups):
            at = role * groups + group
            total = product_over(
                stacked([ref[at] for ref in fetched]), stacked([ref[at] for ref in gathered])
            )
            fold, place = divmod(group * WIDE, out.shape[1])
            first = 3 * SIDE + fold * BLK
            out[first : first + BLK, place : place + WIDE] = (total[:BLK] + total[BLK:]).astype(bf16)


def add_kernel(own_ref, got_ref, local_out, long_out):
    total = own_ref[...].astype(f32) + got_ref[...].astype(f32)
    width = own_ref.shape[1]
    local_out[...] = total[: 3 * SIDE].astype(bf16)
    for fold in range(long_out.shape[1] // width):
        first = 3 * SIDE + fold * BLK
        long_out[:, fold * width : (fold + 1) * width] = total[first : first + BLK].astype(bf16)


def call(kernel, outs, args, scratch=(), hbm_args=(), smem_args=(), smem_outs=(), flops=None):
    def spec(space):
        return pl.BlockSpec(memory_space=space)

    vmem, hbm, smem = (spec(space) for space in (pltpu.VMEM, pltpu.HBM, pltpu.SMEM))
    args = [
        pltpu.with_memory_space_constraint(array, pltpu.HBM) if number in hbm_args else array
        for number, array in enumerate(args)
    ]
    return pl.pallas_call(
        kernel,
        out_shape=[
            pltpu.SMEM(shape, dtype) if number in smem_outs else jax.ShapeDtypeStruct(shape, dtype)
            for number, (shape, dtype) in enumerate(outs)
        ],
        in_specs=[
            smem if number in smem_args else hbm if number in hbm_args else vmem
            for number in range(len(args))
        ],
        out_specs=[smem if number in smem_outs else vmem for number in range(len(outs))],
        scratch_shapes=scratch,
        compiler_params=pltpu.CompilerParams(vmem_limit_bytes=24 * 2**20),
        cost_estimate=flops and pl.CostEstimate(flops=flops, bytes_accessed=0, transcendentals=0),
    )(*args)


def local(
    v_init, g_init, spikes, decay, w_local, w_long, lr_src_tile, lr_src_block, lr_tgt_block,
    adj_v_end, adj_g_end,
):
    rows, neurons = v_init.shape
    blocks = neurons // BLK
    tiles = lax.axis_size("azim")
    chips = tiles // 2
    entries = lr_src_tile.shape[0]
    members = [[tile for tile in range(tiles) if in_group(tile) == k] for k in range(2)]
    pair = [(i, i ^ 1) for i in range(tiles)]

    def spread(values):
        return lax.all_to_all(
            values, "azim", split_axis=0, concat_axis=0, tiled=True, axis_index_groups=members
        )

    state = ((rows, neurons), f32)
    fields = (8, 2 * max(entries, LANES))
    source = ((3, blocks // GROUP, GROUP * rows, WIDE), bf16)
    fetched = ((2 * entries // GROUP, GROUP * rows, LANES), bf16)
    block_row = pltpu.VMEM((blocks, rows, LANES), f32)
    sums = [block_row] * ACCS
    back_scratch = [block_row, pltpu.VMEM((CAP, tiles, rows, LANES), f32), *sums]
    back_outs = [
        ((blocks // GROUP, GROUP * rows, WIDE), bf16),
        ((2 * entries // GROUP, GROUP * rows, WIDE), bf16),
        state,
        state,
        ((chips, rows, 2 * LANES + neurons // 2), bf16),
    ]
    w_sides = w_local.reshape(3, SIDE, neurons)
    w_mate = lax.ppermute(w_sides, "azim", pair)
    w_long_mate = lax.ppermute(w_long, "azim", pair)
    held = (
        v_init, spikes, g_init, adj_v_end, adj_g_end, decay,
        lr_src_tile.T, lr_src_block.T, lr_tgt_block.T,
    )
    pack = ((3 + STEPS // 2, rows, neurons), f32)
    keep, send = call(
        start_kernel,
        [pack, pack],
        held,
        [pltpu.VMEM(array.shape, array.dtype) for array in held]
        + [pltpu.SemaphoreType.DMA((len(held),))],
        hbm_args=range(len(held)),
    )
    w_own, w_long = call(
        hold_kernel,
        [(w_sides.shape, bf16), (w_long.shape, bf16)],
        (w_sides, w_long),
        [pltpu.SemaphoreType.DMA((2,))],
        hbm_args=range(2),
    )
    got = lax.ppermute(send, "azim", pair)
    got, w_mate, w_long_mate, w_own, w_long = lax.optimization_barrier(
        (got, w_mate, w_long_mate, w_own, w_long)
    )
    out, v_start, g_start, adj_volt, adj_cond, spikes, decay, entry_list = call(
        merge_kernel,
        [((chips, rows, neurons), bf16)]
        + [state] * 4
        + [((STEPS, rows, neurons), f32), state, (fields, jnp.int32)],
        (keep, got),
        [pltpu.VMEM(fields, jnp.int32), pltpu.SemaphoreType.DMA],
        smem_outs=(7,),
    )
    weights = (w_own, w_mate, w_long, w_long_mate)
    voltages, conducts, gates, sources, fetches = [v_start], [g_start], [], [], []
    for moment in range(STEPS - 1):
        near = spread(out)
        width = neurons + LANES if moment == 0 else neurons
        outs = [state, state, state, source, fetched, ((chips, rows, width), bf16)]
        scratch = list(sums)
        if moment == 0:
            scratch.append(pltpu.VMEM((chips, rows, LANES), f32))
        if moment == 1:
            outs.append(((chips, LANES), jnp.int32))
        voltage, conduct, gate, source_t, fetched_t, out, *asked = call(
            functools.partial(forward_kernel, moment),
            outs,
            (near, entry_list, *weights, voltages[-1], conducts[-1], decay, spikes),
            scratch,
            smem_args=(1,),
        )
        if moment == 1:
            (asked_blocks,) = asked
        voltages.append(voltage)
        conducts.append(conduct)
        gates.append(gate)
        sources.append(source_t)
        fetches.append(fetched_t)
    near = spread(out)
    conduct, wanted, source_t, fetched_t, *back = call(
        turn_kernel,
        [state, ((chips, LANES), jnp.int32), source, fetched] + back_outs,
        (
            near, entry_list, *weights, voltages[-1], conducts[-1], decay, adj_volt, adj_cond,
            asked_blocks,
        ),
        back_scratch + [pltpu.SemaphoreType.DMA],
        smem_args=(1,),
        smem_outs=(1,),
    )
    conducts.append(conduct)
    sources.append(source_t)
    fetches.append(fetched_t)
    adjs, gathers = [], []
    for moment in reversed(range(STEPS)):
        adj_t, gathered_t, adj_cond, own, placed = back
        adjs.insert(0, adj_t)
        gathers.insert(0, gathered_t)
        received = (
            spread(placed), own, wanted, adj_volt, voltages[moment], conducts[moment + 1], spikes,
        )
        if moment > 0:
            adj_volt, *back = call(
                functools.partial(backward_kernel, moment),
                [state] + back_outs,
                received
                + (
                    adj_cond, voltages[moment - 1], gates[moment - 1], decay, entry_list, *weights,
                ),
                back_scratch,
                smem_args=(2, 11),
            )
    grads = ((3 * SIDE + entries * BLK * BLK // neurons, neurons), bf16)
    grads_own, grads_mate = call(
        grad_kernel, [grads, grads], (*sources, *fetches, *adjs, *gathers)
    )
    got_grads = lax.ppermute(grads_mate, "azim", pair)
    (last,) = call(
        last_kernel, [((2, rows, neurons), f32)], (*received, adj_cond), sums, smem_args=(2,)
    )
    got_last = lax.ppermute(last, "azim", pair)
    grad_local, grad_long = call(
        add_kernel,
        [((3 * SIDE, neurons), bf16), ((BLK, entries * BLK), bf16)],
        (grads_own, got_grads),
        flops=10**10,
    )
    got_last, grad_local, grad_long = lax.optimization_barrier((got_last, grad_local, grad_long))
    adj_volt, adj_cond = call(end_kernel, [state, state], (last, got_last))
    return (adj_volt, adj_cond, grad_local.reshape(9, BLK, neurons), grad_long)


def solution(mesh):
    return jax.shard_map(
        local,
        mesh=mesh,
        in_specs=(
            P("groups", "azim"),
            P("groups", "azim"),
            P(None, "groups", "azim"),
            P("groups", "azim"),
            P("groups", None, "azim"),
            P("groups", "azim"),
            P("azim", "groups"),
            P("azim", "groups"),
            P("azim", "groups"),
            P("groups", "azim"),
            P("groups", "azim"),
        ),
        out_specs=(
            P("groups", "azim"),
            P("groups", "azim"),
            P("groups", None, "azim"),
            P("groups", "azim"),
        ),
        check_vma=False,
    )
```

time: 105 us -> 97.3 us (0.927)
  blocking collectives: 30.3 us -> 79.9 us
  waiting for transfers between devices: 28.9 us -> 0.12 us
  starting transfers between devices: 28.7 us -> 2.02 us
  Pallas kernels: 10.2 us -> 14.1 us
  other arithmetic: 3.31 us -> 0 us
  local copies, waits for them, and re-layouts: 1.58 us -> 0 us
    all_to_all x3 -> x8, blocking collectives: 30.3 us -> 79.9 us  [spread(): lax.all_to_all(values, 'azim', split_axis=0, concat_axis=0, tiled=True, a...]
    all_to_all x5 -> x0, starting transfers between devices: 24.6 us -> none  [the longest x4 17.3 us: local(): lax.all_to_all(placed, 'azim', split_axis=0, concat_axis=0, tiled=True)]
    all_to_all x5 -> x0, waiting for transfers between devices: 23.4 us -> none  [the longest x4 19.5 us: local(): lax.all_to_all(placed, 'azim', split_axis=0, concat_axis=0, tiled=True)]
    ppermute x12 -> x5, waiting for transfers between devices: 5.44 us -> 0.12 us  [the longest x1 0.11 us: local(): w_long_mate = lax.ppermute(w_long, 'azim', pair)]
    pallas_call x14, Pallas kernels: 10.2 us -> 14.1 us  [call(): pl.pallas_call(kernel, out_shape=[pltpu.SMEM(shape, dtype) if number in s...]
    ppermute x12 -> x5, starting transfers between devices: 4.13 us -> 2.02 us  [the longest x1 0.7 us: local(): got_grads = lax.ppermute(grads_mate, 'azim', pair)]
    concatenate x2 -> x0, other arithmetic: 1.51 us -> none  [the longest x1 0.81 us: local(): jnp.concatenate([v_init, g_init, spikes.astype(f32).reshape(STEPS * rows,...]
  transfers between devices with their start and end apart: 17 -> 5, of which waited for: 9 -> 1; matrix products, arithmetic and copies ran while one was open for 2% -> 0% of each run, Pallas kernels for 3% -> 4%
where the time goes in v6:
time: 97.3 us; the launch traced here: 96.8 us
  blocking collectives  79.9 us (82%)
  Pallas kernels  14.1 us (14%)
  starting transfers between devices  2.02 us (2%)
    all_to_all x8, blocking collectives, spread(): lax.all_to_all(values, 'azim', split_axis=0, concat_axis=0, tiled=True, a...  79.9 us
    pallas_call x14, Pallas kernels, call(): pl.pallas_call(kernel, out_shape=[pltpu.SMEM(shape, dtype) if number in s...  14.1 us
  transfers between devices with their start and end apart: 5, of which 1 were waited for; matrix products, arithmetic and copies ran while one was open for 0% of the time, Pallas kernels for 4%

profile of v6, /device:TPU:0, one launch (start us, length us, event | category | flops | bytes accessed | tf_op | source)
XLA Modules:
  0.0 96.8 jit_solution(11403467601380861180)
XLA Ops:
  0.6 0.5 collective-permute-start.1
  1.2 1.1 %shard_map.138 = (f32[5,8,1024]{2,1,0:T(8,128)S(1)}, f32[5,8,1024]{2,1,0:T(8,128)S(1)}) custom-call(f32[8,1024]{1,0:T(8,128)} %refs_0_.1, s32[4,8,1024]{2,1,0:T(8,128)} %refs_1_.1, f32[8,1024]{1,0:T(8,128)} %refs_2_.1, f32[8,1024]{1,0:T(8,128)} %refs_3_.1, f32[8,1024]{1,0:T(8,128)} %refs_4_.1, f32[1,1024]{1,0:T(1,128)} %refs_5_.1, s32[1,16]{1,0:T(1,128)} %bitcast.7, ...), custom_call_target="tpu_custom_call" | custom-call | tf_op jit(solution)/shard_map/pallas_call | solution.py:534
  2.3 0.1 collective-permute-start
  2.4 0.5 collective-permute-start.2
  2.9 1.3 %shard_map.139 = (bf16[3,192,1024]{2,1,0:T(8,128)(2,1)S(1)}, bf16[64,1024]{1,0:T(8,128)(2,1)S(1)}) custom-call(bf16[3,192,1024]{2,1,0:T(8,128)(2,1)} %bitcast.6, bf16[64,1024]{1,0:T(8,128)(2,1)} %w_long_ref.1), custom_call_target="tpu_custom_call" | custom-call | tf_op jit(solution)/shard_map/pallas_call | solution.py:534
  4.1 0.1 collective-permute-done.2.refs_5_.refs_15_
  4.3 0.0 collective-permute-done.got_ref
  4.3 0.0 collective-permute-done.1.refs_3_.refs_13_
  4.3 0.7 shard_map.140
  5.0 13.9 %all_to_all.40.refs_0_ = bf16[8,8,1024]{2,1,0:T(8,128)(2,1)S(1)} all-to-all(bf16[8,8,1024]{2,1,0:T(8,128)(2,1)S(1)} %get-tuple-element.81), channel_id=1, replica_groups={{0,3,4,7,8,11,12,15},{1,2,5,6,9,10,13,14},{16,19,20,23,24,27,28,31},{17..., dimensions={0} | all-to-all | bytes 262144 | tf_op jit(solution)/shard_map/all_to_all | solution.py:564
  18.9 0.8 shard_map.141
  19.7 9.6 %all_to_all.41.refs_0_ = bf16[8,8,1152]{2,1,0:T(8,128)(2,1)S(1)} all-to-all(bf16[8,8,1152]{2,1,0:T(8,128)(2,1)S(1)} %get-tuple-element.91), channel_id=1, replica_groups={{0,3,4,7,8,11,12,15},{1,2,5,6,9,10,13,14},{16,19,20,23,24,27,28,31},{17..., dimensions={0} | all-to-all | bytes 294912 | tf_op jit(solution)/shard_map/all_to_all | solution.py:564
  29.2 0.6 shard_map.142
  29.8 9.9 %all_to_all.42.refs_0_ = bf16[8,8,1024]{2,1,0:T(8,128)(2,1)S(1)} all-to-all(bf16[8,8,1024]{2,1,0:T(8,128)(2,1)S(1)} %get-tuple-element.94), channel_id=1, replica_groups={{0,3,4,7,8,11,12,15},{1,2,5,6,9,10,13,14},{16,19,20,23,24,27,28,31},{17..., dimensions={0} | all-to-all | bytes 262144 | tf_op jit(solution)/shard_map/all_to_all | solution.py:564
  39.8 0.6 shard_map.143
  40.4 9.6 %all_to_all.43.refs_0_ = bf16[8,8,1024]{2,1,0:T(8,128)(2,1)S(1)} all-to-all(bf16[8,8,1024]{2,1,0:T(8,128)(2,1)S(1)} %get-tuple-element.97), channel_id=1, replica_groups={{0,3,4,7,8,11,12,15},{1,2,5,6,9,10,13,14},{16,19,20,23,24,27,28,31},{17..., dimensions={0} | all-to-all | bytes 262144 | tf_op jit(solution)/shard_map/all_to_all | solution.py:564
  50.0 1.7 %shard_map.144 = (f32[8,1024]{1,0:T(8,128)S(1)}, s32[8,128]{1,0:T(8,128)S(4)}, bf16[3,4,32,256]{3,2,1,0:T(8,128)(2,1)S(1)}, bf16[8,32,128]{2,1,0:T(8,128)(2,1)S(...) custom-call(bf16[8,8,1024]{2,1,0:T(8,128)(2,1)S(1)} %all_to_all.43.r, ...), custom_call_target="tpu_custom_call" | custom-call | tf_op jit(solution)/shard_map/pallas_call | solution.py:534
  51.7 9.4 %all_to_all.44.refs_0_ = bf16[8,8,768]{2,1,0:T(8,128)(2,1)S(1)} all-to-all(bf16[8,8,768]{2,1,0:T(8,128)(2,1)S(1)} %get-tuple-element.103), channel_id=1, replica_groups={{0,3,4,7,8,11,12,15},{1,2,5,6,9,10,13,14},{16,19,20,23,24,27,28,31},{17..., dimensions={0} | all-to-all | bytes 196608 | tf_op jit(solution)/shard_map/all_to_all | solution.py:564
  61.1 1.4 %shard_map.145 = (f32[8,1024]{1,0:T(8,128)S(1)}, bf16[4,32,256]{2,1,0:T(8,128)(2,1)S(1)}, bf16[8,32,256]{2,1,0:T(8,128)(2,1)S(1)}, f32[8,1024]{1,0:T(8,128)S(1)}...) custom-call(bf16[8,8,768]{2,1,0:T(8,128)(2,1)S(1)} %all_to_all.44.refs_0_, ...), custom_call_target="tpu_custom_call" | custom-call | tf_op jit(solution)/shard_map/pallas_call | solution.py:534
  62.5 9.0 %all_to_all.45.refs_0_ = bf16[8,8,768]{2,1,0:T(8,128)(2,1)S(1)} all-to-all(bf16[8,8,768]{2,1,0:T(8,128)(2,1)S(1)} %get-tuple-element.109), channel_id=1, replica_groups={{0,3,4,7,8,11,12,15},{1,2,5,6,9,10,13,14},{16,19,20,23,24,27,28,31},{17..., dimensions={0} | all-to-all | bytes 196608 | tf_op jit(solution)/shard_map/all_to_all | solution.py:564
  71.5 1.4 %shard_map.146 = (f32[8,1024]{1,0:T(8,128)S(1)}, bf16[4,32,256]{2,1,0:T(8,128)(2,1)S(1)}, bf16[8,32,256]{2,1,0:T(8,128)(2,1)S(1)}, f32[8,1024]{1,0:T(8,128)S(1)}...) custom-call(bf16[8,8,768]{2,1,0:T(8,128)(2,1)S(1)} %all_to_all.45.refs_0_, ...), custom_call_target="tpu_custom_call" | custom-call | tf_op jit(solution)/shard_map/pallas_call | solution.py:534
  72.8 9.0 %all_to_all.46.refs_0_ = bf16[8,8,768]{2,1,0:T(8,128)(2,1)S(1)} all-to-all(bf16[8,8,768]{2,1,0:T(8,128)(2,1)S(1)} %get-tuple-element.114), channel_id=1, replica_groups={{0,3,4,7,8,11,12,15},{1,2,5,6,9,10,13,14},{16,19,20,23,24,27,28,31},{17..., dimensions={0} | all-to-all | bytes 196608 | tf_op jit(solution)/shard_map/all_to_all | solution.py:564
  81.9 1.4 %shard_map.147 = (f32[8,1024]{1,0:T(8,128)S(1)}, bf16[4,32,256]{2,1,0:T(8,128)(2,1)S(1)}, bf16[8,32,256]{2,1,0:T(8,128)(2,1)S(1)}, f32[8,1024]{1,0:T(8,128)S(1)}...) custom-call(bf16[8,8,768]{2,1,0:T(8,128)(2,1)S(1)} %all_to_all.46.refs_0_, ...), custom_call_target="tpu_custom_call" | custom-call | tf_op jit(solution)/shard_map/pallas_call | solution.py:534
  83.2 1.0 shard_map.149
  84.2 0.7 collective-permute-start.4
  84.9 9.5 %all_to_all.47.refs_0_ = bf16[8,8,768]{2,1,0:T(8,128)(2,1)S(1)} all-to-all(bf16[8,8,768]{2,1,0:T(8,128)(2,1)S(1)} %get-tuple-element.119), channel_id=1, replica_groups={{0,3,4,7,8,11,12,15},{1,2,5,6,9,10,13,14},{16,19,20,23,24,27,28,31},{17..., dimensions={0} | all-to-all | bytes 196608 | tf_op jit(solution)/shard_map/all_to_all | solution.py:564
  94.4 0.2 shard_map.148.last_ref
  94.6 0.2 collective-permute-start.3
  94.8 0.0 collective-permute-done.4.got_ref
  94.8 1.4 %shard_map.150 = (bf16[576,1024]{1,0:T(8,128)(2,1)}, bf16[64,1024]{1,0:T(8,128)(2,1)}) custom-call(bf16[640,1024]{1,0:T(8,128)(2,1)S(1)} %get-tuple-element.139.own_ref, bf16[640,1024]{1,0:T(8,128)(2,1)S(1)} %collective-permute-done.4.got_ref), custom_call_target="tpu_custom_call" | custom-call | flops 10000000000 | tf_op jit(solution)/shard_map/pallas_call | solution.py:534
  96.2 0.0 collective-permute-done.3.got_ref
  96.2 0.6 shard_map.151
Async XLA Ops:
  0.6 3.6 %collective-permute-start.1 = (bf16[3,192,1024]{2,1,0:T(8,128)(2,1)}, bf16[3,192,1024]{2,1,0:T(8,128)(2,1)S(1)}, u32[]{:S(2)}, u32[]{:S(2)}) collective-permute-start(bf16[3,192,1024]{2,1,0:T(8,128)(2,1)} %bitcast.5), channel_id=1, source_target_pairs={{0,1},{1,0},{2,3},{3,2},{4,5},{5,4},{6,7},{7,6},{8,9},{9,8},{10,11... | collective-permute-start | bytes 3538952 | tf_op jit(solution)/shard_map/ppermute | solution.py:583
  2.3 2.0 %collective-permute-start = (f32[5,8,1024]{2,1,0:T(8,128)S(1)}, f32[5,8,1024]{2,1,0:T(8,128)S(1)}, u32[]{:S(2)}, u32[]{:S(2)}) collective-permute-start(f32[5,8,1024]{2,1,0:T(8,128)S(1)} %get-tuple-element.77), channel_id=1, source_target_pairs={{0,1},{1,0},{2,3},{3,2},{4,5},{5,4},{6,7},{7,6},{8,9},{9,8},{10,11... | collective-permute-start | bytes 491528 | tf_op jit(solution)/shard_map/ppermute | solution.py:605
  2.4 1.9 %collective-permute-start.2 = (bf16[64,1024]{1,0:T(8,128)(2,1)}, bf16[64,1024]{1,0:T(8,128)(2,1)S(1)}, u32[]{:S(2)}, u32[]{:S(2)}) collective-permute-start(bf16[64,1024]{1,0:T(8,128)(2,1)} %w_long_ref.1), channel_id=1, source_target_pairs={{0,1},{1,0},{2,3},{3,2},{4,5},{5,4},{6,7},{7,6},{8,9},{9,8},{10,11... | collective-permute-start | bytes 393224 | tf_op jit(solution)/shard_map/ppermute | solution.py:584
  84.2 10.6 %collective-permute-start.4 = (bf16[640,1024]{1,0:T(8,128)(2,1)S(1)}, bf16[640,1024]{1,0:T(8,128)(2,1)S(1)}, u32[]{:S(2)}, u32[]{:S(2)}) collective-permute-start(bf16[640,1024]{1,0:T(8,128)(2,1)S(1)} %get-tuple-element.140), channel_id=1, source_target_pairs={{0,1},{1,0},{2,3},{3,2},{4,5},{5,4},{6,7},{7,6},{8,9},{9,8},{10,11... | collective-permute-start | bytes 3932168 | tf_op jit(solution)/shard_map/ppermute | solution.py:681
  94.6 1.6 %collective-permute-start.3 = (f32[2,8,1024]{2,1,0:T(8,128)S(1)}, f32[2,8,1024]{2,1,0:T(8,128)S(1)}, u32[]{:S(2)}, u32[]{:S(2)}) collective-permute-start(f32[2,8,1024]{2,1,0:T(8,128)S(1)} %shard_map.148.last_ref), channel_id=1, source_target_pairs={{0,1},{1,0},{2,3},{3,2},{4,5},{5,4},{6,7},{7,6},{8,9},{9,8},{10,11... | collective-permute-start | bytes 196616 | tf_op jit(solution)/shard_map/ppermute | solution.py:685

commit v7 on v6

--- a/solution.py
+++ b/solution.py
@@ -151,7 +151,7 @@
 
 def merge_kernel(
     keep_ref, got_ref, out_ref, v_out, g_out, adj_v_out, adj_g_out, spikes_out, decay_out,
-    entry_out, fields_ref, sem,
+    fields_ref,
 ):
     core = lax.axis_index("azim") & 1
     rows, neurons = v_out.shape
@@ -166,8 +166,6 @@
             code >> 9, (code >> 8) & 1, code & 15,
         )
         fields_ref[:, columns] = jnp.concatenate(fields, axis=0)
-    copy = pltpu.make_async_copy(fields_ref, entry_out, sem)
-    copy.start()
     merged = []
     for low, high in zip(first[:-1], second[:-1]):
         merged += [row_halves(low, turned(high)), row_halves(turned(low), high)]
@@ -185,7 +183,6 @@
         jnp.broadcast_to(first[-1][0:1, :], (rows, neurons)),
         jnp.broadcast_to(second[-1][0:1, :], (rows, neurons)),
     )
-    copy.wait()
 
 
 def entry_index(entry_ref, role, entry):
@@ -194,7 +191,7 @@
 
 def forward_part(
     near_ref, entry_ref, w_ref, w_mate_ref, w_long_ref, w_long_mate_ref, source_ref, fetched_ref,
-    acc_refs,
+    acc_refs, ready=None,
 ):
     chips, rows, _ = near_ref.shape
     neurons = w_ref.shape[2]
@@ -205,66 +202,78 @@
     core = me & 1
     for ref in acc_refs:
         ref[...] = jnp.zeros_like(ref)
-    groups = fetched_ref.shape[0] // 2
-    row_half = sublane_half(rows, LANES)
-    for role, long_ref in enumerate((w_long_ref, w_long_mate_ref)):
-        own_row = core if role == 0 else 1 - core
-        for group in range(groups):
-            pieces, targets = [], []
-            for entry in range(GROUP * group, GROUP * (group + 1)):
-                at = entry_index(entry_ref, role, entry)
-                lanes = pl.ds(pl.multiple_of(entry_ref[1, at], LANES), LANES)
-                piece = near_ref[entry_ref[0, at], :, lanes].astype(f32)
-                piece = jnp.where(entry_ref[2, at] == own_row, piece, turned(piece))
-                chosen = (row_half == own_row) & (half == entry_ref[3, at])
-                pieces.append(jnp.where(chosen, piece, 0.0))
-                targets.append(entry_ref[4, at])
-            fetched = stacked(pieces).astype(bf16)
-            fetched_ref[role * groups + group] = fetched
-            weights = long_ref[:, group * WIDE : (group + 1) * WIDE]
-            total = product(fetched, stacked([weights, weights]))
-            for at, target in enumerate(targets):
-                lanes = slice(at // 2 * LANES, (at // 2 + 1) * LANES)
-                acc_refs[(at + 2 * group) % len(acc_refs)][target] += total[
-                    at * rows : (at + 1) * rows, lanes
-                ]
-    own = near_ref[chip, :, :neurons].astype(f32)
-    left = near_ref[jnp.maximum(chip - 1, 0), :, :neurons].astype(f32)
-    right = near_ref[jnp.minimum(chip + 1, chips - 1), :, :neurons].astype(f32)
-    left = jnp.where(chip > 0, turned(left), 0.0)
-    right = jnp.where(chip < chips - 1, turned(right), 0.0)
-    sides = (row_halves(left, turned(own)), own, row_halves(turned(own), right))
-    for side, values in enumerate(sides):
-        even = chunks_of(values)
-        odd = odd_chunks(even, half)
-        even = even + [jnp.zeros((rows, LANES), f32)]
+    def local_part():
+        own = near_ref[chip, :, :neurons].astype(f32)
+        left = near_ref[jnp.maximum(chip - 1, 0), :, :neurons].astype(f32)
+        right = near_ref[jnp.minimum(chip + 1, chips - 1), :, :neurons].astype(f32)
+        left = jnp.where(chip > 0, turned(left), 0.0)
+        right = jnp.where(chip < chips - 1, turned(right), 0.0)
+        sides = (row_halves(left, turned(own)), own, row_halves(turned(own), right))
+        for side, values in enumerate(sides):
+            even = chunks_of(values)
+            odd = odd_chunks(even, half)
+            even = even + [jnp.zeros((rows, LANES), f32)]
+            for group in range(blocks // GROUP):
+                pieces = []
+                for block in range(GROUP * group, GROUP * (group + 1)):
+                    line = even if block % 2 else odd
+                    pieces.append((line[block // 2], line[block // 2 + 1]))
+                source_ref[side, group] = jnp.concatenate(
+                    [stacked([piece[k] for piece in pieces]) for k in range(2)], axis=1
+                ).astype(bf16)
+        own_rows = tile_rows(WIDE) == core
+        drive = []
         for group in range(blocks // GROUP):
-            pieces = []
-            for block in range(GROUP * group, GROUP * (group + 1)):
-                line = even if block % 2 else odd
-                pieces.append((line[block // 2], line[block // 2 + 1]))
-            source_ref[side, group] = jnp.concatenate(
-                [stacked([piece[k] for piece in pieces]) for k in range(2)], axis=1
-            ).astype(bf16)
-    own_rows = tile_rows(WIDE) == core
-    drive = []
-    for group in range(blocks // GROUP):
-        columns = slice(group * WIDE, (group + 1) * WIDE)
-        totals = []
-        for ref in (w_ref, w_mate_ref):
-            total = product(source_ref[0, group][:, :SIDE], ref[0, :, columns])
-            for side in range(1, 3):
-                total = total + product(source_ref[side, group][:, :SIDE], ref[side, :, columns])
-            totals.append(total)
-        total = jnp.where(own_rows, *totals)
-        for pair in range(GROUP // 2):
-            lanes = slice(pair * LANES, (pair + 1) * LANES)
-            at = 2 * pair * rows
-            drive.append(
-                half_pair(
-                    total[at : at + rows, lanes], total[at + rows : at + 2 * rows, lanes], half
+            columns = slice(group * WIDE, (group + 1) * WIDE)
+            totals = []
+            for ref in (w_ref, w_mate_ref):
+                total = product(source_ref[0, group][:, :SIDE], ref[0, :, columns])
+                for side in range(1, 3):
+                    total = total + product(source_ref[side, group][:, :SIDE], ref[side, :, columns])
+                totals.append(total)
+            total = jnp.where(own_rows, *totals)
+            for pair in range(GROUP // 2):
+                lanes = slice(pair * LANES, (pair + 1) * LANES)
+                at = 2 * pair * rows
+                drive.append(
+                    half_pair(
+                        total[at : at + rows, lanes], total[at + rows : at + 2 * rows, lanes], half
+                    )
                 )
-            )
+        return drive
+
+    def long_part():
+        groups = fetched_ref.shape[0] // 2
+        row_half = sublane_half(rows, LANES)
+        for role, long_ref in enumerate((w_long_ref, w_long_mate_ref)):
+            own_row = core if role == 0 else 1 - core
+            for group in range(groups):
+                pieces, targets = [], []
+                for entry in range(GROUP * group, GROUP * (group + 1)):
+                    at = entry_index(entry_ref, role, entry)
+                    lanes = pl.ds(pl.multiple_of(entry_ref[1, at], LANES), LANES)
+                    piece = near_ref[entry_ref[0, at], :, lanes].astype(f32)
+                    piece = jnp.where(entry_ref[2, at] == own_row, piece, turned(piece))
+                    chosen = (row_half == own_row) & (half == entry_ref[3, at])
+                    pieces.append(jnp.where(chosen, piece, 0.0))
+                    targets.append(entry_ref[4, at])
+                fetched = stacked(pieces).astype(bf16)
+                fetched_ref[role * groups + group] = fetched
+                weights = long_ref[:, group * WIDE : (group + 1) * WIDE]
+                total = product(fetched, stacked([weights, weights]))
+                for at, target in enumerate(targets):
+                    lanes = slice(at // 2 * LANES, (at // 2 + 1) * LANES)
+                    acc_refs[(at + 2 * group) % len(acc_refs)][target] += total[
+                        at * rows : (at + 1) * rows, lanes
+                    ]
+
+    if ready is None:
+        long_part()
+        drive = local_part()
+    else:
+        drive = local_part()
+        ready.wait()
+        long_part()
     extra = folded(acc_refs, half)
     return jnp.concatenate([a + b for a, b in zip(drive, extra)], axis=1)
 
@@ -273,7 +282,12 @@
     near_ref, entry_ref, w_ref, w_mate_ref, w_long_ref, w_long_mate_ref = refs[:6]
     v_ref, g_ref, decay_ref, spikes_ref = refs[6:10]
     v_out, g_out, gate_out, source_ref, fetched_ref, act_ref = refs[10:16]
-    acc_refs = refs[16 : 16 + ACCS] if moment != 1 else refs[17 : 17 + ACCS]
+    acc_refs = refs[16 : 16 + ACCS] if moment == 2 else refs[17 : 17 + ACCS]
+    ready = None
+    if moment == 0:
+        ready = pltpu.make_async_copy(entry_ref, refs[16], refs[-1])
+        ready.start()
+        entry_ref = refs[16]
     chips = act_ref.shape[0]
     rows, neurons = v_ref.shape
     if moment == 1:
@@ -283,7 +297,7 @@
             asked_ref[chip : chip + 1, :] = asked[0:1, :].astype(jnp.int32)
     drive = forward_part(
         near_ref, entry_ref, w_ref, w_mate_ref, w_long_ref, w_long_mate_ref, source_ref,
-        fetched_ref, acc_refs,
+        fetched_ref, acc_refs, ready,
     )
     voltage = v_ref[...]
     conduct = decay_ref[...] * g_ref[...] + jax.nn.softplus(drive)
@@ -295,7 +309,7 @@
     for chip in range(chips):
         act_ref[chip, :, :neurons] = activity
     if moment == 0:
-        ask_ref = refs[-1]
+        ask_ref = refs[-2]
         core = lax.axis_index("azim") & 1
         lane = lax.broadcasted_iota(jnp.int32, (rows, LANES), 1)
         ask_ref[...] = jnp.zeros_like(ask_ref)
@@ -379,14 +393,13 @@
             gathered = jnp.concatenate([stacked(left), stacked(right)], axis=1).astype(bf16)
             gathered_ref[role * groups + group] = gathered
             weights = long_ref[:, group * WIDE : (group + 1) * WIDE]
-            back = product_back(gathered, stacked([weights, weights]))
-            for at, slot in enumerate(slots):
-                slot_ref[slot] += back[at * rows : (at + 1) * rows]
+            back = product_back(gathered, weights)
+            for at, (rank, tile) in enumerate(slots):
+                slot_ref[role, rank, tile] = back[at * rows : (at + 1) * rows]
     for tile in range(2 * chips):
         lanes = slice(tile % 2 * LANES, (tile % 2 + 1) * LANES)
-        placed_out[tile // 2, :, lanes] = half_pair(
-            slot_ref[0, tile], slot_ref[1, tile], half
-        ).astype(bf16)
+        parts = [slot_ref[0, rank, tile] + slot_ref[1, rank, tile] for rank in range(CAP)]
+        placed_out[tile // 2, :, lanes] = jnp.concatenate(parts, axis=1).astype(bf16)
     for group in range(blocks // GROUP):
         left = stacked([half_only(chunks[2 * group], half, k) for k in range(2)] + [zero, zero])
         right = stacked(
@@ -501,7 +514,7 @@
             for side in range(3):
                 source = stacked([ref[side, group] for ref in sources])
                 total = product_over(source[:, :SIDE], adj)
-                out[side * SIDE : (side + 1) * SIDE, columns] = total.astype(bf16)
+                out[side * SIDE : (side + 1) * SIDE, columns] = total.astype(out.dtype)
         groups = gathered[0].shape[0] // 2
         for group in range(groups):
             at = role * groups + group
@@ -510,11 +523,13 @@
             )
             fold, place = divmod(group * WIDE, out.shape[1])
             first = 3 * SIDE + fold * BLK
-            out[first : first + BLK, place : place + WIDE] = (total[:BLK] + total[BLK:]).astype(bf16)
+            out[first : first + BLK, place : place + WIDE] = (total[:BLK] + total[BLK:]).astype(
+                out.dtype
+            )
 
 
 def add_kernel(own_ref, got_ref, local_out, long_out):
-    total = own_ref[...].astype(f32) + got_ref[...].astype(f32)
+    total = own_ref[...] + got_ref[...].astype(f32)
     width = own_ref.shape[1]
     local_out[...] = total[: 3 * SIDE].astype(bf16)
     for fold in range(long_out.shape[1] // width):
@@ -571,7 +586,7 @@
     fetched = ((2 * entries // GROUP, GROUP * rows, LANES), bf16)
     block_row = pltpu.VMEM((blocks, rows, LANES), f32)
     sums = [block_row] * ACCS
-    back_scratch = [block_row, pltpu.VMEM((CAP, tiles, rows, LANES), f32), *sums]
+    back_scratch = [block_row, pltpu.VMEM((2, CAP, tiles, rows, BLK), f32), *sums]
     back_outs = [
         ((blocks // GROUP, GROUP * rows, WIDE), bf16),
         ((2 * entries // GROUP, GROUP * rows, WIDE), bf16),
@@ -606,14 +621,12 @@
     got, w_mate, w_long_mate, w_own, w_long = lax.optimization_barrier(
         (got, w_mate, w_long_mate, w_own, w_long)
     )
-    out, v_start, g_start, adj_volt, adj_cond, spikes, decay, entry_list = call(
+    out, v_start, g_start, adj_volt, adj_cond, spikes, decay, entry_rows = call(
         merge_kernel,
         [((chips, rows, neurons), bf16)]
         + [state] * 4
         + [((STEPS, rows, neurons), f32), state, (fields, jnp.int32)],
         (keep, got),
-        [pltpu.VMEM(fields, jnp.int32), pltpu.SemaphoreType.DMA],
-        smem_outs=(7,),
     )
     weights = (w_own, w_mate, w_long, w_long_mate)
     voltages, conducts, gates, sources, fetches = [v_start], [g_start], [], [], []
@@ -623,16 +636,23 @@
         outs = [state, state, state, source, fetched, ((chips, rows, width), bf16)]
         scratch = list(sums)
         if moment == 0:
-            scratch.append(pltpu.VMEM((chips, rows, LANES), f32))
+            outs.append((fields, jnp.int32))
+            scratch += [pltpu.VMEM((chips, rows, LANES), f32), pltpu.SemaphoreType.DMA]
         if moment == 1:
             outs.append(((chips, LANES), jnp.int32))
         voltage, conduct, gate, source_t, fetched_t, out, *asked = call(
             functools.partial(forward_kernel, moment),
             outs,
-            (near, entry_list, *weights, voltages[-1], conducts[-1], decay, spikes),
+            (
+                near, entry_rows if moment == 0 else entry_list, *weights, voltages[-1],
+                conducts[-1], decay, spikes,
+            ),
             scratch,
-            smem_args=(1,),
+            smem_args=(1,) if moment else (),
+            smem_outs=() if moment else (6,),
         )
+        if moment == 0:
+            (entry_list,) = asked
         if moment == 1:
             (asked_blocks,) = asked
         voltages.append(voltage)
@@ -674,9 +694,9 @@
                 back_scratch,
                 smem_args=(2, 11),
             )
-    grads = ((3 * SIDE + entries * BLK * BLK // neurons, neurons), bf16)
+    grads = (3 * SIDE + entries * BLK * BLK // neurons, neurons)
     grads_own, grads_mate = call(
-        grad_kernel, [grads, grads], (*sources, *fetches, *adjs, *gathers)
+        grad_kernel, [(grads, f32), (grads, bf16)], (*sources, *fetches, *adjs, *gathers)
     )
     got_grads = lax.ppermute(grads_mate, "azim", pair)
     (last,) = call(

time: 97.3 us -> 96.8 us (level)
  no operation moved by 1% of the time
where the time goes in v7:
time: 96.8 us; the launch traced here: 96.4 us
  blocking collectives  79.9 us (83%)
  Pallas kernels  13.6 us (14%)
  starting transfers between devices  2.03 us (2%)
    all_to_all x8, blocking collectives, spread(): lax.all_to_all(values, 'azim', split_axis=0, concat_axis=0, tiled=True, a...  79.9 us
    pallas_call x14, Pallas kernels, call(): pl.pallas_call(kernel, out_shape=[pltpu.SMEM(shape, dtype) if number in s...  13.6 us
  transfers between devices with their start and end apart: 5, of which 1 were waited for; matrix products, arithmetic and copies ran while one was open for 0% of the time, Pallas kernels for 4%

profile of v7, /device:TPU:0, one launch (start us, length us, event | category | flops | bytes accessed | tf_op | source)
XLA Modules:
  0.0 96.4 jit_solution(4069089729742032327)
XLA Ops:
  0.6 0.5 collective-permute-start.1
  1.2 1.1 %shard_map.138 = (f32[5,8,1024]{2,1,0:T(8,128)S(1)}, f32[5,8,1024]{2,1,0:T(8,128)S(1)}) custom-call(f32[8,1024]{1,0:T(8,128)} %refs_0_.1, s32[4,8,1024]{2,1,0:T(8,128)} %refs_1_.1, f32[8,1024]{1,0:T(8,128)} %refs_2_.1, f32[8,1024]{1,0:T(8,128)} %refs_3_.1, f32[8,1024]{1,0:T(8,128)} %refs_4_.1, f32[1,1024]{1,0:T(1,128)} %refs_5_.1, s32[1,16]{1,0:T(1,128)} %bitcast.7, ...), custom_call_target="tpu_custom_call" | custom-call | tf_op jit(solution)/shard_map/pallas_call | solution.py:549
  2.3 0.1 collective-permute-start
  2.4 0.5 collective-permute-start.2
  2.9 1.3 %shard_map.139 = (bf16[3,192,1024]{2,1,0:T(8,128)(2,1)S(1)}, bf16[64,1024]{1,0:T(8,128)(2,1)S(1)}) custom-call(bf16[3,192,1024]{2,1,0:T(8,128)(2,1)} %bitcast.6, bf16[64,1024]{1,0:T(8,128)(2,1)} %w_long_ref.1), custom_call_target="tpu_custom_call" | custom-call | tf_op jit(solution)/shard_map/pallas_call | solution.py:549
  4.1 0.1 collective-permute-done.2.refs_5_.refs_15_
  4.3 0.0 collective-permute-done.got_ref
  4.3 0.0 collective-permute-done.1.refs_3_.refs_13_
  4.3 0.1 shard_map.140
  4.3 13.9 %all_to_all.40.refs_0_ = bf16[8,8,1024]{2,1,0:T(8,128)(2,1)S(1)} all-to-all(bf16[8,8,1024]{2,1,0:T(8,128)(2,1)S(1)} %get-tuple-element.82), channel_id=1, replica_groups={{0,3,4,7,8,11,12,15},{1,2,5,6,9,10,13,14},{16,19,20,23,24,27,28,31},{17..., dimensions={0} | all-to-all | bytes 262144 | tf_op jit(solution)/shard_map/all_to_all | solution.py:579
  18.3 1.2 %shard_map.141 = (f32[8,1024]{1,0:T(8,128)S(1)}, f32[8,1024]{1,0:T(8,128)S(1)}, f32[8,1024]{1,0:T(8,128)S(1)}, bf16[3,4,32,256]{3,2,1,0:T(8,128)(2,1)S(1)}, bf16...) custom-call(bf16[8,8,1024]{2,1,0:T(8,128)(2,1)S(1)} %all_to_all.40.refs_0_, ...), custom_call_target="tpu_custom_call" | custom-call | tf_op jit(solution)/shard_map/pallas_call | solution.py:549
  19.5 9.6 %all_to_all.41.refs_0_ = bf16[8,8,1152]{2,1,0:T(8,128)(2,1)S(1)} all-to-all(bf16[8,8,1152]{2,1,0:T(8,128)(2,1)S(1)} %get-tuple-element.92), channel_id=1, replica_groups={{0,3,4,7,8,11,12,15},{1,2,5,6,9,10,13,14},{16,19,20,23,24,27,28,31},{17..., dimensions={0} | all-to-all | bytes 294912 | tf_op jit(solution)/shard_map/all_to_all | solution.py:579
  29.0 0.6 shard_map.142
  29.6 9.9 %all_to_all.42.refs_0_ = bf16[8,8,1024]{2,1,0:T(8,128)(2,1)S(1)} all-to-all(bf16[8,8,1024]{2,1,0:T(8,128)(2,1)S(1)} %get-tuple-element.96), channel_id=1, replica_groups={{0,3,4,7,8,11,12,15},{1,2,5,6,9,10,13,14},{16,19,20,23,24,27,28,31},{17..., dimensions={0} | all-to-all | bytes 262144 | tf_op jit(solution)/shard_map/all_to_all | solution.py:579
  39.6 0.6 shard_map.143
  40.2 9.6 %all_to_all.43.refs_0_ = bf16[8,8,1024]{2,1,0:T(8,128)(2,1)S(1)} all-to-all(bf16[8,8,1024]{2,1,0:T(8,128)(2,1)S(1)} %get-tuple-element.99), channel_id=1, replica_groups={{0,3,4,7,8,11,12,15},{1,2,5,6,9,10,13,14},{16,19,20,23,24,27,28,31},{17..., dimensions={0} | all-to-all | bytes 262144 | tf_op jit(solution)/shard_map/all_to_all | solution.py:579
  49.8 1.7 %shard_map.144 = (f32[8,1024]{1,0:T(8,128)S(1)}, s32[8,128]{1,0:T(8,128)S(4)}, bf16[3,4,32,256]{3,2,1,0:T(8,128)(2,1)S(1)}, bf16[8,32,128]{2,1,0:T(8,128)(2,1)S(...) custom-call(bf16[8,8,1024]{2,1,0:T(8,128)(2,1)S(1)} %all_to_all.43.r, ...), custom_call_target="tpu_custom_call" | custom-call | tf_op jit(solution)/shard_map/pallas_call | solution.py:549
  51.5 9.4 %all_to_all.44.refs_0_ = bf16[8,8,768]{2,1,0:T(8,128)(2,1)S(1)} all-to-all(bf16[8,8,768]{2,1,0:T(8,128)(2,1)S(1)} %get-tuple-element.105), channel_id=1, replica_groups={{0,3,4,7,8,11,12,15},{1,2,5,6,9,10,13,14},{16,19,20,23,24,27,28,31},{17..., dimensions={0} | all-to-all | bytes 196608 | tf_op jit(solution)/shard_map/all_to_all | solution.py:579
  60.9 1.3 %shard_map.145 = (f32[8,1024]{1,0:T(8,128)S(1)}, bf16[4,32,256]{2,1,0:T(8,128)(2,1)S(1)}, bf16[8,32,256]{2,1,0:T(8,128)(2,1)S(1)}, f32[8,1024]{1,0:T(8,128)S(1)}...) custom-call(bf16[8,8,768]{2,1,0:T(8,128)(2,1)S(1)} %all_to_all.44.refs_0_, ...), custom_call_target="tpu_custom_call" | custom-call | tf_op jit(solution)/shard_map/pallas_call | solution.py:549
  62.2 9.0 %all_to_all.45.refs_0_ = bf16[8,8,768]{2,1,0:T(8,128)(2,1)S(1)} all-to-all(bf16[8,8,768]{2,1,0:T(8,128)(2,1)S(1)} %get-tuple-element.111), channel_id=1, replica_groups={{0,3,4,7,8,11,12,15},{1,2,5,6,9,10,13,14},{16,19,20,23,24,27,28,31},{17..., dimensions={0} | all-to-all | bytes 196608 | tf_op jit(solution)/shard_map/all_to_all | solution.py:579
  71.2 1.3 %shard_map.146 = (f32[8,1024]{1,0:T(8,128)S(1)}, bf16[4,32,256]{2,1,0:T(8,128)(2,1)S(1)}, bf16[8,32,256]{2,1,0:T(8,128)(2,1)S(1)}, f32[8,1024]{1,0:T(8,128)S(1)}...) custom-call(bf16[8,8,768]{2,1,0:T(8,128)(2,1)S(1)} %all_to_all.45.refs_0_, ...), custom_call_target="tpu_custom_call" | custom-call | tf_op jit(solution)/shard_map/pallas_call | solution.py:549
  72.5 9.0 %all_to_all.46.refs_0_ = bf16[8,8,768]{2,1,0:T(8,128)(2,1)S(1)} all-to-all(bf16[8,8,768]{2,1,0:T(8,128)(2,1)S(1)} %get-tuple-element.116), channel_id=1, replica_groups={{0,3,4,7,8,11,12,15},{1,2,5,6,9,10,13,14},{16,19,20,23,24,27,28,31},{17..., dimensions={0} | all-to-all | bytes 196608 | tf_op jit(solution)/shard_map/all_to_all | solution.py:579
  81.5 1.3 %shard_map.147 = (f32[8,1024]{1,0:T(8,128)S(1)}, bf16[4,32,256]{2,1,0:T(8,128)(2,1)S(1)}, bf16[8,32,256]{2,1,0:T(8,128)(2,1)S(1)}, f32[8,1024]{1,0:T(8,128)S(1)}...) custom-call(bf16[8,8,768]{2,1,0:T(8,128)(2,1)S(1)} %all_to_all.46.refs_0_, ...), custom_call_target="tpu_custom_call" | custom-call | tf_op jit(solution)/shard_map/pallas_call | solution.py:549
  82.8 1.0 shard_map.149
  83.8 0.7 collective-permute-start.4
  84.5 9.5 %all_to_all.47.refs_0_ = bf16[8,8,768]{2,1,0:T(8,128)(2,1)S(1)} all-to-all(bf16[8,8,768]{2,1,0:T(8,128)(2,1)S(1)} %get-tuple-element.121), channel_id=1, replica_groups={{0,3,4,7,8,11,12,15},{1,2,5,6,9,10,13,14},{16,19,20,23,24,27,28,31},{17..., dimensions={0} | all-to-all | bytes 196608 | tf_op jit(solution)/shard_map/all_to_all | solution.py:579
  94.0 0.2 shard_map.148.last_ref
  94.2 0.2 collective-permute-start.3
  94.4 0.0 collective-permute-done.4.got_ref
  94.4 1.3 %shard_map.150 = (bf16[576,1024]{1,0:T(8,128)(2,1)}, bf16[64,1024]{1,0:T(8,128)(2,1)}) custom-call(f32[640,1024]{1,0:T(8,128)S(1)} %get-tuple-element.141.own_ref, bf16[640,1024]{1,0:T(8,128)(2,1)S(1)} %collective-permute-done.4.got_ref), custom_call_target="tpu_custom_call" | custom-call | flops 10000000000 | tf_op jit(solution)/shard_map/pallas_call | solution.py:549
  95.7 0.0 collective-permute-done.3.got_ref
  95.7 0.6 shard_map.151
Async XLA Ops:
  0.6 3.6 %collective-permute-start.1 = (bf16[3,192,1024]{2,1,0:T(8,128)(2,1)}, bf16[3,192,1024]{2,1,0:T(8,128)(2,1)S(1)}, u32[]{:S(2)}, u32[]{:S(2)}) collective-permute-start(bf16[3,192,1024]{2,1,0:T(8,128)(2,1)} %bitcast.5), channel_id=1, source_target_pairs={{0,1},{1,0},{2,3},{3,2},{4,5},{5,4},{6,7},{7,6},{8,9},{9,8},{10,11... | collective-permute-start | bytes 3538952 | tf_op jit(solution)/shard_map/ppermute | solution.py:598
  2.3 2.0 %collective-permute-start = (f32[5,8,1024]{2,1,0:T(8,128)S(1)}, f32[5,8,1024]{2,1,0:T(8,128)S(1)}, u32[]{:S(2)}, u32[]{:S(2)}) collective-permute-start(f32[5,8,1024]{2,1,0:T(8,128)S(1)} %get-tuple-element.78), channel_id=1, source_target_pairs={{0,1},{1,0},{2,3},{3,2},{4,5},{5,4},{6,7},{7,6},{8,9},{9,8},{10,11... | collective-permute-start | bytes 491528 | tf_op jit(solution)/shard_map/ppermute | solution.py:620
  2.4 1.9 %collective-permute-start.2 = (bf16[64,1024]{1,0:T(8,128)(2,1)}, bf16[64,1024]{1,0:T(8,128)(2,1)S(1)}, u32[]{:S(2)}, u32[]{:S(2)}) collective-permute-start(bf16[64,1024]{1,0:T(8,128)(2,1)} %w_long_ref.1), channel_id=1, source_target_pairs={{0,1},{1,0},{2,3},{3,2},{4,5},{5,4},{6,7},{7,6},{8,9},{9,8},{10,11... | collective-permute-start | bytes 393224 | tf_op jit(solution)/shard_map/ppermute | solution.py:599
  83.8 10.7 %collective-permute-start.4 = (bf16[640,1024]{1,0:T(8,128)(2,1)S(1)}, bf16[640,1024]{1,0:T(8,128)(2,1)S(1)}, u32[]{:S(2)}, u32[]{:S(2)}) collective-permute-start(bf16[640,1024]{1,0:T(8,128)(2,1)S(1)} %get-tuple-element.142), channel_id=1, source_target_pairs={{0,1},{1,0},{2,3},{3,2},{4,5},{5,4},{6,7},{7,6},{8,9},{9,8},{10,11... | collective-permute-start | bytes 3932168 | tf_op jit(solution)/shard_map/ppermute | solution.py:701
  94.2 1.5 %collective-permute-start.3 = (f32[2,8,1024]{2,1,0:T(8,128)S(1)}, f32[2,8,1024]{2,1,0:T(8,128)S(1)}, u32[]{:S(2)}, u32[]{:S(2)}) collective-permute-start(f32[2,8,1024]{2,1,0:T(8,128)S(1)} %shard_map.148.last_ref), channel_id=1, source_target_pairs={{0,1},{1,0},{2,3},{3,2},{4,5},{5,4},{6,7},{7,6},{8,9},{9,8},{10,11... | collective-permute-start | bytes 196616 | tf_op jit(solution)/shard_map/ppermute | solution.py:705

commit v8 on v7

--- a/solution.py
+++ b/solution.py
@@ -150,22 +150,22 @@
 
 
 def merge_kernel(
-    keep_ref, got_ref, out_ref, v_out, g_out, adj_v_out, adj_g_out, spikes_out, decay_out,
+    entries, keep_ref, got_ref, out_ref, v_out, g_out, adj_v_out, adj_g_out, spikes_out, decay_out,
     fields_ref,
 ):
     core = lax.axis_index("azim") & 1
     rows, neurons = v_out.shape
     first = [jnp.where(core == 0, keep_ref[k], got_ref[k]) for k in range(keep_ref.shape[0])]
     second = [jnp.where(core == 0, got_ref[k], keep_ref[k]) for k in range(keep_ref.shape[0])]
-    lanes = fields_ref.shape[1] // 2
-    for at, block in enumerate((keep_ref[len(first) - 1], got_ref[len(first) - 1])):
-        code = block[1:2, :lanes].astype(jnp.int32)
-        columns = slice(at * lanes, (at + 1) * lanes)
-        fields = (
-            code >> 10, ((code & 15) >> 1) * LANES, (code >> 9) & 1, code & 1, (code >> 4) & 15,
-            code >> 9, (code >> 8) & 1, code & 15,
-        )
-        fields_ref[:, columns] = jnp.concatenate(fields, axis=0)
+    lanes = fields_ref.shape[1]
+    ours, mates = (ref[len(first) - 1][1:2, :lanes] for ref in (keep_ref, got_ref))
+    lane = lax.broadcasted_iota(jnp.int32, (1, lanes), 1)
+    code = jnp.where(lane < entries, ours, pltpu.roll(mates, entries, 1)).astype(jnp.int32)
+    fields = (
+        code >> 10, ((code & 15) >> 1) * LANES, (code >> 9) & 1, code & 1, (code >> 4) & 15,
+        code >> 9, (code >> 8) & 1, code & 15,
+    )
+    fields_ref[...] = jnp.concatenate(fields, axis=0)
     merged = []
     for low, high in zip(first[:-1], second[:-1]):
         merged += [row_halves(low, turned(high)), row_halves(turned(low), high)]
@@ -183,10 +183,6 @@
         jnp.broadcast_to(first[-1][0:1, :], (rows, neurons)),
         jnp.broadcast_to(second[-1][0:1, :], (rows, neurons)),
     )
-
-
-def entry_index(entry_ref, role, entry):
-    return role * (entry_ref.shape[1] // 2) + entry
 
 
 def forward_part(
@@ -250,7 +246,7 @@
             for group in range(groups):
                 pieces, targets = [], []
                 for entry in range(GROUP * group, GROUP * (group + 1)):
-                    at = entry_index(entry_ref, role, entry)
+                    at = role * groups * GROUP + entry
                     lanes = pl.ds(pl.multiple_of(entry_ref[1, at], LANES), LANES)
                     piece = near_ref[entry_ref[0, at], :, lanes].astype(f32)
                     piece = jnp.where(entry_ref[2, at] == own_row, piece, turned(piece))
@@ -316,7 +312,7 @@
         for role in range(2):
             own_row = core if role == 0 else 1 - core
             for entry in range(fetched_ref.shape[0] // 2 * GROUP):
-                at = entry_index(entry_ref, role, entry)
+                at = role * (fetched_ref.shape[0] // 2 * GROUP) + entry
                 place = own_row * 4 + entry_ref[2, at] * CAP + entry_ref[6, at]
                 chip = entry_ref[0, at]
                 ask_ref[chip] = jnp.where(
@@ -359,6 +355,7 @@
 def backward_part(
     adj_cond, adj_volt, voltage, gate, decay, entry_ref, w_ref, w_mate_ref, w_long_ref,
     w_long_mate_ref, adj_ref, gathered_ref, cond_out, own_out, placed_out, block_ref, slot_ref,
+    long_first,
 ):
     rows, neurons = voltage.shape
     blocks = neurons // BLK
@@ -376,49 +373,55 @@
         moved = swapped(piece)
         block_ref[2 * number] = half_pair(piece, moved, half)
         block_ref[2 * number + 1] = half_pair(moved, piece, half)
-    slot_ref[...] = jnp.zeros_like(slot_ref)
-    groups = gathered_ref.shape[0] // 2
-    row_half = sublane_half(rows, LANES)
-    for role, long_ref in enumerate((w_long_ref, w_long_mate_ref)):
-        own_row = core if role == 0 else 1 - core
-        for group in range(groups):
-            left, right, slots = [], [], []
-            for at in range(GROUP):
-                entry = entry_index(entry_ref, role, GROUP * group + at)
-                slots.append((entry_ref[6, entry], entry_ref[5, entry]))
-                chosen = (row_half == own_row) & (half == at % 2)
-                piece = jnp.where(chosen, block_ref[entry_ref[4, entry]], 0.0)
-                left.append(piece if at < 2 else zero)
-                right.append(zero if at < 2 else piece)
-            gathered = jnp.concatenate([stacked(left), stacked(right)], axis=1).astype(bf16)
-            gathered_ref[role * groups + group] = gathered
-            weights = long_ref[:, group * WIDE : (group + 1) * WIDE]
-            back = product_back(gathered, weights)
-            for at, (rank, tile) in enumerate(slots):
-                slot_ref[role, rank, tile] = back[at * rows : (at + 1) * rows]
-    for tile in range(2 * chips):
-        lanes = slice(tile % 2 * LANES, (tile % 2 + 1) * LANES)
-        parts = [slot_ref[0, rank, tile] + slot_ref[1, rank, tile] for rank in range(CAP)]
-        placed_out[tile // 2, :, lanes] = jnp.concatenate(parts, axis=1).astype(bf16)
-    for group in range(blocks // GROUP):
-        left = stacked([half_only(chunks[2 * group], half, k) for k in range(2)] + [zero, zero])
-        right = stacked(
-            [zero, zero] + [half_only(chunks[2 * group + 1], half, k) for k in range(2)]
+    def long_part():
+        slot_ref[...] = jnp.zeros_like(slot_ref)
+        groups = gathered_ref.shape[0] // 2
+        row_half = sublane_half(rows, LANES)
+        for role, long_ref in enumerate((w_long_ref, w_long_mate_ref)):
+            own_row = core if role == 0 else 1 - core
+            for group in range(groups):
+                left, right, slots = [], [], []
+                for at in range(GROUP):
+                    entry = GROUP * (role * groups + group) + at
+                    slots.append((entry_ref[6, entry], entry_ref[5, entry]))
+                    chosen = (row_half == own_row) & (half == at % 2)
+                    piece = jnp.where(chosen, block_ref[entry_ref[4, entry]], 0.0)
+                    left.append(piece if at < 2 else zero)
+                    right.append(zero if at < 2 else piece)
+                gathered = jnp.concatenate([stacked(left), stacked(right)], axis=1).astype(bf16)
+                gathered_ref[role * groups + group] = gathered
+                weights = long_ref[:, group * WIDE : (group + 1) * WIDE]
+                back = product_back(gathered, weights)
+                for at, (rank, tile) in enumerate(slots):
+                    slot_ref[role, rank, tile] = back[at * rows : (at + 1) * rows]
+        for tile in range(2 * chips):
+            lanes = slice(tile % 2 * LANES, (tile % 2 + 1) * LANES)
+            parts = [slot_ref[0, rank, tile] + slot_ref[1, rank, tile] for rank in range(CAP)]
+            placed_out[tile // 2, :, lanes] = jnp.concatenate(parts, axis=1).astype(bf16)
+
+    def local_part():
+        for group in range(blocks // GROUP):
+            left = stacked([half_only(chunks[2 * group], half, k) for k in range(2)] + [zero, zero])
+            right = stacked(
+                [zero, zero] + [half_only(chunks[2 * group + 1], half, k) for k in range(2)]
+            )
+            adj_ref[group] = jnp.concatenate([left, right], axis=1).astype(bf16)
+        own_rows = tile_rows(SIDE) == core
+        before, own, after = (
+            toward_side(side, adj_ref, w_ref, w_mate_ref, own_rows) for side in range(3)
         )
-        adj_ref[group] = jnp.concatenate([left, right], axis=1).astype(bf16)
-    own_rows = tile_rows(SIDE) == core
-    before, own, after = (
-        toward_side(side, adj_ref, w_ref, w_mate_ref, own_rows) for side in range(3)
-    )
-    own_out[...] = own + row_halves(turned(before), turned(after))
-    middle = neurons // 2
-    to_left = row_halves(before[:, :middle], turned(before[:, middle:])).astype(bf16)
-    to_right = row_halves(turned(after[:, :middle]), after[:, middle:]).astype(bf16)
-    unused = jnp.zeros_like(to_left)
-    for other in range(chips):
-        placed_out[other, :, 2 * LANES :] = unused
-    placed_out[jnp.where(chip > 0, chip - 1, chip), :, 2 * LANES :] = to_left
-    placed_out[jnp.where(chip < chips - 1, chip + 1, chip), :, 2 * LANES :] = to_right
+        own_out[...] = own + row_halves(turned(before), turned(after))
+        middle = neurons // 2
+        to_left = row_halves(before[:, :middle], turned(before[:, middle:])).astype(bf16)
+        to_right = row_halves(turned(after[:, :middle]), after[:, middle:]).astype(bf16)
+        unused = jnp.zeros_like(to_left)
+        for other in range(chips):
+            placed_out[other, :, 2 * LANES :] = unused
+        placed_out[jnp.where(chip > 0, chip - 1, chip), :, 2 * LANES :] = to_left
+        placed_out[jnp.where(chip < chips - 1, chip + 1, chip), :, 2 * LANES :] = to_right
+
+    for part in (long_part, local_part) if long_first else (local_part, long_part):
+        part()
 
 
 def turn_kernel(*refs):
@@ -435,7 +438,7 @@
     g_out[...] = decay * g_ref[...] + jax.nn.softplus(drive)
     backward_part(
         adj_g_ref[...], adj_v_ref[...], v_ref[...], jax.nn.sigmoid(drive), decay,
-        entry_ref, w_ref, w_mate_ref, w_long_ref, w_long_mate_ref, *refs[16:23],
+        entry_ref, w_ref, w_mate_ref, w_long_ref, w_long_mate_ref, *refs[16:23], True,
     )
     copy.wait()
 
@@ -480,7 +483,7 @@
     adj_v_out[...] = adj_volt
     backward_part(
         adj_g_ref[...], adj_volt, v_ref[...], gate_ref[...], decay_ref[...],
-        entry_ref, *weights, *refs[17:24],
+        entry_ref, *weights, *refs[17:24], False,
     )
 
 
@@ -581,7 +584,7 @@
         )
 
     state = ((rows, neurons), f32)
-    fields = (8, 2 * max(entries, LANES))
+    fields = (8, max(2 * entries, LANES))
     source = ((3, blocks // GROUP, GROUP * rows, WIDE), bf16)
     fetched = ((2 * entries // GROUP, GROUP * rows, LANES), bf16)
     block_row = pltpu.VMEM((blocks, rows, LANES), f32)
@@ -622,7 +625,7 @@
         (got, w_mate, w_long_mate, w_own, w_long)
     )
     out, v_start, g_start, adj_volt, adj_cond, spikes, decay, entry_rows = call(
-        merge_kernel,
+        functools.partial(merge_kernel, entries),
         [((chips, rows, neurons), bf16)]
         + [state] * 4
         + [((STEPS, rows, neurons), f32), state, (fields, jnp.int32)],

time: 96.8 us -> 96.4 us (level)
  no operation moved by 1% of the time
where the time goes in v8:
time: 96.4 us; the launch traced here: 96 us
  blocking collectives  79.9 us (83%)
  Pallas kernels  13.1 us (14%)
  starting transfers between devices  2.02 us (2%)
    all_to_all x8, blocking collectives, spread(): lax.all_to_all(values, 'azim', split_axis=0, concat_axis=0, tiled=True, a...  79.9 us
    pallas_call x14, Pallas kernels, call(): pl.pallas_call(kernel, out_shape=[pltpu.SMEM(shape, dtype) if number in s...  13.1 us
  transfers between devices with their start and end apart: 5, of which 1 were waited for; matrix products, arithmetic and copies ran while one was open for 0% of the time, Pallas kernels for 4%

profile of v8, /device:TPU:0, one launch (start us, length us, event | category | flops | bytes accessed | tf_op | source)
XLA Modules:
  0.0 96.0 jit_solution(2029872636952862596)
XLA Ops:
  0.6 0.5 collective-permute-start.1
  1.2 1.1 %shard_map.138 = (f32[5,8,1024]{2,1,0:T(8,128)S(1)}, f32[5,8,1024]{2,1,0:T(8,128)S(1)}) custom-call(f32[8,1024]{1,0:T(8,128)} %refs_0_.1, s32[4,8,1024]{2,1,0:T(8,128)} %refs_1_.1, f32[8,1024]{1,0:T(8,128)} %refs_2_.1, f32[8,1024]{1,0:T(8,128)} %refs_3_.1, f32[8,1024]{1,0:T(8,128)} %refs_4_.1, f32[1,1024]{1,0:T(1,128)} %refs_5_.1, s32[1,16]{1,0:T(1,128)} %bitcast.7, ...), custom_call_target="tpu_custom_call" | custom-call | tf_op jit(solution)/shard_map/pallas_call | solution.py:552
  2.3 0.1 collective-permute-start
  2.4 0.5 collective-permute-start.2
  2.9 1.3 %shard_map.139 = (bf16[3,192,1024]{2,1,0:T(8,128)(2,1)S(1)}, bf16[64,1024]{1,0:T(8,128)(2,1)S(1)}) custom-call(bf16[3,192,1024]{2,1,0:T(8,128)(2,1)} %bitcast.6, bf16[64,1024]{1,0:T(8,128)(2,1)} %w_long_ref.1), custom_call_target="tpu_custom_call" | custom-call | tf_op jit(solution)/shard_map/pallas_call | solution.py:552
  4.1 0.1 collective-permute-done.2.refs_5_.refs_15_
  4.3 0.0 collective-permute-done.got_ref
  4.3 0.0 collective-permute-done.1.refs_3_.refs_13_
  4.3 0.1 shard_map.140
  4.4 13.9 %all_to_all.40.refs_0_ = bf16[8,8,1024]{2,1,0:T(8,128)(2,1)S(1)} all-to-all(bf16[8,8,1024]{2,1,0:T(8,128)(2,1)S(1)} %get-tuple-element.82), channel_id=1, replica_groups={{0,3,4,7,8,11,12,15},{1,2,5,6,9,10,13,14},{16,19,20,23,24,27,28,31},{17..., dimensions={0} | all-to-all | bytes 262144 | tf_op jit(solution)/shard_map/all_to_all | solution.py:582
  18.3 1.2 %shard_map.141 = (f32[8,1024]{1,0:T(8,128)S(1)}, f32[8,1024]{1,0:T(8,128)S(1)}, f32[8,1024]{1,0:T(8,128)S(1)}, bf16[3,4,32,256]{3,2,1,0:T(8,128)(2,1)S(1)}, bf16...) custom-call(bf16[8,8,1024]{2,1,0:T(8,128)(2,1)S(1)} %all_to_all.40.refs_0_, ...), custom_call_target="tpu_custom_call" | custom-call | tf_op jit(solution)/shard_map/pallas_call | solution.py:552
  19.5 9.6 %all_to_all.41.refs_0_ = bf16[8,8,1152]{2,1,0:T(8,128)(2,1)S(1)} all-to-all(bf16[8,8,1152]{2,1,0:T(8,128)(2,1)S(1)} %get-tuple-element.92), channel_id=1, replica_groups={{0,3,4,7,8,11,12,15},{1,2,5,6,9,10,13,14},{16,19,20,23,24,27,28,31},{17..., dimensions={0} | all-to-all | bytes 294912 | tf_op jit(solution)/shard_map/all_to_all | solution.py:582
  29.0 0.6 shard_map.142
  29.6 9.9 %all_to_all.42.refs_0_ = bf16[8,8,1024]{2,1,0:T(8,128)(2,1)S(1)} all-to-all(bf16[8,8,1024]{2,1,0:T(8,128)(2,1)S(1)} %get-tuple-element.96), channel_id=1, replica_groups={{0,3,4,7,8,11,12,15},{1,2,5,6,9,10,13,14},{16,19,20,23,24,27,28,31},{17..., dimensions={0} | all-to-all | bytes 262144 | tf_op jit(solution)/shard_map/all_to_all | solution.py:582
  39.6 0.6 shard_map.143
  40.2 9.6 %all_to_all.43.refs_0_ = bf16[8,8,1024]{2,1,0:T(8,128)(2,1)S(1)} all-to-all(bf16[8,8,1024]{2,1,0:T(8,128)(2,1)S(1)} %get-tuple-element.99), channel_id=1, replica_groups={{0,3,4,7,8,11,12,15},{1,2,5,6,9,10,13,14},{16,19,20,23,24,27,28,31},{17..., dimensions={0} | all-to-all | bytes 262144 | tf_op jit(solution)/shard_map/all_to_all | solution.py:582
  49.8 1.7 %shard_map.144 = (f32[8,1024]{1,0:T(8,128)S(1)}, s32[8,128]{1,0:T(8,128)S(4)}, bf16[3,4,32,256]{3,2,1,0:T(8,128)(2,1)S(1)}, bf16[8,32,128]{2,1,0:T(8,128)(2,1)S(...) custom-call(bf16[8,8,1024]{2,1,0:T(8,128)(2,1)S(1)} %all_to_all.43.r, ...), custom_call_target="tpu_custom_call" | custom-call | tf_op jit(solution)/shard_map/pallas_call | solution.py:552
  51.5 9.4 %all_to_all.44.refs_0_ = bf16[8,8,768]{2,1,0:T(8,128)(2,1)S(1)} all-to-all(bf16[8,8,768]{2,1,0:T(8,128)(2,1)S(1)} %get-tuple-element.105), channel_id=1, replica_groups={{0,3,4,7,8,11,12,15},{1,2,5,6,9,10,13,14},{16,19,20,23,24,27,28,31},{17..., dimensions={0} | all-to-all | bytes 196608 | tf_op jit(solution)/shard_map/all_to_all | solution.py:582
  60.9 1.2 %shard_map.145 = (f32[8,1024]{1,0:T(8,128)S(1)}, bf16[4,32,256]{2,1,0:T(8,128)(2,1)S(1)}, bf16[8,32,256]{2,1,0:T(8,128)(2,1)S(1)}, f32[8,1024]{1,0:T(8,128)S(1)}...) custom-call(bf16[8,8,768]{2,1,0:T(8,128)(2,1)S(1)} %all_to_all.44.refs_0_, ...), custom_call_target="tpu_custom_call" | custom-call | tf_op jit(solution)/shard_map/pallas_call | solution.py:552
  62.1 9.0 %all_to_all.45.refs_0_ = bf16[8,8,768]{2,1,0:T(8,128)(2,1)S(1)} all-to-all(bf16[8,8,768]{2,1,0:T(8,128)(2,1)S(1)} %get-tuple-element.111), channel_id=1, replica_groups={{0,3,4,7,8,11,12,15},{1,2,5,6,9,10,13,14},{16,19,20,23,24,27,28,31},{17..., dimensions={0} | all-to-all | bytes 196608 | tf_op jit(solution)/shard_map/all_to_all | solution.py:582
  71.1 1.2 %shard_map.146 = (f32[8,1024]{1,0:T(8,128)S(1)}, bf16[4,32,256]{2,1,0:T(8,128)(2,1)S(1)}, bf16[8,32,256]{2,1,0:T(8,128)(2,1)S(1)}, f32[8,1024]{1,0:T(8,128)S(1)}...) custom-call(bf16[8,8,768]{2,1,0:T(8,128)(2,1)S(1)} %all_to_all.45.refs_0_, ...), custom_call_target="tpu_custom_call" | custom-call | tf_op jit(solution)/shard_map/pallas_call | solution.py:552
  72.2 9.1 %all_to_all.46.refs_0_ = bf16[8,8,768]{2,1,0:T(8,128)(2,1)S(1)} all-to-all(bf16[8,8,768]{2,1,0:T(8,128)(2,1)S(1)} %get-tuple-element.116), channel_id=1, replica_groups={{0,3,4,7,8,11,12,15},{1,2,5,6,9,10,13,14},{16,19,20,23,24,27,28,31},{17..., dimensions={0} | all-to-all | bytes 196608 | tf_op jit(solution)/shard_map/all_to_all | solution.py:582
  81.3 1.2 %shard_map.147 = (f32[8,1024]{1,0:T(8,128)S(1)}, bf16[4,32,256]{2,1,0:T(8,128)(2,1)S(1)}, bf16[8,32,256]{2,1,0:T(8,128)(2,1)S(1)}, f32[8,1024]{1,0:T(8,128)S(1)}...) custom-call(bf16[8,8,768]{2,1,0:T(8,128)(2,1)S(1)} %all_to_all.46.refs_0_, ...), custom_call_target="tpu_custom_call" | custom-call | tf_op jit(solution)/shard_map/pallas_call | solution.py:552
  82.4 0.9 shard_map.149
  83.4 0.7 collective-permute-start.4
  84.1 9.5 %all_to_all.47.refs_0_ = bf16[8,8,768]{2,1,0:T(8,128)(2,1)S(1)} all-to-all(bf16[8,8,768]{2,1,0:T(8,128)(2,1)S(1)} %get-tuple-element.121), channel_id=1, replica_groups={{0,3,4,7,8,11,12,15},{1,2,5,6,9,10,13,14},{16,19,20,23,24,27,28,31},{17..., dimensions={0} | all-to-all | bytes 196608 | tf_op jit(solution)/shard_map/all_to_all | solution.py:582
  93.6 0.2 shard_map.148.last_ref
  93.8 0.2 collective-permute-start.3
  94.0 0.0 collective-permute-done.4.got_ref
  94.0 1.3 %shard_map.150 = (bf16[576,1024]{1,0:T(8,128)(2,1)}, bf16[64,1024]{1,0:T(8,128)(2,1)}) custom-call(f32[640,1024]{1,0:T(8,128)S(1)} %get-tuple-element.141.own_ref, bf16[640,1024]{1,0:T(8,128)(2,1)S(1)} %collective-permute-done.4.got_ref), custom_call_target="tpu_custom_call" | custom-call | flops 10000000000 | tf_op jit(solution)/shard_map/pallas_call | solution.py:552
  95.3 0.0 collective-permute-done.3.got_ref
  95.3 0.6 shard_map.151
Async XLA Ops:
  0.6 3.6 %collective-permute-start.1 = (bf16[3,192,1024]{2,1,0:T(8,128)(2,1)}, bf16[3,192,1024]{2,1,0:T(8,128)(2,1)S(1)}, u32[]{:S(2)}, u32[]{:S(2)}) collective-permute-start(bf16[3,192,1024]{2,1,0:T(8,128)(2,1)} %bitcast.5), channel_id=1, source_target_pairs={{0,1},{1,0},{2,3},{3,2},{4,5},{5,4},{6,7},{7,6},{8,9},{9,8},{10,11... | collective-permute-start | bytes 3538952 | tf_op jit(solution)/shard_map/ppermute | solution.py:601
  2.3 2.0 %collective-permute-start = (f32[5,8,1024]{2,1,0:T(8,128)S(1)}, f32[5,8,1024]{2,1,0:T(8,128)S(1)}, u32[]{:S(2)}, u32[]{:S(2)}) collective-permute-start(f32[5,8,1024]{2,1,0:T(8,128)S(1)} %get-tuple-element.78), channel_id=1, source_target_pairs={{0,1},{1,0},{2,3},{3,2},{4,5},{5,4},{6,7},{7,6},{8,9},{9,8},{10,11... | collective-permute-start | bytes 491528 | tf_op jit(solution)/shard_map/ppermute | solution.py:623
  2.4 1.9 %collective-permute-start.2 = (bf16[64,1024]{1,0:T(8,128)(2,1)}, bf16[64,1024]{1,0:T(8,128)(2,1)S(1)}, u32[]{:S(2)}, u32[]{:S(2)}) collective-permute-start(bf16[64,1024]{1,0:T(8,128)(2,1)} %w_long_ref.1), channel_id=1, source_target_pairs={{0,1},{1,0},{2,3},{3,2},{4,5},{5,4},{6,7},{7,6},{8,9},{9,8},{10,11... | collective-permute-start | bytes 393224 | tf_op jit(solution)/shard_map/ppermute | solution.py:602
  83.4 10.6 %collective-permute-start.4 = (bf16[640,1024]{1,0:T(8,128)(2,1)S(1)}, bf16[640,1024]{1,0:T(8,128)(2,1)S(1)}, u32[]{:S(2)}, u32[]{:S(2)}) collective-permute-start(bf16[640,1024]{1,0:T(8,128)(2,1)S(1)} %get-tuple-element.142), channel_id=1, source_target_pairs={{0,1},{1,0},{2,3},{3,2},{4,5},{5,4},{6,7},{7,6},{8,9},{9,8},{10,11... | collective-permute-start | bytes 3932168 | tf_op jit(solution)/shard_map/ppermute | solution.py:704
  93.8 1.5 %collective-permute-start.3 = (f32[2,8,1024]{2,1,0:T(8,128)S(1)}, f32[2,8,1024]{2,1,0:T(8,128)S(1)}, u32[]{:S(2)}, u32[]{:S(2)}) collective-permute-start(f32[2,8,1024]{2,1,0:T(8,128)S(1)} %shard_map.148.last_ref), channel_id=1, source_target_pairs={{0,1},{1,0},{2,3},{3,2},{4,5},{5,4},{6,7},{7,6},{8,9},{9,8},{10,11... | collective-permute-start | bytes 196616 | tf_op jit(solution)/shard_map/ppermute | solution.py:708
